TPU v7x, 32 devices: a whole 2x2x4 slice. The times are simulated.
32 devices in a mesh: tm: 2 (over x), space: 4 (over z), clip: 4 (over y, core).
Axes of the slice: x: 2, y: 2, z: 4, core: 2. Of those that a mesh axis runs over, the one named last changes fastest.
Arguments:
- clips_in: bfloat16 [4, 32, 4, 49, 512], P('clip', 'tm', 'space'), may hold values from -6 to 6
- ln1_gain: bfloat16 [2, 512], P(None, ('tm', 'space', 'clip')), may hold values from 0.5 to 1.5
- ln1_bias: bfloat16 [2, 512], P(None, ('tm', 'space', 'clip')), may hold values from -1 to 1
- qkv_weight: bfloat16 [2, 512, 1536], P(None, ('tm', 'space', 'clip')), may hold values from -0.25 to 0.25
- qv_bias: bfloat16 [2, 1024], P(None, ('tm', 'space', 'clip')), may hold values from -1.5 to 1.5
- out_weight: bfloat16 [2, 512, 512], P(None, ('tm', 'space', 'clip')), may hold values from -1 to 1
- out_bias: bfloat16 [2, 512], P(None, ('tm', 'space', 'clip')), may hold values from -1 to 1
- ln2_gain: bfloat16 [2, 512], P(None, ('tm', 'space', 'clip')), may hold values from 0.5 to 1.5
- ln2_bias: bfloat16 [2, 512], P(None, ('tm', 'space', 'clip')), may hold values from -1 to 1
- fc1_weight: bfloat16 [2, 512, 2048], P(None, ('tm', 'space', 'clip')), may hold values from -0.25 to 0.25
- fc1_bias: bfloat16 [2, 2048], P(None, ('tm', 'space', 'clip')), may hold values from -1.5 to 1.5
- fc2_weight: bfloat16 [2, 2048, 512], P(None, ('tm', 'space', 'clip')), may hold values from -0.125 to 0.125
- fc2_bias: bfloat16 [2, 512], P(None, ('tm', 'space', 'clip')), may hold values from -1 to 1
- pos_table: bfloat16 [2, 2535, 16], P(None, None, 'tm'), may hold values from -4 to 4
- out_grad: bfloat16 [4, 32, 4, 49, 512], P('clip', 'tm', 'space'), may hold values from -6 to 6
Outputs:
- clips_out: bfloat16 [4, 32, 4, 49, 512], P('clip', 'tm', 'space')
- in_grad: bfloat16 [4, 32, 4, 49, 512], P('clip', 'tm', 'space')
- ln1_gain_grad: float32 [2, 512], P(None, ('tm', 'space', 'clip'))
- ln1_bias_grad: float32 [2, 512], P(None, ('tm', 'space', 'clip'))
- qkv_weight_grad: float32 [2, 512, 1536], P(None, ('tm', 'space', 'clip'))
- qv_bias_grad: float32 [2, 1024], P(None, ('tm', 'space', 'clip'))
- out_weight_grad: float32 [2, 512, 512], P(None, ('tm', 'space', 'clip'))
- out_bias_grad: float32 [2, 512], P(None, ('tm', 'space', 'clip'))
- ln2_gain_grad: float32 [2, 512], P(None, ('tm', 'space', 'clip'))
- ln2_bias_grad: float32 [2, 512], P(None, ('tm', 'space', 'clip'))
- fc1_weight_grad: float32 [2, 512, 2048], P(None, ('tm', 'space', 'clip'))
- fc1_bias_grad: float32 [2, 2048], P(None, ('tm', 'space', 'clip'))
- fc2_weight_grad: float32 [2, 2048, 512], P(None, ('tm', 'space', 'clip'))
- fc2_bias_grad: float32 [2, 512], P(None, ('tm', 'space', 'clip'))
- pos_table_grad: float32 [2, 2535, 16], P(None, None, 'tm')
All inputs are finite; a program needn't handle non-finite values.
Results may differ from a plain program's by a relative error of at most 0.017.
Values may be sent and summed in bfloat16 or wider, within the bound.
No kernel may reach another device: no remote copies, remote signals or barrier semaphores. Data moves between devices by JAX's collectives and lax.ppermute only.
A program may use at most 320 MiB of HBM per device.

v0:
```python
import jax
import jax.numpy as jnp
from jax import lax
from jax.sharding import PartitionSpec as P

HEADS = 16
WIN_T = 8
WIN_HW = 7
LAYERS = 2


masked_score = -1000000000.0


def partner(value, axis, bit):
    mask = 2**bit
    pairs = [(source, source ^ mask) for source in range(lax.axis_size(axis))]
    return lax.ppermute(value, axis, pairs)


def norm_rows(values, gain, offset):
    mean_row = jnp.mean(values, axis=-1, keepdims=True)
    centered = values - mean_row
    spread = jnp.mean(centered * centered, axis=-1, keepdims=True)
    return centered * lax.rsqrt(spread + 1e-05) * gain + offset


def gelu_exact(values):
    return jax.nn.gelu(values, approximate=False)


def project(left, right):
    return jnp.einsum("...i,ij->...j", left, right, preferred_element_type=jnp.float32)


def project_back(left, right):
    return jnp.einsum("...j,ij->...i", left, right, preferred_element_type=jnp.float32)


def outer_sum(left, right):
    flat_left = left.reshape(-1, left.shape[-1])
    flat_right = right.reshape(-1, right.shape[-1])
    return jnp.einsum("ti,tj->ij", flat_left, flat_right, preferred_element_type=jnp.float32)


def column_sum(values):
    return jnp.sum(values.reshape(-1, values.shape[-1]).astype(jnp.float32), axis=0)


def relative_index(win_t, win_hw):
    count = win_t * win_hw * win_hw
    positions = jnp.arange(count, dtype=jnp.int32)
    frame_pos = positions // (win_hw * win_hw)
    row_pos = positions // win_hw % win_hw
    col_pos = positions % win_hw
    span = 2 * win_hw - 1
    frame_off = frame_pos[:, None] - frame_pos[None, :] + win_t - 1
    row_off = row_pos[:, None] - row_pos[None, :] + win_hw - 1
    col_off = col_pos[:, None] - col_pos[None, :] + win_hw - 1
    return frame_off * span * span + row_off * span + col_off


def band_label(coord, extent, window, reach):
    return jnp.where(coord < extent - window, 0, jnp.where(coord < extent - reach, 1, 2)).astype(
        jnp.int32
    )


def region_match(frames):
    quadrant = lax.axis_index("space")
    row_quad = quadrant // 2
    col_quad = quadrant % 2
    local = jnp.arange(WIN_HW, dtype=jnp.int32)
    label_t = band_label(jnp.arange(frames, dtype=jnp.int32), frames, WIN_T, WIN_T // 2)
    label_r = band_label(row_quad * WIN_HW + local, 2 * WIN_HW, WIN_HW, WIN_HW // 2)
    label_c = band_label(col_quad * WIN_HW + local, 2 * WIN_HW, WIN_HW, WIN_HW // 2)
    region = label_t[:, None, None] * 9 + label_r[None, :, None] * 3 + label_c[None, None, :]
    region = region.reshape(frames // WIN_T, WIN_T * WIN_HW * WIN_HW)
    return region[:, :, None] == region[:, None, :]


def space_roll(field, onward):
    side = field.shape[2]
    reach = side // 2
    sent_rows = field[:, :, :reach] if onward else field[:, :, side - reach :]
    came_rows = partner(sent_rows, "space", 1)
    if onward:
        rows_done = jnp.concatenate([field, came_rows], axis=2)[:, :, reach : reach + side]
    else:
        rows_done = jnp.concatenate([came_rows, field], axis=2)[:, :, :side]
    sent_cols = rows_done[:, :, :, :reach] if onward else rows_done[:, :, :, side - reach :]
    came_cols = partner(sent_cols, "space", 0)
    if onward:
        return jnp.concatenate([rows_done, came_cols], axis=3)[:, :, :, reach : reach + side]
    return jnp.concatenate([came_cols, rows_done], axis=3)[:, :, :, :side]


def gather_layer(shards, layer):
    parts = tuple((w[layer] for w in shards))
    return (
        lax.all_gather(parts[0], ("tm", "space", "clip"), axis=0, tiled=True),
        lax.all_gather(parts[1], ("tm", "space", "clip"), axis=0, tiled=True),
        lax.all_gather(parts[2], ("tm", "space", "clip"), axis=0, tiled=True),
        lax.all_gather(parts[3], ("tm", "space", "clip"), axis=0, tiled=True),
        lax.all_gather(parts[4], ("tm", "space", "clip"), axis=0, tiled=True),
        lax.all_gather(parts[5], ("tm", "space", "clip"), axis=0, tiled=True),
        lax.all_gather(parts[6], ("tm", "space", "clip"), axis=0, tiled=True),
        lax.all_gather(parts[7], ("tm", "space", "clip"), axis=0, tiled=True),
        lax.all_gather(parts[8], ("tm", "space", "clip"), axis=0, tiled=True),
        lax.all_gather(parts[9], ("tm", "space", "clip"), axis=0, tiled=True),
        lax.all_gather(parts[10], ("tm", "space", "clip"), axis=0, tiled=True),
        lax.all_gather(parts[11], ("tm", "space", "clip"), axis=0, tiled=True),
    )


def gather_again(shards, layer):
    parts = tuple((w[layer] for w in shards))
    return (
        lax.all_gather(parts[0], ("tm", "space", "clip"), axis=0, tiled=True),
        lax.all_gather(parts[1], ("tm", "space", "clip"), axis=0, tiled=True),
        lax.all_gather(parts[2], ("tm", "space", "clip"), axis=0, tiled=True),
        lax.all_gather(parts[3], ("tm", "space", "clip"), axis=0, tiled=True),
        lax.all_gather(parts[4], ("tm", "space", "clip"), axis=0, tiled=True),
        lax.all_gather(parts[5], ("tm", "space", "clip"), axis=0, tiled=True),
        lax.all_gather(parts[6], ("tm", "space", "clip"), axis=0, tiled=True),
        lax.all_gather(parts[7], ("tm", "space", "clip"), axis=0, tiled=True),
        lax.all_gather(parts[8], ("tm", "space", "clip"), axis=0, tiled=True),
        lax.all_gather(parts[9], ("tm", "space", "clip"), axis=0, tiled=True),
        lax.all_gather(parts[10], ("tm", "space", "clip"), axis=0, tiled=True),
        lax.all_gather(parts[11], ("tm", "space", "clip"), axis=0, tiled=True),
    )


def table_bias(table):
    rel = relative_index(WIN_T, WIN_HW)
    return table.astype(jnp.float32)[rel].transpose(2, 0, 1)


def window_scores(queries, keys, bias, same, scale):
    scores = (
        jnp.einsum("wqhd,wkhd->whqk", queries, keys, preferred_element_type=jnp.float32) * scale
        + bias[None]
    )
    if same is not None:
        scores = jnp.where(same[:, None], scores, masked_score)
    return scores


def to_windows(field):
    clips, frames, cells, heads_here, head_size = field.shape
    return field.reshape(clips, frames // WIN_T, WIN_T * cells, heads_here, head_size)


def to_frames(field, frames):
    clips = field.shape[0]
    return field.reshape(clips, frames, WIN_HW * WIN_HW, field.shape[3], field.shape[4])


def layer_forward(stream, params, table, shifted):
    (
        gain_one,
        bias_one,
        mix_weight,
        mix_bias,
        proj_weight,
        proj_bias,
        gain_two,
        bias_two,
        wide_weight,
        wide_bias,
        narrow_weight,
        narrow_bias,
    ) = params
    clips, frames_here, side = (stream.shape[0], stream.shape[1], stream.shape[2])
    width = stream.shape[-1]
    head_size = width // HEADS
    scale = head_size ** (-0.5)
    normed = norm_rows(stream, gain_one.astype(jnp.float32), bias_one.astype(jnp.float32)).astype(
        jnp.bfloat16
    )
    if shifted:
        normed = space_roll(normed, True)
    mixed = project(normed, mix_weight)
    mix_bias32 = mix_bias.astype(jnp.float32)
    head_shape = (clips, frames_here, side * side, HEADS, head_size)
    queries = (mixed[..., :width] + mix_bias32[:width]).astype(jnp.bfloat16).reshape(head_shape)
    keys = mixed[..., width : 2 * width].astype(jnp.bfloat16).reshape(head_shape)
    values = (mixed[..., 2 * width :] + mix_bias32[width:]).astype(jnp.bfloat16).reshape(head_shape)
    queries, keys, values = (
        lax.all_to_all(queries, "tm", split_axis=3, concat_axis=1, tiled=True),
        lax.all_to_all(keys, "tm", split_axis=3, concat_axis=1, tiled=True),
        lax.all_to_all(values, "tm", split_axis=3, concat_axis=1, tiled=True),
    )
    frames = queries.shape[1]
    if shifted:
        queries = jnp.roll(queries, -(WIN_T // 2), axis=1)
        keys = jnp.roll(keys, -(WIN_T // 2), axis=1)
        values = jnp.roll(values, -(WIN_T // 2), axis=1)
    queries, keys, values = (to_windows(queries), to_windows(keys), to_windows(values))
    bias = table_bias(table)
    same = region_match(frames) if shifted else None

    def attend_clip(items):
        clip_queries, clip_keys, clip_values = items
        scores = window_scores(clip_queries, clip_keys, bias, same, scale)
        peak = jnp.max(scores, axis=-1, keepdims=True)
        raised = jnp.exp(scores - peak)
        total = jnp.sum(raised, axis=-1, keepdims=True)
        probs = (raised / total).astype(jnp.bfloat16)
        out_win = jnp.einsum(
            "whqk,wkhd->wqhd", probs, clip_values, preferred_element_type=jnp.float32
        ).astype(jnp.bfloat16)
        return (out_win, peak + jnp.log(total))

    attended_heads, log_total = lax.map(attend_clip, (queries, keys, values))
    attended_heads = to_frames(attended_heads, frames)
    if shifted:
        attended_heads = jnp.roll(attended_heads, WIN_T // 2, axis=1)
    attended = lax.all_to_all(attended_heads, "tm", split_axis=1, concat_axis=3, tiled=True)
    attended = attended.reshape(clips, frames_here, side, side, width)
    if shifted:
        attended = space_roll(attended, False)
    middle = stream + project(attended, proj_weight) + proj_bias.astype(jnp.float32)
    normed_two = norm_rows(
        middle, gain_two.astype(jnp.float32), bias_two.astype(jnp.float32)
    ).astype(jnp.bfloat16)
    hidden_pre = project(normed_two, wide_weight) + wide_bias.astype(jnp.float32)
    hidden = gelu_exact(hidden_pre).astype(jnp.bfloat16)
    after = middle + project(hidden, narrow_weight) + narrow_bias.astype(jnp.float32)
    stash = (
        stream,
        normed,
        queries,
        keys,
        values,
        log_total,
        attended,
        middle,
        normed_two,
        hidden_pre,
        hidden,
    )
    return (stash, after)


def layer_backward(grad_after, params, table, stash, shifted):
    (
        gain_one,
        bias_one,
        mix_weight,
        mix_bias,
        proj_weight,
        proj_bias,
        gain_two,
        bias_two,
        wide_weight,
        wide_bias,
        narrow_weight,
        narrow_bias,
    ) = params
    (
        stream,
        normed,
        queries,
        keys,
        values,
        log_total,
        attended,
        middle,
        normed_two,
        hidden_pre,
        hidden,
    ) = stash
    clips, frames_here, side = (stream.shape[0], stream.shape[1], stream.shape[2])
    width = stream.shape[-1]
    head_size = width // HEADS
    scale = head_size ** (-0.5)
    frames = queries.shape[1] * WIN_T
    grad_branch_two = grad_after.astype(jnp.bfloat16)
    narrow_grad = outer_sum(hidden, grad_branch_two)
    narrow_bias_grad = column_sum(grad_branch_two)
    grad_hidden = project_back(grad_branch_two, narrow_weight)
    gelu_pull = jax.vjp(gelu_exact, hidden_pre)[1]
    grad_pre = gelu_pull(grad_hidden)[0].astype(jnp.bfloat16)
    wide_grad = outer_sum(normed_two, grad_pre)
    wide_bias_grad = column_sum(grad_pre)
    grad_normed_two = project_back(grad_pre, wide_weight)
    norm_pull_two = jax.vjp(
        norm_rows, middle, gain_two.astype(jnp.float32), bias_two.astype(jnp.float32)
    )[1]
    grad_mid_part, gain_two_grad, bias_two_grad = norm_pull_two(grad_normed_two)
    grad_middle = grad_after + grad_mid_part
    grad_branch_one = grad_middle.astype(jnp.bfloat16)
    proj_grad = outer_sum(attended, grad_branch_one)
    proj_bias_grad = column_sum(grad_branch_one)
    grad_attended = project_back(grad_branch_one, proj_weight).astype(jnp.bfloat16)
    if shifted:
        grad_attended = space_roll(grad_attended, True)
    grad_attended = grad_attended.reshape(clips, frames_here, side * side, HEADS, head_size)
    grad_attended = lax.all_to_all(grad_attended, "tm", split_axis=3, concat_axis=1, tiled=True)
    if shifted:
        grad_attended = jnp.roll(grad_attended, -(WIN_T // 2), axis=1)
    grad_attended = to_windows(grad_attended)
    bias = table_bias(table)
    same = region_match(frames) if shifted else None

    def attend_back(carry, items):
        clip_queries, clip_keys, clip_values, clip_grad, clip_log = items
        scores = window_scores(clip_queries, clip_keys, bias, same, scale)
        probs = jnp.exp(scores - clip_log)
        grad_probs = jnp.einsum(
            "wqhd,wkhd->whqk", clip_grad, clip_values, preferred_element_type=jnp.float32
        )
        inner = jnp.sum(probs * grad_probs, axis=-1, keepdims=True)
        grad_scores = (probs * (grad_probs - inner)).astype(jnp.bfloat16)
        grad_q = (
            jnp.einsum(
                "whqk,wkhd->wqhd", grad_scores, clip_keys, preferred_element_type=jnp.float32
            )
            * scale
        ).astype(jnp.bfloat16)
        grad_k = (
            jnp.einsum(
                "whqk,wqhd->wkhd", grad_scores, clip_queries, preferred_element_type=jnp.float32
            )
            * scale
        ).astype(jnp.bfloat16)
        grad_v = jnp.einsum(
            "whqk,wqhd->wkhd",
            probs.astype(jnp.bfloat16),
            clip_grad,
            preferred_element_type=jnp.float32,
        ).astype(jnp.bfloat16)
        carry = carry + jnp.sum(grad_scores.astype(jnp.float32), axis=0)
        return (carry, (grad_q, grad_k, grad_v))

    window_tokens = queries.shape[2]
    start_bias = jnp.zeros((queries.shape[3], window_tokens, window_tokens), jnp.float32)
    bias_grad, grads_win = lax.scan(
        attend_back, start_bias, (queries, keys, values, grad_attended, log_total)
    )
    grad_q, grad_k, grad_v = (to_frames(g, frames) for g in grads_win)
    if shifted:
        grad_q = jnp.roll(grad_q, WIN_T // 2, axis=1)
        grad_k = jnp.roll(grad_k, WIN_T // 2, axis=1)
        grad_v = jnp.roll(grad_v, WIN_T // 2, axis=1)
    grad_q, grad_k, grad_v = (
        lax.all_to_all(grad_q, "tm", split_axis=1, concat_axis=3, tiled=True),
        lax.all_to_all(grad_k, "tm", split_axis=1, concat_axis=3, tiled=True),
        lax.all_to_all(grad_v, "tm", split_axis=1, concat_axis=3, tiled=True),
    )
    token_shape = (clips, frames_here, side, side, width)
    grad_q, grad_k, grad_v = (
        grad_q.reshape(token_shape),
        grad_k.reshape(token_shape),
        grad_v.reshape(token_shape),
    )
    grad_mix = jnp.concatenate([grad_q, grad_k, grad_v], axis=-1)
    mix_grad = outer_sum(normed, grad_mix)
    mix_bias_grad = jnp.concatenate([column_sum(grad_q), column_sum(grad_v)])
    grad_normed = project_back(grad_mix, mix_weight)
    if shifted:
        grad_normed = space_roll(grad_normed.astype(jnp.bfloat16), False).astype(jnp.float32)
    norm_pull_one = jax.vjp(
        norm_rows, stream, gain_one.astype(jnp.float32), bias_one.astype(jnp.float32)
    )[1]
    grad_stream_part, gain_one_grad, bias_one_grad = norm_pull_one(grad_normed)
    grad_stream = grad_middle + grad_stream_part
    rel = relative_index(WIN_T, WIN_HW).reshape(-1)
    table_grad = (
        jnp.zeros(table.shape, jnp.float32).at[rel].add(bias_grad.reshape(bias_grad.shape[0], -1).T)
    )
    weight_grads = (
        gain_one_grad,
        bias_one_grad,
        mix_grad,
        mix_bias_grad,
        proj_grad,
        proj_bias_grad,
        gain_two_grad,
        bias_two_grad,
        wide_grad,
        wide_bias_grad,
        narrow_grad,
        narrow_bias_grad,
    )
    return (grad_stream, weight_grads, table_grad)


def per_device(
    clips_in,
    ln1_gain,
    ln1_bias,
    qkv_weight,
    qv_bias,
    out_weight,
    out_bias,
    ln2_gain,
    ln2_bias,
    fc1_weight,
    fc1_bias,
    fc2_weight,
    fc2_bias,
    pos_table,
    out_grad,
):
    clips, frames_here, quads, cells, width = clips_in.shape
    grid_shape = (clips, frames_here, WIN_HW, WIN_HW, width)
    shards = (
        ln1_gain,
        ln1_bias,
        qkv_weight,
        qv_bias,
        out_weight,
        out_bias,
        ln2_gain,
        ln2_bias,
        fc1_weight,
        fc1_bias,
        fc2_weight,
        fc2_bias,
    )
    stream = clips_in.astype(jnp.float32).reshape(grid_shape)
    kept_params = []
    kept_stash = []
    for layer in range(LAYERS):
        params = gather_layer(shards, layer)
        stash, stream = layer_forward(stream, params, pos_table[layer], layer % 2 == 1)
        kept_params.append(params)
        kept_stash.append(stash)
    clips_out = stream.astype(jnp.bfloat16).reshape(clips_in.shape)
    grad_stream = out_grad.astype(jnp.float32).reshape(grid_shape)
    layer_shares = [None] * LAYERS
    table_parts = [None] * LAYERS
    for layer in reversed(range(LAYERS)):
        params = gather_again(shards, layer)
        grad_stream, weight_grads, table_grad = layer_backward(
            grad_stream, params, pos_table[layer], kept_stash[layer], layer % 2 == 1
        )
        layer_shares[layer] = (
            lax.psum_scatter(
                weight_grads[0], ("tm", "space", "clip"), scatter_dimension=0, tiled=True
            ),
            lax.psum_scatter(
                weight_grads[1], ("tm", "space", "clip"), scatter_dimension=0, tiled=True
            ),
            lax.psum_scatter(
                weight_grads[2], ("tm", "space", "clip"), scatter_dimension=0, tiled=True
            ),
            lax.psum_scatter(
                weight_grads[3], ("tm", "space", "clip"), scatter_dimension=0, tiled=True
            ),
            lax.psum_scatter(
                weight_grads[4], ("tm", "space", "clip"), scatter_dimension=0, tiled=True
            ),
            lax.psum_scatter(
                weight_grads[5], ("tm", "space", "clip"), scatter_dimension=0, tiled=True
            ),
            lax.psum_scatter(
                weight_grads[6], ("tm", "space", "clip"), scatter_dimension=0, tiled=True
            ),
            lax.psum_scatter(
                weight_grads[7], ("tm", "space", "clip"), scatter_dimension=0, tiled=True
            ),
            lax.psum_scatter(
                weight_grads[8], ("tm", "space", "clip"), scatter_dimension=0, tiled=True
            ),
            lax.psum_scatter(
                weight_grads[9], ("tm", "space", "clip"), scatter_dimension=0, tiled=True
            ),
            lax.psum_scatter(
                weight_grads[10], ("tm", "space", "clip"), scatter_dimension=0, tiled=True
            ),
            lax.psum_scatter(
                weight_grads[11], ("tm", "space", "clip"), scatter_dimension=0, tiled=True
            ),
        )
        table_parts[layer] = table_grad
    in_grad = grad_stream.astype(jnp.bfloat16).reshape(clips_in.shape)
    table_total = lax.psum(jnp.stack(table_parts), ("space", "clip"))
    stacked = tuple(
        (jnp.stack([layer_shares[n][slot] for n in range(LAYERS)]) for slot in range(12))
    )
    return (
        clips_out,
        in_grad,
        stacked[0],
        stacked[1],
        stacked[2],
        stacked[3],
        stacked[4],
        stacked[5],
        stacked[6],
        stacked[7],
        stacked[8],
        stacked[9],
        stacked[10],
        stacked[11],
        table_total,
    )


def solution(mesh):
    placed = (
        P("clip", "tm", "space", None, None),
        P(None, ("tm", "space", "clip")),
        P(None, ("tm", "space", "clip")),
        P(None, ("tm", "space", "clip"), None),
        P(None, ("tm", "space", "clip")),
        P(None, ("tm", "space", "clip"), None),
        P(None, ("tm", "space", "clip")),
        P(None, ("tm", "space", "clip")),
        P(None, ("tm", "space", "clip")),
        P(None, ("tm", "space", "clip"), None),
        P(None, ("tm", "space", "clip")),
        P(None, ("tm", "space", "clip"), None),
        P(None, ("tm", "space", "clip")),
        P(None, None, "tm"),
        P("clip", "tm", "space", None, None),
    )
    return jax.shard_map(
        per_device,
        mesh=mesh,
        in_specs=placed,
        out_specs=(
            P("clip", "tm", "space", None, None),
            P("clip", "tm", "space", None, None),
            P(None, ("tm", "space", "clip")),
            P(None, ("tm", "space", "clip")),
            P(None, ("tm", "space", "clip"), None),
            P(None, ("tm", "space", "clip")),
            P(None, ("tm", "space", "clip"), None),
            P(None, ("tm", "space", "clip")),
            P(None, ("tm", "space", "clip")),
            P(None, ("tm", "space", "clip")),
            P(None, ("tm", "space", "clip"), None),
            P(None, ("tm", "space", "clip")),
            P(None, ("tm", "space", "clip"), None),
            P(None, ("tm", "space", "clip")),
            P(None, None, "tm"),
        ),
        check_vma=False,
    )
```

profile of v0, /device:TPU:0, one launch (start us, length us, event | category | flops | bytes accessed | tf_op | source)
XLA Modules:
  0.0 3776.5 jit_solution(1213392347329711466)
XLA Ops:
  25.0 43.0 %all-reduce.33 = (bf16[512]{0:T(512)(128)(2,1)S(1)}, bf16[512]{0:T(512)(128)(2,1)S(1)}, bf16[1024]{0:T(1024)(128)(2,1)S(1)}, bf16[512]{0:T(512)(128)(2,1)S(1)}, ...) all-reduce(bf16[512]{0:T(512)(128)(2,1)S(1)} %dynamic-update-slice., ...), channel_id=3, replica_groups=mesh['tm'=2,'space'=4,'clip'=4] {'tm','space','clip'}, use_global_device_ids=true, to_apply=%add.1 | all-reduce | flops 12288 | bytes 49152
  142.2 282.6 %gather_fusion = f32[153664,8]{1,0:T(8,128)} fusion(f32[2535,8]{1,0:T(8,128)S(1)} %bitcast_convert_fusion.1, s32[154624]{0:T(1024)S(1)} %copy-done.34), kind=kCustom, calls=%fused_computation | custom fusion | bytes 10449152 | tf_op jit(solution)/shard_map/gather | solution.py:136
  424.9 52.7 %copy.191 = f32[392,392,8]{0,1,2:T(8,128)} copy(f32[392,392,8]{2,1,0:T(8,128)} %bitcast.18) | data formatting | bytes 9834496 | tf_op jit(solution)/shard_map/gather | solution.py:136
  570.0 45.9 %all-gather.4 = bf16[1,512,512]{2,1,0:T(8,128)(2,1)} all-gather(bf16[1,16,512]{2,1,0:T(8,128)(2,1)S(1)} %get-tuple-element.241), channel_id=6, replica_groups=mesh['tm'=2,'space'=4,'clip'=4] {'tm','space','clip'}, dimensions={1}, use_global_device_ids=true | all-gather | bytes 540672 | tf_op jit(solution)/shard_map/all_gather | solution.py:105
  645.0 16.2 multiply_convert_fusion.3
  668.8 15.6 collective-permute-done
  759.5 310.1 %gather_fusion.1 = f32[153664,8]{1,0:T(8,128)} fusion(f32[2535,8]{1,0:T(8,128)S(1)} %bitcast_convert_fusion, s32[154624]{0:T(1024)} %pad_clamp_fusion), kind=kCustom, calls=%fused_computation.1 | custom fusion | bytes 10449152 | tf_op jit(solution)/shard_map/gather | solution.py:136
  1069.6 52.6 %copy.212 = f32[392,392,8]{0,1,2:T(8,128)} copy(f32[392,392,8]{2,1,0:T(8,128)} %bitcast.59) | data formatting | bytes 9834496 | tf_op jit(solution)/shard_map/gather | solution.py:136
  1175.2 14.4 fusion.175
  1221.5 13.4 all_to_all.252
  1254.3 16.1 collective-permute-done.2
  1271.9 45.0 %all-gather.16 = bf16[1,512,512]{2,1,0:T(8,128)(2,1)S(1)} all-gather(bf16[1,16,512]{2,1,0:T(8,128)(2,1)S(1)} %copy-done.108), channel_id=18, replica_groups=mesh['tm'=2,'space'=4,'clip'=4] {'tm','space','clip'}, dimensions={1}, use_global_device_ids=true | all-gather | bytes 540672 | tf_op jit(solution)/shard_map/all_gather | solution.py:105
  1327.3 16.2 multiply_convert_fusion.2
  1359.0 15.7 collective-permute-done.4
  1442.7 16.9 multiply_reduce_fusion.1
  1480.2 22.0 convert_reduce_fusion
  1723.8 16.1 multiply_reduce_fusion
  1756.5 22.1 convert_reduce_fusion.1
  1950.5 35.0 copy.263
  1985.4 819.6 %scatter_custom_fusion.1 = f32[2535,8]{1,0:T(8,128)S(1)} fusion(s32[153664]{0:T(1024)} %fusion.123, f32[153664,8]{1,0:T(8,128)} %copy.263, f32[]{:T(128)} %constant.254.clone.1), kind=kCustom, calls=%fused_computation.238 | custom fusion | flops 1229312 | bytes 81632 | tf_op jit(solution)/shard_map/scatter-add | solution.py:371
  2824.7 35.0 copy.261
  2859.6 820.2 %scatter_custom_fusion = f32[2535,8]{1,0:T(8,128)} fusion(s32[153664]{0:T(1024)} %fusion.123, f32[153664,8]{1,0:T(8,128)} %copy.261, f32[]{:T(128)} %constant.254.clone.1), kind=kCustom, calls=%fused_computation.240 | custom fusion | flops 1229312 | bytes 81632 | tf_op jit(solution)/shard_map/scatter-add | solution.py:371
  3690.6 39.3 %all-reduce.32 = (f32[512]{0:T(512)S(1)}, f32[512]{0:T(512)S(1)}, f32[512]{0:T(512)S(1)}, f32[512]{0:T(512)S(1)}, f32[1024]{0:T(1024)S(1)}, /*index=5*/f32[1024]...) all-reduce(f32[512]{0:T(512)S(1)} %copy-done.129, ...), channel_id=27, replica_groups=mesh['tm'=2,'space'=4,'clip'=4] {'tm','space','clip'}, use_global_device_ids=true, to_apply=%region_25.26.clone | all-reduce | flops 12288 | bytes 98304
  3745.1 23.1 all-reduce.36.cloned.1.call-done
  (746 shorter events, 970.9 us)
Async XLA Ops:
  7.2 64.0 %all-gather.31.cloned.1.call-start = ((), (), s32[]{:S(2)}) async-start(), calls=%async_computation.33 | async-start | bytes 1622016 | tf_op jit(solution)/shard_map/all_gather | solution.py:103
  8.8 628.3 %all-gather.33.cloned.1.call-start = ((), (), s32[]{:S(2)}) async-start(), calls=%async_computation.34 | async-start | bytes 2162688 | tf_op jit(solution)/shard_map/all_gather | solution.py:109
  10.4 650.9 %all-gather.35.cloned.1.call-start = ((), (), s32[]{:S(2)}) async-start(), calls=%async_computation.35 | async-start | bytes 2162688 | tf_op jit(solution)/shard_map/all_gather | solution.py:111
  12.0 672.6 %all-gather.37.cloned.1.call-start = ((), (), s32[]{:S(2)}) async-start(), calls=%async_computation.36 | async-start | bytes 1622016 | tf_op jit(solution)/shard_map/all_gather | solution.py:103
  137.8 366.0 %all-to-all-start.1 = ((bf16[2,2,100352]{2,1,0:T(2,128)(2,1)}), bf16[2,2,100352]{2,1,0:T(2,128)(2,1)}, u32[]{:S(2)}, u32[]{:S(2)}) async-start(bf16[2,2,100352]{2,1,0:T(2,128)(2,1)} %reshape.1477), calls=%async_computation.1 | async-start | bytes 1605632 | tf_op jit(solution)/shard_map/all_to_all | solution.py:190
  565.8 50.1 %all-to-all-start.3 = ((bf16[2,2,100352]{2,1,0:T(2,128)(2,1)}), bf16[2,2,100352]{2,1,0:T(2,128)(2,1)S(1)}, u32[]{:S(2)}, u32[]{:S(2)}) async-start(bf16[2,2,100352]{2,1,0:T(2,128)(2,1)} %reshape.1481), calls=%async_computation.3 | async-start | bytes 1605632 | tf_op jit(solution)/shard_map/all_to_all | solution.py:219
  569.4 749.9 %all-gather.39.cloned.1.call-start = ((), (), s32[]{:S(2)}) async-start(), calls=%async_computation.37 | async-start | bytes 2162688 | tf_op jit(solution)/shard_map/all_gather | solution.py:109
  754.3 389.1 %all-to-all-start.5 = ((bf16[2,2,100352]{2,1,0:T(2,128)(2,1)}), bf16[2,2,100352]{2,1,0:T(2,128)(2,1)}, u32[]{:S(2)}, u32[]{:S(2)}) async-start(bf16[2,2,100352]{2,1,0:T(2,128)(2,1)} %reshape.1485), calls=%async_computation.5 | async-start | bytes 1605632 | tf_op jit(solution)/shard_map/all_to_all | solution.py:190
  758.6 584.9 %all-gather.41.cloned.1.call-start = ((), (), s32[]{:S(2)}) async-start(), calls=%async_computation.38 | async-start | bytes 2162688 | tf_op jit(solution)/shard_map/all_gather | solution.py:111
  1271.7 45.3 %collective-permute-start.3 = (bf16[1,16,7,3,512]{4,1,3,2,0:T(8,128)(2,1)S(1)}, bf16[1,16,7,3,512]{4,1,3,2,0:T(8,128)(2,1)}, u32[]{:S(2)}, u32[]{:S(2)}) collective-permute-start(bf16[1,16,7,3,512]{4,1,3,2,0:T(8,128)(2,1)S(1)} %slice.326), channel_id=1, source_target_pairs={{0,4},{4,0},{8,12},{12,8},{1,5},{5,1},{9,13},{13,9},{2,6},{6,2},{1... | collective-permute-start | bytes 1032200 | tf_op jit(solution)/shard_map/ppermute | solution.py:18
  1476.6 45.9 %all-to-all-start.11 = ((bf16[2,2,100352]{2,1,0:T(2,128)(2,1)}), bf16[2,2,100352]{2,1,0:T(2,128)(2,1)S(1)}, u32[]{:S(2)}, u32[]{:S(2)}) async-start(bf16[2,2,100352]{2,1,0:T(2,128)(2,1)} %reshape.1493), calls=%async_computation.11 | async-start | bytes 1605632 | tf_op jit(solution)/shard_map/all_to_all | solution.py:350
  1522.5 28.6 all-to-all-start.9
  1551.2 44.1 %all-to-all-start.10 = ((bf16[2,2,100352]{2,1,0:T(2,128)(2,1)}), bf16[2,2,100352]{2,1,0:T(2,128)(2,1)S(1)}, u32[]{:S(2)}, u32[]{:S(2)}) async-start(bf16[2,2,100352]{2,1,0:T(2,128)(2,1)} %reshape.1495), calls=%async_computation.10 | async-start | bytes 1605632 | tf_op jit(solution)/shard_map/all_to_all | solution.py:349
  1554.7 2183.9 %reduce-scatter.15.cloned.1.call-start = ((), (), s32[]{:S(2)}) async-start(), calls=%async_computation.27 | async-start | bytes 1081344 | tf_op jit(solution)/shard_map/reduce_scatter | solution.py:453
  1640.3 2098.3 %reduce-scatter.13.cloned.1.call-start = ((), (), s32[]{:S(2)}) async-start(), calls=%async_computation.26 | async-start | bytes 1081344 | tf_op jit(solution)/shard_map/reduce_scatter | solution.py:453
  1690.0 2050.1 %reduce-scatter.11.cloned.1.call-start = ((), (), s32[]{:S(2)}) async-start(), calls=%async_computation.25 | async-start | bytes 3244032 | tf_op jit(solution)/shard_map/reduce_scatter | solution.py:447
  1752.2 42.1 %all-to-all-start.15 = ((bf16[2,2,100352]{2,1,0:T(2,128)(2,1)}), bf16[2,2,100352]{2,1,0:T(2,128)(2,1)}, u32[]{:S(2)}, u32[]{:S(2)}) async-start(bf16[2,2,100352]{2,1,0:T(2,128)(2,1)} %reshape.1501), calls=%async_computation.15 | async-start | bytes 1605632 | tf_op jit(solution)/shard_map/all_to_all | solution.py:350
  1818.3 43.5 %all-to-all-start.14 = ((bf16[2,2,100352]{2,1,0:T(2,128)(2,1)}), bf16[2,2,100352]{2,1,0:T(2,128)(2,1)}, u32[]{:S(2)}, u32[]{:S(2)}) async-start(bf16[2,2,100352]{2,1,0:T(2,128)(2,1)} %reshape.1503), calls=%async_computation.14 | async-start | bytes 1605632 | tf_op jit(solution)/shard_map/all_to_all | solution.py:349
  1822.6 1917.4 %reduce-scatter.9.cloned.1.call-start = ((), (), s32[]{:S(2)}) async-start(), calls=%async_computation.24 | async-start | bytes 3244032 | tf_op jit(solution)/shard_map/reduce_scatter | solution.py:447
  1886.3 1855.3 %reduce-scatter.19.cloned.1.call-start = ((), (), s32[]{:S(2)}) async-start(), calls=%async_computation.29 | async-start | bytes 4325376 | tf_op jit(solution)/shard_map/reduce_scatter | solution.py:465
  1894.3 1847.4 %reduce-scatter.17.cloned.1.call-start = ((), (), s32[]{:S(2)}) async-start(), calls=%async_computation.28 | async-start | bytes 4325376 | tf_op jit(solution)/shard_map/reduce_scatter | solution.py:465
  1902.1 1841.2 %reduce-scatter.23.cloned.1.call-start = ((), (), s32[]{:S(2)}) async-start(), calls=%async_computation.31 | async-start | bytes 4325376 | tf_op jit(solution)/shard_map/reduce_scatter | solution.py:471
  1909.7 1833.7 %reduce-scatter.21.cloned.1.call-start = ((), (), s32[]{:S(2)}) async-start(), calls=%async_computation.30 | async-start | bytes 4325376 | tf_op jit(solution)/shard_map/reduce_scatter | solution.py:471
  1917.4 1850.8 %all-reduce.36.cloned.1.call-start = ((), (), s32[]{:S(2)}) async-start(), calls=%async_computation.32 | async-start | bytes 327680 | tf_op jit(solution)/shard_map/psum | solution.py:480
  (166 other events, 3786.5 us)
Sparse Core Ops, SparseCore 0:
  11.5 57.8 all-gather.30
  72.8 56.5 all-gather.32
  132.9 55.2 all-gather.34
  190.9 53.8 all-gather.36
  667.7 56.7 all-gather.38
  1271.9 54.2 all-gather.40
  1640.4 134.2 reduce-scatter.14
  1777.1 131.6 reduce-scatter.12
  1914.2 97.5 reduce-scatter.10
  2017.0 100.5 reduce-scatter.8
  2119.9 139.9 reduce-scatter.18
  2262.0 137.2 reduce-scatter.16
  2401.6 137.6 reduce-scatter.22
  2541.4 137.4 reduce-scatter.20
  3682.4 85.7 all-reduce.35
where the time goes:
time: 3800 us; the launch traced here: 3780 us
  other arithmetic  1810 us (48%)
  local copies, waits for them, and re-layouts  1350 us (36%)
  matrix products  230 us (6%)
  blocking collectives  186 us (5%)
  waiting for transfers between devices  123 us (3%)
  starting transfers between devices  63.8 us (2%)
    scatter-add x2, other arithmetic, layer_backward(): jnp.zeros(table.shape, jnp.float32).at[rel]  1640 us
    gather x4, local copies, waits for them, and re-layouts, table_bias(): return table.astype(jnp.float32)[rel].transpose(2, 0, 1)  698 us
    unnamed x378, local copies, waits for them, and re-layouts  245 us
    all_gather x2, blocking collectives, gather_layer(): lax.all_gather(parts[4], ('tm', 'space', 'clip'), axis=0, tiled=True)  90.8 us
    ppermute x8, waiting for transfers between devices, partner(): return lax.ppermute(value, axis, pairs)  83.6 us
    unnamed x2, blocking collectives  82.2 us
  transfers between devices with their start and end apart: 38, of which 10 were waited for; matrix products, arithmetic and copies ran while one was open for 86% of the time, Pallas kernels for 0%

commit v1 on v0

--- a/solution.py
+++ b/solution.py
@@ -1,6 +1,12 @@
+import functools
+import math
+
 import jax
 import jax.numpy as jnp
+import numpy as np
 from jax import lax
+from jax.experimental import pallas as pl
+from jax.experimental.pallas import tpu as pltpu
 from jax.sharding import PartitionSpec as P
 
 HEADS = 16
@@ -500,6 +506,801 @@
     )
 
 
+F32 = jnp.float32
+BF16 = jnp.bfloat16
+TOKENS = WIN_T * WIN_HW * WIN_HW
+CELLS = WIN_HW * WIN_HW
+SPAN = 2 * WIN_HW - 1
+STEPS = 2 * WIN_T - 1
+LOG2E = math.log2(math.e)
+VMEM_BYTES = 56 * 1024 * 1024
+
+
+def mm(left, right, left_dim=1, right_dim=0):
+    dims = (((left_dim,), (right_dim,)), ((), ()))
+    return lax.dot_general(left, right, dims, preferred_element_type=F32)
+
+
+def call(kernel, grid, in_specs, out_specs, out_shape, flops, scratch=()):
+    return pl.pallas_call(
+        kernel,
+        grid=grid,
+        in_specs=in_specs,
+        out_specs=out_specs,
+        out_shape=out_shape,
+        scratch_shapes=scratch,
+        cost_estimate=pl.CostEstimate(
+            flops=int(flops), transcendentals=0, bytes_accessed=8 * 1024 * 1024
+        ),
+        compiler_params=pltpu.CompilerParams(vmem_limit_bytes=VMEM_BYTES),
+    )
+
+
+def whole_block(shape):
+    return pl.BlockSpec(shape, lambda *ids: (0,) * len(shape))
+
+
+def win_block(width, column=0):
+    return pl.BlockSpec((1, TOKENS, width), lambda w: (w, 0, column))
+
+
+def halo_plan(frames_here):
+    half_t, reach = WIN_T // 2, WIN_HW // 2
+    frame, row, col = np.meshgrid(
+        np.arange(frames_here), np.arange(WIN_HW), np.arange(WIN_HW), indexing="ij"
+    )
+    frame, row, col = frame.reshape(-1), row.reshape(-1), col.reshape(-1)
+    new_t = (frame - half_t) % frames_here
+    new_r = (row - reach) % WIN_HW
+    new_c = (col - reach) % WIN_HW
+    target = new_t * CELLS + new_r * WIN_HW + new_c
+    leaves = (frame < half_t) * 4 + (row < reach) * 2 + (col < reach) * 1
+    parts = []
+    for kind in range(1, 8):
+        source = np.nonzero(leaves == kind)[0]
+        parts.append((kind, source, target[source]))
+    stay = np.nonzero(leaves == 0)[0]
+    return parts, (stay, target[stay])
+
+
+def halo_matrices(frames_here):
+    parts, (stay, stay_to) = halo_plan(frames_here)
+    count = frames_here * CELLS
+    rows = [-(-len(source) // 16) * 16 for _, source, _ in parts]
+    starts = np.concatenate([[0], np.cumsum(rows)])
+    send = np.zeros((starts[-1], count), np.float32)
+    place = np.zeros((count, starts[-1]), np.float32)
+    own = np.zeros((count, count), np.float32)
+    for (_, source, to), start in zip(parts, starts[:-1]):
+        slots = start + np.arange(len(source))
+        send[slots, source] = 1
+        place[to, slots] = 1
+    own[stay_to, stay] = 1
+    return send, place, own, rows, starts, [kind for kind, _, _ in parts]
+
+
+def halo_permute(packed, rows, starts, kinds, onward):
+    ring, quads = lax.axis_size("tm"), lax.axis_size("space")
+    came = []
+    for kind, start, count in zip(kinds, starts, rows):
+        piece = packed[start : start + count]
+        step = 0 if not kind & 4 else (-1 if onward else 1)
+        pairs = []
+        for frame_at in range(ring):
+            for quad in range(quads):
+                to = (frame_at + step) % ring * quads + (quad ^ (kind & 3))
+                pairs.append((frame_at * quads + quad, to))
+        came.append(lax.ppermute(piece, ("tm", "space"), pairs))
+    return came
+
+
+def pack_kernel(center, send_ref, x_ref, out_ref):
+    windows = x_ref.shape[0]
+    total = None
+    for w in range(windows):
+        x = x_ref[w]
+        if center:
+            x = x - jnp.mean(x, axis=-1, keepdims=True)
+        part = mm(send_ref[:, w * TOKENS : (w + 1) * TOKENS], x.astype(BF16))
+        total = part if total is None else total + part
+    out_ref[...] = total.astype(BF16)
+
+
+def halo_pack(x, send, center):
+    windows, _, width = x.shape
+    rows = send.shape[0]
+    return call(
+        functools.partial(pack_kernel, center),
+        (),
+        [pl.BlockSpec(memory_space=pltpu.VMEM)] * 2,
+        pl.BlockSpec(memory_space=pltpu.VMEM),
+        jax.ShapeDtypeStruct((rows, width), BF16),
+        2 * rows * windows * TOKENS * width,
+    )(jnp.asarray(send, BF16), x)
+
+
+def unpack_kernel(center, add_mean, starts, own_ref, place_ref, x_ref, base_ref, *refs):
+    came_refs, out_ref = refs[:-1], refs[-1]
+    windows = x_ref.shape[0]
+    total = jnp.zeros((windows * TOKENS, x_ref.shape[-1]), F32)
+    for w in range(windows):
+        x = x_ref[w].astype(F32)
+        if center:
+            x = x - jnp.mean(x, axis=-1, keepdims=True)
+        high = x.astype(BF16)
+        cols = own_ref[:, w * TOKENS : (w + 1) * TOKENS]
+        total = total + mm(cols, high)
+        if x_ref.dtype == F32:
+            total = total + mm(cols, (x - high.astype(F32)).astype(BF16))
+    came = jnp.concatenate([r[...] for r in came_refs], axis=0)
+    total = total + mm(place_ref[...], came)
+    for w in range(windows):
+        piece = total[w * TOKENS : (w + 1) * TOKENS]
+        if add_mean:
+            piece = piece + jnp.mean(base_ref[w], axis=-1, keepdims=True)
+        out_ref[w] = piece.astype(out_ref.dtype)
+
+
+def halo_unpack(x, came, own, place, starts, dtype, center=False, mean_of=None):
+    windows, _, width = x.shape
+    base = jnp.zeros((windows, 8, 128), F32) if mean_of is None else mean_of
+    return call(
+        functools.partial(unpack_kernel, center, mean_of is not None, starts),
+        (),
+        [pl.BlockSpec(memory_space=pltpu.VMEM)] * (4 + len(came)),
+        pl.BlockSpec(memory_space=pltpu.VMEM),
+        jax.ShapeDtypeStruct((windows, TOKENS, width), dtype),
+        4 * (windows * TOKENS) ** 2 * width,
+    )(jnp.asarray(own, BF16), jnp.asarray(place, BF16), x, base, *came)
+
+
+def index_bits():
+    bits = []
+    for axis in ("tm", "space", "clip"):
+        count = lax.axis_size(axis).bit_length() - 1
+        bits += [(axis, b) for b in reversed(range(count))]
+    return bits
+
+
+def bit_of(axis, bit):
+    return (lax.axis_index(axis) // 2**bit) % 2
+
+
+def stage_orders():
+    bits = index_bits()
+    inner = [("clip", 0)] if lax.axis_size("clip") > 1 else []
+    tm = [b for b in bits if b[0] == "tm"]
+    clip = [b for b in bits if b[0] == "clip" and b not in inner]
+    space = [b for b in bits if b[0] == "space"]
+    return inner + tm + clip + space, inner + clip + tm + space
+
+
+def gather_all(shard, order):
+    bits = index_bits()
+    out = shard.reshape((1,) * len(bits) + shard.shape)
+    for axis, bit in reversed(order):
+        dim = bits.index((axis, bit))
+        other = partner(out, axis, bit)
+        out = jnp.where(
+            bit_of(axis, bit) == 1,
+            jnp.concatenate([other, out], dim),
+            jnp.concatenate([out, other], dim),
+        )
+    return out.reshape((-1,) + shard.shape[1:])
+
+
+def scatter_all(grad, order):
+    bits = index_bits()
+    width = grad.shape[-1]
+    out = grad.reshape((2,) * len(bits) + (-1, width))
+    for axis, bit in order:
+        dim = bits.index((axis, bit))
+        here = bit_of(axis, bit)
+        mine = lax.dynamic_slice_in_dim(out, here, 1, dim)
+        sent = lax.dynamic_slice_in_dim(out, 1 - here, 1, dim).astype(BF16)
+        out = mine + partner(sent, axis, bit).astype(F32)
+    return out.reshape(-1, width)
+
+
+def table_shift_matrix():
+    shift = np.zeros((CELLS, 256, 128), np.float32)
+    for row in range(WIN_HW):
+        for col in range(WIN_HW):
+            offset = (WIN_HW - 1 - row) * SPAN + WIN_HW - 1 - col
+            for m in range((WIN_HW - 1) * SPAN + WIN_HW):
+                shift[row * WIN_HW + col, m + offset, m] = 1
+    return shift
+
+
+def cell_spread():
+    spread = np.zeros((WIN_T * 128, TOKENS), np.float32)
+    for frame in range(WIN_T):
+        for row in range(WIN_HW):
+            for col in range(WIN_HW):
+                spread[frame * 128 + row * SPAN + col, frame * CELLS + row * WIN_HW + col] = 1
+    return spread
+
+
+def bias_kernel(slab_ref, spread_ref, out_ref):
+    spread = spread_ref[...]
+    for key_frame in range(WIN_T):
+        first = WIN_T - 1 - key_frame
+        slabs = jnp.concatenate([slab_ref[0, first + n] for n in range(WIN_T)], axis=1)
+        out_ref[0, key_frame * CELLS : (key_frame + 1) * CELLS, :] = mm(slabs, spread) * LOG2E
+
+
+def table_to_bias(tables):
+    layers, heads, _ = tables.shape
+    slabs = tables.reshape(layers * heads, STEPS, SPAN * SPAN)
+    slabs = jnp.pad(slabs, ((0, 0), (0, 0), (0, 256 - SPAN * SPAN)))
+    shift = jnp.asarray(table_shift_matrix(), BF16)
+    shifted = jnp.einsum("hje,kem->hjkm", slabs, shift, preferred_element_type=F32).astype(BF16)
+    return call(
+        bias_kernel,
+        (layers * heads,),
+        [
+            pl.BlockSpec((1, STEPS, CELLS, 128), lambda h: (h, 0, 0, 0)),
+            whole_block((WIN_T * 128, TOKENS)),
+        ],
+        pl.BlockSpec((1, TOKENS, TOKENS), lambda h: (h, 0, 0)),
+        jax.ShapeDtypeStruct((layers * heads, TOKENS, TOKENS), F32),
+        2 * layers * heads * TOKENS * WIN_T * 128 * TOKENS,
+    )(shifted, jnp.asarray(cell_spread(), BF16))
+
+
+def bias_grad_to_table(parts):
+    shift = jnp.asarray(table_shift_matrix(), F32)
+    table = jnp.einsum(
+        "hjkm,kem->hje", parts, shift, precision=lax.Precision.HIGH, preferred_element_type=F32
+    )
+    return table[:, :, : SPAN * SPAN].reshape(parts.shape[0], -1)
+
+
+def unit_rows(x):
+    centered = x - jnp.mean(x, axis=-1, keepdims=True)
+    inverse = lax.rsqrt(jnp.mean(centered * centered, axis=-1, keepdims=True) + 1e-05)
+    return centered * inverse, inverse
+
+
+def norm_back(grad, unit, inverse, gain):
+    scaled = grad * gain
+    return inverse * (
+        scaled
+        - jnp.mean(scaled, axis=-1, keepdims=True)
+        - unit * jnp.mean(scaled * unit, axis=-1, keepdims=True)
+    )
+
+
+def qkv_kernel(x_ref, vec_ref, w_ref, out_ref):
+    width = x_ref.shape[-1]
+    unit, _ = unit_rows(x_ref[0].astype(F32))
+    normed = (unit * vec_ref[0:1] + vec_ref[1:2]).astype(BF16)
+    for part in range(3):
+        cols = slice(part * width, (part + 1) * width)
+        out = mm(normed, w_ref[:, cols])
+        if part == 0:
+            out = out + vec_ref[2:3]
+        if part == 2:
+            out = out + vec_ref[3:4]
+        out_ref[0, :, cols] = out.astype(BF16)
+
+
+def run_qkv(x, vec, w_qkv):
+    windows, _, width = x.shape
+    return call(
+        qkv_kernel,
+        (windows,),
+        [win_block(width), whole_block(vec.shape), whole_block(w_qkv.shape)],
+        win_block(3 * width),
+        jax.ShapeDtypeStruct((windows, TOKENS, 3 * width), BF16),
+        2 * windows * TOKENS * width * 3 * width,
+    )(x, vec, w_qkv)
+
+
+GROUP = 4
+
+
+def head_masks(head_size):
+    lane = lax.broadcasted_iota(jnp.int32, (1, GROUP * head_size), 1)
+    return [
+        jnp.where((lane >= h * head_size) & (lane < (h + 1) * head_size), 1.0, 0.0).astype(BF16)
+        for h in range(GROUP)
+    ]
+
+
+def attend_kernel(shifted, head_size, q_ref, k_ref, v_ref, bias_ref, col_ref, row_ref, out_ref, log_ref):
+    q, k = q_ref[0], k_ref[0]
+    turned = v_ref[0].astype(F32).T.astype(BF16)
+    factor = head_size**-0.5 * LOG2E
+    masks = head_masks(head_size)
+    outs, logs = [], []
+    for h in range(GROUP):
+        scores = mm(k * masks[h], q, 1, 1) * factor + bias_ref[h]
+        if shifted:
+            scores = jnp.where(col_ref[0] == row_ref[0], scores, masked_score)
+        peak = jnp.max(scores, axis=0, keepdims=True)
+        raised = jnp.exp2(scores - peak)
+        total = jnp.sum(raised, axis=0, keepdims=True)
+        mixed = mm(turned[h * head_size : (h + 1) * head_size], raised.astype(BF16))
+        outs.append(mixed / total)
+        logs.append(peak + jnp.log2(total))
+    out_ref[0] = jnp.concatenate(outs, axis=0).T.astype(BF16)
+    log_ref[0, 0] = jnp.concatenate(logs + logs, axis=0)
+
+
+def attend_specs(width):
+    wide = GROUP * (width // HEADS)
+    groups = HEADS // GROUP
+    qkv = [
+        pl.BlockSpec((1, TOKENS, wide), lambda g, w, p=part: (w, 0, p * groups + g))
+        for part in range(3)
+    ]
+    bias = pl.BlockSpec((GROUP, TOKENS, TOKENS), lambda g, w: (g, 0, 0))
+    col = pl.BlockSpec((1, TOKENS, 1), lambda g, w: (w, 0, 0))
+    row = pl.BlockSpec((1, 1, TOKENS), lambda g, w: (w, 0, 0))
+    flat = pl.BlockSpec((1, TOKENS, wide), lambda g, w: (w, 0, g))
+    log = pl.BlockSpec((1, 1, 2 * GROUP, TOKENS), lambda g, w: (w, g, 0, 0))
+    return qkv, bias, col, row, flat, log
+
+
+def run_attend(qkv, bias, labels, shifted):
+    windows, _, width3 = qkv.shape
+    width = width3 // 3
+    groups = HEADS // GROUP
+    qkv_specs, bias_spec, col, row, flat, log = attend_specs(width)
+    return call(
+        functools.partial(attend_kernel, shifted, width // HEADS),
+        (groups, windows),
+        qkv_specs + [bias_spec, col, row],
+        [flat, log],
+        [
+            jax.ShapeDtypeStruct((windows, TOKENS, width), BF16),
+            jax.ShapeDtypeStruct((windows, groups, 2 * GROUP, TOKENS), F32),
+        ],
+        32 * windows * TOKENS * TOKENS * width,
+    )(qkv, qkv, qkv, bias, labels[0], labels[1])
+
+
+def attend_back_kernel(
+    shifted, head_size, q_ref, k_ref, v_ref, g_ref, bias_ref, col_ref, row_ref, log_ref, spread_ref,
+    dq_ref, dk_ref, dv_ref, table_ref, sum_ref, slab_ref,
+):
+    w = pl.program_id(1)
+    q, k, v, g = q_ref[0], k_ref[0], v_ref[0], g_ref[0]
+    turned = k.astype(F32).T.astype(BF16)
+    scale = head_size**-0.5
+    factor = scale * LOG2E
+    masks = head_masks(head_size)
+    grad_q, grad_k, grad_v = [], None, None
+    for h in range(GROUP):
+        scores = mm(k * masks[h], q, 1, 1) * factor + bias_ref[h]
+        if shifted:
+            scores = jnp.where(col_ref[0] == row_ref[0], scores, masked_score)
+        probs = jnp.exp2(scores - log_ref[0, 0, h : h + 1])
+        grad_probs = mm(v * masks[h], g, 1, 1)
+        inner = jnp.sum(probs * grad_probs, axis=0, keepdims=True)
+        grad_scores = (probs * (grad_probs - inner)).astype(BF16)
+        part_v = mm(probs.astype(BF16), g * masks[h])
+        part_k = mm(grad_scores, q * masks[h])
+        grad_v = part_v if grad_v is None else grad_v + part_v
+        grad_k = part_k if grad_k is None else grad_k + part_k
+        grad_q.append(mm(turned[h * head_size : (h + 1) * head_size], grad_scores))
+
+        @pl.when(w == 0)
+        def _():
+            sum_ref[h] = grad_scores.astype(F32)
+
+        @pl.when(w != 0)
+        def _():
+            sum_ref[h] += grad_scores.astype(F32)
+
+    dq_ref[0] = (jnp.concatenate(grad_q, axis=0) * scale).T.astype(BF16)
+    dk_ref[0] = (grad_k * scale).astype(BF16)
+    dv_ref[0] = grad_v.astype(BF16)
+
+    @pl.when(w == pl.num_programs(1) - 1)
+    def _():
+        spread = spread_ref[...]
+        for h in range(GROUP):
+            slab_ref[...] = jnp.zeros_like(slab_ref)
+            for key_frame in range(WIN_T):
+                rows = sum_ref[h, key_frame * CELLS : (key_frame + 1) * CELLS, :]
+                first = (WIN_T - 1 - key_frame) * 128
+                slab_ref[:, first : first + WIN_T * 128] += mm(rows.astype(BF16), spread, 1, 1)
+            for step in range(STEPS):
+                table_ref[h, step] = slab_ref[:, step * 128 : (step + 1) * 128]
+
+
+def run_attend_back(qkv, grad, bias, labels, log, shifted):
+    windows, _, width3 = qkv.shape
+    width = width3 // 3
+    groups = HEADS // GROUP
+    qkv_specs, bias_spec, col, row, flat, log_spec = attend_specs(width)
+    flat_shape = jax.ShapeDtypeStruct((windows, TOKENS, width), BF16)
+    return call(
+        functools.partial(attend_back_kernel, shifted, width // HEADS),
+        (groups, windows),
+        qkv_specs + [flat, bias_spec, col, row, log_spec]
+        + [pl.BlockSpec((WIN_T * 128, TOKENS), lambda g, w: (0, 0))],
+        [flat, flat, flat, pl.BlockSpec((GROUP, STEPS, CELLS, 128), lambda g, w: (g, 0, 0, 0))],
+        [flat_shape] * 3 + [jax.ShapeDtypeStruct((HEADS, STEPS, CELLS, 128), F32)],
+        80 * windows * TOKENS * TOKENS * width,
+        [pltpu.VMEM((GROUP, TOKENS, TOKENS), F32), pltpu.VMEM((CELLS, STEPS * 128), F32)],
+    )(qkv, qkv, qkv, grad, bias, labels[0], labels[1], log, jnp.asarray(cell_spread(), BF16))
+
+
+def branch_kernel(x_ref, att_ref, vec_ref, wo_ref, w1_ref, w2_ref, mid_ref, hid_ref, slope_ref, out_ref):
+    chunk = 512
+    middle = x_ref[0].astype(F32) + mm(att_ref[0], wo_ref[...]) + vec_ref[4:5]
+    mid_ref[0] = middle
+    unit, _ = unit_rows(middle)
+    normed = (unit * vec_ref[5:6] + vec_ref[6:7]).astype(BF16)
+    after = middle + vec_ref[7:8]
+    for n in range(w1_ref.shape[1] // chunk):
+        cols = slice(n * chunk, (n + 1) * chunk)
+        pre = mm(normed, w1_ref[:, cols]) + vec_ref[8 + n : 9 + n]
+        below = 0.5 * (1.0 + lax.erf(pre * math.sqrt(0.5)))
+        bell = jnp.exp(-0.5 * pre * pre) * (1.0 / math.sqrt(2 * math.pi))
+        hidden = (pre * below).astype(BF16)
+        hid_ref[0, :, cols] = hidden
+        slope_ref[0, :, cols] = (below + pre * bell).astype(BF16)
+        after = after + mm(hidden, w2_ref[cols, :])
+    out_ref[0] = after.astype(out_ref.dtype)
+
+
+def run_branch(x, attended, vec, w_mid, w2, out_dtype):
+    windows, _, width = x.shape
+    wide = w2.shape[0]
+    return call(
+        branch_kernel,
+        (windows,),
+        [
+            win_block(width),
+            win_block(width),
+            whole_block(vec.shape),
+            pl.BlockSpec((width, width), lambda w: (0, wide // width)),
+            pl.BlockSpec((width, wide), lambda w: (0, 0)),
+            whole_block(w2.shape),
+        ],
+        [win_block(width), win_block(wide), win_block(wide), win_block(width)],
+        [
+            jax.ShapeDtypeStruct((windows, TOKENS, width), F32),
+            jax.ShapeDtypeStruct((windows, TOKENS, wide), BF16),
+            jax.ShapeDtypeStruct((windows, TOKENS, wide), BF16),
+            jax.ShapeDtypeStruct((windows, TOKENS, width), out_dtype),
+        ],
+        2 * windows * TOKENS * width * (width + 2 * wide),
+    )(x, attended, vec, w_mid, w_mid, w2)
+
+
+def add_rows(ref, rows, value):
+    ref[rows, :] += jnp.sum(value.astype(F32), axis=0, keepdims=True)
+
+
+def branch_back_kernel(
+    grad_ref, mid_ref, att_ref, hid_ref, slope_ref, vec_ref, wo_ref, w1_ref, w2_ref,
+    gm_ref, ga_ref, d1_ref, d2_ref, vecs_ref,
+):
+    chunk = 512
+    wide = w2_ref.shape[0]
+
+    @pl.when(pl.program_id(0) == 0)
+    def _():
+        d1_ref[...] = jnp.zeros_like(d1_ref)
+        d2_ref[...] = jnp.zeros_like(d2_ref)
+        vecs_ref[...] = jnp.zeros_like(vecs_ref)
+
+    grad = grad_ref[0].astype(F32)
+    branch = grad.astype(BF16)
+    unit, inverse = unit_rows(mid_ref[0])
+    normed = (unit * vec_ref[5:6] + vec_ref[6:7]).astype(BF16)
+    add_rows(vecs_ref, slice(7, 8), branch)
+    back = None
+    for n in range(wide // chunk):
+        cols = slice(n * chunk, (n + 1) * chunk)
+        d2_ref[cols, :] += mm(hid_ref[0, :, cols], branch, 0, 0)
+        grad_pre = mm(branch, w2_ref[cols, :], 1, 1) * slope_ref[0, :, cols].astype(F32)
+        add_rows(vecs_ref, slice(8 + n, 9 + n), grad_pre.astype(BF16))
+        grad_pre = grad_pre.astype(BF16)
+        d1_ref[:, cols] += mm(normed, grad_pre, 0, 0)
+        part = mm(grad_pre, w1_ref[:, cols], 1, 1)
+        back = part if back is None else back + part
+    add_rows(vecs_ref, slice(5, 6), back * unit)
+    add_rows(vecs_ref, slice(6, 7), back)
+    middle_grad = grad + norm_back(back, unit, inverse, vec_ref[5:6])
+    gm_ref[0] = middle_grad
+    branch = middle_grad.astype(BF16)
+    add_rows(vecs_ref, slice(4, 5), branch)
+    d1_ref[:, wide:] += mm(att_ref[0], branch, 0, 0)
+    ga_ref[0] = mm(branch, wo_ref[...], 1, 1).astype(BF16)
+
+
+def run_branch_back(grad, middle, attended, hidden, slope, vec, w_mid, w2):
+    windows, _, width = middle.shape
+    wide = w2.shape[0]
+    flat = win_block(width)
+    return call(
+        branch_back_kernel,
+        (windows,),
+        [
+            flat,
+            flat,
+            flat,
+            win_block(wide),
+            win_block(wide),
+            whole_block(vec.shape),
+            pl.BlockSpec((width, width), lambda w: (0, wide // width)),
+            pl.BlockSpec((width, wide), lambda w: (0, 0)),
+            whole_block(w2.shape),
+        ],
+        [flat, flat, whole_block(w_mid.shape), whole_block(w2.shape), whole_block(vec.shape)],
+        [
+            jax.ShapeDtypeStruct((windows, TOKENS, width), F32),
+            jax.ShapeDtypeStruct((windows, TOKENS, width), BF16),
+            jax.ShapeDtypeStruct(w_mid.shape, F32),
+            jax.ShapeDtypeStruct(w2.shape, F32),
+            jax.ShapeDtypeStruct(vec.shape, F32),
+        ],
+        4 * windows * TOKENS * width * (width + 2 * wide),
+    )(grad, middle, attended, hidden, slope, vec, w_mid, w_mid, w2)
+
+
+def qkv_back_kernel(dq_ref, dk_ref, dv_ref, x_ref, gm_ref, vec_ref, w_ref, out_ref, dw_ref, vecs_ref):
+    width = x_ref.shape[-1]
+
+    @pl.when(pl.program_id(0) == 0)
+    def _():
+        dw_ref[...] = jnp.zeros_like(dw_ref)
+        vecs_ref[...] = jnp.zeros_like(vecs_ref)
+
+    unit, inverse = unit_rows(x_ref[0].astype(F32))
+    normed = (unit * vec_ref[0:1] + vec_ref[1:2]).astype(BF16)
+    back = None
+    for part, ref in enumerate((dq_ref, dk_ref, dv_ref)):
+        cols = slice(part * width, (part + 1) * width)
+        grad = ref[0]
+        dw_ref[:, cols] += mm(normed, grad, 0, 0)
+        here = mm(grad, w_ref[:, cols], 1, 1)
+        back = here if back is None else back + here
+        if part == 0:
+            add_rows(vecs_ref, slice(2, 3), grad)
+        if part == 2:
+            add_rows(vecs_ref, slice(3, 4), grad)
+    add_rows(vecs_ref, slice(0, 1), back * unit)
+    add_rows(vecs_ref, slice(1, 2), back)
+    out_ref[0] = (gm_ref[0] + norm_back(back, unit, inverse, vec_ref[0:1])).astype(out_ref.dtype)
+
+
+def run_qkv_back(grads, x, grad_middle, vec, w_qkv, out_dtype):
+    windows, _, width = x.shape
+    flat = win_block(width)
+    return call(
+        qkv_back_kernel,
+        (windows,),
+        [flat] * 5 + [whole_block(vec.shape), whole_block(w_qkv.shape)],
+        [flat, whole_block(w_qkv.shape), whole_block((8, width))],
+        [
+            jax.ShapeDtypeStruct((windows, TOKENS, width), out_dtype),
+            jax.ShapeDtypeStruct(w_qkv.shape, F32),
+            jax.ShapeDtypeStruct((8, width), F32),
+        ],
+        4 * windows * TOKENS * width * 3 * width,
+    )(*grads, x, grad_middle, vec, w_qkv)
+
+
+def vectors_in(shards):
+    gain_one, bias_one, mix_bias, proj_bias, gain_two, bias_two, wide_bias, narrow_bias = shards
+    own = gain_one.shape[1]
+    rows = []
+    for v in (gain_one, bias_one, mix_bias, proj_bias, gain_two, bias_two, narrow_bias, wide_bias):
+        rows.append(v.reshape(LAYERS, -1, own))
+    block = jnp.concatenate(rows, axis=1)
+    block = block.transpose(1, 0, 2).reshape(block.shape[1], LAYERS * own)
+    return jnp.pad(block, ((0, 16 - block.shape[0]), (0, 128 - block.shape[1])))
+
+
+def vectors_whole(blocks, own):
+    devices = blocks.shape[0] // 16
+    parts = blocks.reshape(devices, 16, 128)[:, :, : LAYERS * own]
+    parts = parts.reshape(devices, 16, LAYERS, own).transpose(2, 0, 1, 3).astype(F32)
+
+    def joined(first, count):
+        return parts[:, :, first : first + count].reshape(LAYERS, -1, devices * own)
+
+    singles = parts.transpose(0, 2, 1, 3).reshape(LAYERS, 16, devices * own)
+    return jnp.concatenate(
+        [singles[:, 0:2], joined(2, 2), singles[:, 4:8], joined(8, 4), singles[:, 12:16]], axis=1
+    )
+
+
+def vectors_split(rows, devices):
+    own = rows.shape[1] // devices
+
+    def shared(first, count):
+        return rows[first : first + count].reshape(devices, count, own)
+
+    singles = rows.reshape(16, devices, own).transpose(1, 0, 2)
+    block = jnp.concatenate(
+        [singles[:, 0:2], shared(2, 2), singles[:, 4:8], shared(8, 4), singles[:, 12:16]], axis=1
+    )
+    return jnp.pad(block, ((0, 0), (0, 0), (0, 128 - own))).reshape(devices * 16, 128)
+
+
+def after_that(value, *others):
+    return lax.optimization_barrier((value,) + others)[0]
+
+
+def window_labels(frames_here, windows):
+    token = np.arange(TOKENS)
+    late_t = token // CELLS >= WIN_T - WIN_T // 2
+    late_r = token // WIN_HW % WIN_HW >= WIN_HW - WIN_HW // 2
+    late_c = token % WIN_HW >= WIN_HW - WIN_HW // 2
+    quadrant = lax.axis_index("space")
+    last = (lax.axis_index("tm") == lax.axis_size("tm") - 1).astype(jnp.int32)
+    at_end = last * (jnp.arange(windows) == windows - 1).astype(jnp.int32)
+    label = (
+        4 * at_end[:, None] * jnp.asarray(late_t, jnp.int32)
+        + 2 * (quadrant // 2) * jnp.asarray(late_r, jnp.int32)
+        + (quadrant % 2) * jnp.asarray(late_c, jnp.int32)
+    ).astype(F32)
+    return label[:, :, None], label[:, None, :]
+
+
+def local_windows(
+    clips_in,
+    ln1_gain,
+    ln1_bias,
+    qkv_weight,
+    qv_bias,
+    out_weight,
+    out_bias,
+    ln2_gain,
+    ln2_bias,
+    fc1_weight,
+    fc1_bias,
+    fc2_weight,
+    fc2_bias,
+    pos_table,
+    out_grad,
+):
+    _, frames_here, _, _, width = clips_in.shape
+    windows = frames_here // WIN_T
+    own = ln1_gain.shape[1]
+    devices = width // own
+    one, two = stage_orders()
+    half = 3 * width // 2
+    flat = (windows, TOKENS, width)
+
+    small = vectors_in(
+        (ln1_gain, ln1_bias, qv_bias, out_bias, ln2_gain, ln2_bias, fc1_bias, fc2_bias)
+    )
+    first = gather_all(jnp.concatenate([qkv_weight[0][:, :half], small], axis=1), one)
+    second = gather_all(qkv_weight[0][:, half:], two)
+    vec = vectors_whole(first[:, half:], own)
+    w_qkv = [jnp.concatenate([first[:, :half], second], axis=1), None]
+
+    tables = pos_table.transpose(0, 2, 1)
+    beside = partner(tables, "tm", 0)
+    tables = jnp.where(
+        lax.axis_index("tm") == 1,
+        jnp.concatenate([beside, tables], 1),
+        jnp.concatenate([tables, beside], 1),
+    )
+    bias = table_to_bias(tables).reshape(LAYERS, HEADS, TOKENS, TOKENS)
+    labels = window_labels(frames_here, windows)
+    send, place, stay, rows, starts, kinds = halo_matrices(frames_here)
+
+    w_mid, w_two = [], []
+    gate = (first, second)
+    for layer in range(LAYERS):
+        if layer > 0:
+            shard = after_that(qkv_weight[layer], *gate)
+            parts = (gather_all(shard[:, :half], one), gather_all(shard[:, half:], two))
+            w_qkv[layer] = jnp.concatenate(parts, axis=1)
+            gate = parts
+        shard = jnp.concatenate([fc1_weight[layer], out_weight[layer]], axis=1)
+        shard, down = lax.optimization_barrier((shard, fc2_weight[layer]) + gate)[:2]
+        w_mid.append(gather_all(shard, one))
+        w_two.append(gather_all(down, two))
+        gate = (w_mid[-1], w_two[-1])
+
+    stream0 = clips_in.reshape(flat)
+    qkv0 = run_qkv(stream0, vec[0], w_qkv[0])
+    att0, log0 = run_attend(qkv0, bias[0], labels, False)
+    mid0, hid0, slope0, stream1 = run_branch(stream0, att0, vec[0], w_mid[0], w_two[0], F32)
+    came = halo_permute(halo_pack(stream1, send, True), rows, starts, kinds, True)
+    rolled1 = halo_unpack(stream1, came, stay, place, starts, F32, center=True)
+    qkv1 = run_qkv(rolled1, vec[1], w_qkv[1])
+    att1, log1 = run_attend(qkv1, bias[1], labels, True)
+    mid1, hid1, slope1, rolled_out = run_branch(rolled1, att1, vec[1], w_mid[1], w_two[1], F32)
+    back = halo_permute(halo_pack(rolled_out, place.T, False), rows, starts, kinds, False)
+    clips_out = halo_unpack(rolled_out, back, stay.T, send.T, starts, BF16, mean_of=stream1)
+
+    grad_in = after_that(out_grad, *gate).reshape(flat)
+    came = halo_permute(halo_pack(grad_in, send, False), rows, starts, kinds, True)
+    grad = halo_unpack(grad_in, came, stay, place, starts, BF16)
+
+    kept = (
+        (stream0, qkv0, att0, log0, mid0, hid0, slope0),
+        (rolled1, qkv1, att1, log1, mid1, hid1, slope1),
+    )
+    shares, table_parts = [None] * LAYERS, [None] * LAYERS
+    for layer in reversed(range(LAYERS)):
+        stream, qkv, att, log, mid, hid, slope = kept[layer]
+        grad_mid, grad_att, d_mid, d_two, vecs = run_branch_back(
+            grad, mid, att, hid, slope, vec[layer], w_mid[layer], w_two[layer]
+        )
+        mid_share = scatter_all(d_mid, one)
+        two_share = scatter_all(d_two, two)
+        *grads, table = run_attend_back(qkv, grad_att, bias[layer], labels, log, layer == 1)
+        grad_stream, d_qkv, vecs_one = run_qkv_back(
+            grads, stream, grad_mid, vec[layer], w_qkv[layer], F32 if layer else BF16
+        )
+        vecs = jnp.concatenate([vecs_one[:4], vecs[4:]], axis=0)
+        packed = jnp.concatenate([d_qkv[:, :half], vectors_split(vecs, devices)], axis=1)
+        left = scatter_all(packed, one)
+        right = scatter_all(d_qkv[:, half:], two)
+        shares[layer] = (mid_share, two_share, left, right)
+        table = bias_grad_to_table(table)
+        heads_here = pos_table.shape[2]
+        mine = lax.dynamic_slice_in_dim(table, lax.axis_index("tm") * heads_here, heads_here, 0)
+        theirs = lax.dynamic_slice_in_dim(
+            table, (1 - lax.axis_index("tm")) * heads_here, heads_here, 0
+        )
+        table = mine + partner(theirs, "tm", 0)
+        for axis, bit in one:
+            if axis != "tm":
+                table = table + partner(table, axis, bit)
+        table_parts[layer] = table
+        if layer:
+            back = halo_permute(halo_pack(grad_stream, place.T, False), rows, starts, kinds, False)
+            grad = halo_unpack(grad_stream, back, stay.T, send.T, starts, F32)
+    in_grad = grad_stream
+
+    wide = fc1_weight.shape[2]
+    mid_share, two_share, left, right = (jnp.stack(s) for s in zip(*shares))
+    small = left[:, :, half : half + own]
+
+    def vector(row, count=1):
+        return small[:, row : row + count].reshape(LAYERS, count * own)
+
+    return (
+        clips_out.reshape(clips_in.shape),
+        in_grad.reshape(clips_in.shape),
+        vector(0),
+        vector(1),
+        jnp.concatenate([left[:, :, :half], right], axis=2),
+        vector(2, 2),
+        mid_share[:, :, wide:],
+        vector(4),
+        vector(5),
+        vector(6),
+        mid_share[:, :, :wide],
+        vector(8, 4),
+        two_share,
+        vector(7),
+        jnp.stack(table_parts).transpose(0, 2, 1),
+    )
+
+
+def windows_are_local(mesh):
+    def decide(clips_in, *rest):
+        clips, frames_here = clips_in.shape[:2]
+        own = rest[0].shape[1]
+        return (
+            clips == 1
+            and frames_here % WIN_T == 0
+            and own == 16
+            and mesh.shape["tm"] == 2
+            and mesh.shape["space"] == 4
+        )
+
+    def program(*args):
+        return local_windows(*args) if decide(*args) else per_device(*args)
+
+    return program
+
+
 def solution(mesh):
     placed = (
         P("clip", "tm", "space", None, None),
@@ -519,7 +1320,7 @@
         P("clip", "tm", "space", None, None),
     )
     return jax.shard_map(
-        per_device,
+        windows_are_local(mesh),
         mesh=mesh,
         in_specs=placed,
         out_specs=(

time: 3800 us -> 909 us (0.24)
  other arithmetic: 1810 us -> 32.8 us
  local copies, waits for them, and re-layouts: 1350 us -> 110 us
  Pallas kernels: 0 us -> 368 us
  matrix products: 230 us -> 20.6 us
  blocking collectives: 186 us -> 0 us
  waiting for transfers between devices: 123 us -> 237 us
  starting transfers between devices: 63.8 us -> 130 us
    scatter-add x2 -> x0, other arithmetic: 1640 us -> none  [layer_backward(): jnp.zeros(table.shape, jnp.float32).at[rel]]
    gather x4 -> x0, local copies, waits for them, and re-layouts: 698 us -> none  [table_bias(): return table.astype(jnp.float32)[rel].transpose(2, 0, 1)]
    pallas_call x0 -> x21, Pallas kernels: none -> 368 us  [the longest x2 153 us: run_attend_back(): call(functools.partial(attend_back_kernel, shifted, width // HEADS), (gro...]
    unnamed x378 -> x98, local copies, waits for them, and re-layouts: 245 us -> 11.3 us
    dot_general x36 -> x3, matrix products: 230 us -> 20.6 us  [the longest x2 17 us: bias_grad_to_table(): jnp.einsum('hjkm,kem->hje', parts, shift, precision=lax.Precision.HIGH, p...]
    ppermute x8 -> x91, waiting for transfers between devices: 83.6 us -> 227 us  [partner(): return lax.ppermute(value, axis, pairs)]
    reshape x38 -> x27, local copies, waits for them, and re-layouts: 148 us -> 19 us  [the longest x8 5.5 us: vectors_in(): rows.append(v.reshape(LAYERS, -1, own))]
    all_gather x2 -> x0, blocking collectives: 90.8 us -> none  [gather_layer(): lax.all_gather(parts[4], ('tm', 'space', 'clip'), axis=0, tiled=True)]
  transfers between devices with their start and end apart: 38 -> 119, of which waited for: 10 -> 55; matrix products, arithmetic and copies ran while one was open for 86% -> 16% of each run, Pallas kernels for 0% -> 38%
where the time goes in v1:
time: 909 us; the launch traced here: 902 us
  Pallas kernels  368 us (40%)
  waiting for transfers between devices  237 us (26%)
  starting transfers between devices  130 us (14%)
  local copies, waits for them, and re-layouts  110 us (12%)
  other arithmetic  32.8 us (4%)
  matrix products  20.6 us (2%)
    ppermute x91, waiting for transfers between devices, partner(): return lax.ppermute(value, axis, pairs)  227 us
    pallas_call x2, Pallas kernels, run_attend_back(): call(functools.partial(attend_back_kernel, shifted, width // HEADS), (gro...  153 us
    ppermute x91, starting transfers between devices, partner(): return lax.ppermute(value, axis, pairs)  82.3 us
    pallas_call x1, Pallas kernels, table_to_bias(): call(bias_kernel, (layers * heads,), [pl.BlockSpec((1, STEPS, CELLS, 128)...  53.5 us
    ppermute x28, starting transfers between devices, halo_permute(): came.append(lax.ppermute(piece, ('tm', 'space'), pairs))  47.9 us
    pallas_call x2, Pallas kernels, run_branch_back(): call(branch_back_kernel, (windows,), [flat, flat, flat, win_block(wide),...  38.5 us
    pallas_call x2, Pallas kernels, run_attend(): call(functools.partial(attend_kernel, shifted, width // HEADS), (groups,...  36.2 us
    pallas_call x2, Pallas kernels, run_branch(): call(branch_kernel, (windows,), [win_block(width), win_block(width), whol...  23.1 us
  transfers between devices with their start and end apart: 119, of which 55 were waited for; matrix products, arithmetic and copies ran while one was open for 16% of the time, Pallas kernels for 38%

profile of v1, /device:TPU:0, one launch (start us, length us, event | category | flops | bytes accessed | tf_op | source)
XLA Modules:
  0.0 902.0 jit_solution(13699397928587103243)
XLA Ops:
  36.0 53.5 %shard_map.452 = f32[32,392,392]{2,1,0:T(8,128)} custom-call(bf16[32,15,49,128]{3,2,1,0:T(8,128)(2,1)} %copy.218.slab_ref, bf16[1024,392]{1,0:T(8,128)(2,1)} %constant.434.clone.spread_ref), custom_call_target="tpu_custom_call" | custom-call | flops 10070523904 | bytes 8388608 | tf_op jit(solution)/shard_map/pallas_call | solution.py:738
  101.0 16.6 %fusion.90 = (f32[16,392,392]{2,1,0:T(8,128)}, f32[16,392,392]{2,1,0:T(8,128)}) fusion(f32[32,392,392]{2,1,0:T(8,128)} %shard_map.452), kind=kLoop, calls=%fused_computation.310 | loop fusion | bytes 39337984 | tf_op jit(solution)/shard_map/slice | solution.py:1214
  129.7 8.0 collective-permute-done.17
  142.1 7.4 collective-permute-done.13
  153.1 11.7 %collective-permute-done.14 = bf16[1,2,2,2,1,16,2560]{6,5,2,1,3,4,0:T(8,128)(2,1)S(1)} collective-permute-done((bf16[1,2,2,2,1,16,2560]{6,5,2,1,3,4,0:T(8,128)(2,1)S(1)}, bf16[1,2,2,2,1,16,2560]{6,5,2,1,3,4,0:T(8,128)(2,1)S(1)}, u32[]{:S(2)}, u32[]{:S(2)}) %collective-permute-start.14) | collective-permute-done | bytes 655392 | tf_op jit(solution)/shard_map/ppermute | solution.py:24
  172.4 17.8 %shard_map.453 = (bf16[2,392,512]{2,1,0:T(8,128)(2,1)}, f32[2,4,8,392]{3,2,1,0:T(8,128)}) custom-call(bf16[2,392,1536]{2,1,0:T(8,128)(2,1)} %shard_map.451.q_ref.k_ref.v_ref, bf16[2,392,1536]{2,1,0:T(8,128)(2,1)} %shard_map.451.q_ref.k_ref.v_ref, bf16[2,392,1536]{2,1,0:T(8,128)(2,1)} %shard_map.451.q_ref.k_ref.v_ref, ...), custom_call_target="tpu_custom_call" | custom-call | flops 5035261952 | bytes 8388608 | tf_op jit(solution)/shard_map/pallas_call | solution.py:851
  196.3 11.7 %shard_map.454 = (f32[2,392,512]{2,1,0:T(8,128)}, bf16[2,392,2048]{2,1,0:T(8,128)(2,1)}, bf16[2,392,2048]{2,1,0:T(8,128)(2,1)}, f32[2,392,512]{2,1,0:T(8,128)}) custom-call(bf16[2,392,512]{2,1,0:T(8,128)(2,1)} %reshape.6003.x_ref, bf16[2,392,512]{2,1,0:T(8,128)(2,1)} %get-tuple-element.57.att_ref, f32[16,512]{1,0:T(8,128)} %get-tuple-element.215.vec_ref, ...), custom_call_target="tpu_custom_call" | custom-call | flops 3699376128 | bytes 8388608 | tf_op jit(solution)/shard_map/pallas_call | solution.py:954
  261.3 7.8 collective-permute-done.40
  273.1 12.9 %collective-permute-done.41 = bf16[1,2,2,2,1,16,2560]{6,5,4,3,2,1,0:T(8,128)(2,1)S(1)} collective-permute-done((bf16[1,2,2,2,1,16,2560]{6,5,4,3,2,1,0:T(8,128)(2,1)S(1)}, bf16[1,2,2,2,1,16,2560]{6,5,4,3,2,1,0:T(8,128)(2,1)S(1)}, u32[]{:S(2)}, u32[]{:S(2)}) %collective-permute-start.41) | collective-permute-done | bytes 655392 | tf_op jit(solution)/shard_map/ppermute | solution.py:24
  290.9 7.2 collective-permute-done.46
  299.8 6.1 shard_map.456.x_ref
  311.9 18.4 %shard_map.458 = (bf16[2,392,512]{2,1,0:T(8,128)(2,1)}, f32[2,4,8,392]{3,2,1,0:T(8,128)}) custom-call(bf16[2,392,1536]{2,1,0:T(8,128)(2,1)} %shard_map.457.q_ref.k_ref.v_ref, bf16[2,392,1536]{2,1,0:T(8,128)(2,1)} %shard_map.457.q_ref.k_ref.v_ref, bf16[2,392,1536]{2,1,0:T(8,128)(2,1)} %shard_map.457.q_ref.k_ref.v_ref, ...), custom_call_target="tpu_custom_call" | custom-call | flops 5035261952 | bytes 8388608 | tf_op jit(solution)/shard_map/pallas_call | solution.py:851
  344.2 11.5 %shard_map.459 = (f32[2,392,512]{2,1,0:T(8,128)}, bf16[2,392,2048]{2,1,0:T(8,128)(2,1)}, bf16[2,392,2048]{2,1,0:T(8,128)(2,1)}, f32[2,392,512]{2,1,0:T(8,128)}) custom-call(f32[2,392,512]{2,1,0:T(8,128)} %shard_map.456.x_ref, bf16[2,392,512]{2,1,0:T(8,128)(2,1)} %get-tuple-element.62.att_ref, f32[16,512]{1,0:T(8,128)} %get-tuple-element.214.vec_ref, ...), custom_call_target="tpu_custom_call" | custom-call | flops 3699376128 | bytes 8388608 | tf_op jit(solution)/shard_map/pallas_call | solution.py:954
  394.4 19.8 %shard_map.464 = (f32[2,392,512]{2,1,0:T(8,128)}, bf16[2,392,512]{2,1,0:T(8,128)(2,1)}, f32[512,2560]{1,0:T(8,128)}, f32[2048,512]{1,0:T(8,128)}, f32[16,512]{1,0:T(8,128)}) custom-call(bf16[2,392,512]{2,1,0:T(8,128)(2,1)} %shard_map.463.grad_ref, f32[2,392,512]{2,1,0:T(8,128)} %get-tuple-element.67.mid_ref, bf16[2,392,512]{2,1,0:T(8,128)(2,1)} %get-tuple-element.62.att_ref, ...), custom_call_target="tpu_custom_call" | custom-call | flops 7398752256 | bytes 8388608 | tf_op jit(solution)/shard_map/pallas_call | solution.py:1022
  414.2 77.6 %shard_map.465 = (bf16[2,392,512]{2,1,0:T(8,128)(2,1)}, bf16[2,392,512]{2,1,0:T(8,128)(2,1)}, bf16[2,392,512]{2,1,0:T(8,128)(2,1)}, f32[16,15,49,128]{3,2,1,0:T(8,128)}) custom-call(bf16[2,392,1536]{2,1,0:T(8,128)(2,1)} %shard_map.457.q_ref.k_ref.v_ref, bf16[2,392,1536]{2,1,0:T(8,128)(2,1)} %shard_map.457.q_ref.k_ref.v_ref, ...), custom_call_target="tpu_custom_call" | custom-call | flops 12588154880 | bytes 8388608 | tf_op jit(solution)/shard_map/pallas_call | solution.py:920
  491.7 9.3 %shard_map.466 = (f32[2,392,512]{2,1,0:T(8,128)}, f32[512,1536]{1,0:T(8,128)}, f32[8,512]{1,0:T(8,128)}) custom-call(bf16[2,392,512]{2,1,0:T(8,128)(2,1)} %get-tuple-element.72.dq_ref, bf16[2,392,512]{2,1,0:T(8,128)(2,1)} %get-tuple-element.73.dk_ref, bf16[2,392,512]{2,1,0:T(8,128)(2,1)} %get-tuple-element.74.dv_ref, f32[2,392,512]{2,1,0:T(8,128)} %shard_map.456.x_ref, ...), custom_call_target="tpu_custom_call" | custom-call | flops 2466250752 | bytes 8388608 | tf_op jit(solution)/shard_map/pallas_call | solution.py:1077
  542.6 8.4 fusion.7
  576.3 18.8 %shard_map.469 = (f32[2,392,512]{2,1,0:T(8,128)}, bf16[2,392,512]{2,1,0:T(8,128)(2,1)}, f32[512,2560]{1,0:T(8,128)}, f32[2048,512]{1,0:T(8,128)}, f32[16,512]{1,0:T(8,128)}) custom-call(f32[2,392,512]{2,1,0:T(8,128)} %shard_map.468.grad_ref, f32[2,392,512]{2,1,0:T(8,128)} %get-tuple-element.77.mid_ref, bf16[2,392,512]{2,1,0:T(8,128)(2,1)} %get-tuple-element.57.att_ref, ...), custom_call_target="tpu_custom_call" | custom-call | flops 7398752256 | bytes 8388608 | tf_op jit(solution)/shard_map/pallas_call | solution.py:1022
  595.1 75.1 %shard_map.470 = (bf16[2,392,512]{2,1,0:T(8,128)(2,1)}, bf16[2,392,512]{2,1,0:T(8,128)(2,1)}, bf16[2,392,512]{2,1,0:T(8,128)(2,1)}, f32[16,15,49,128]{3,2,1,0:T(8,128)}) custom-call(bf16[2,392,1536]{2,1,0:T(8,128)(2,1)} %shard_map.451.q_ref.k_ref.v_ref, bf16[2,392,1536]{2,1,0:T(8,128)(2,1)} %shard_map.451.q_ref.k_ref.v_ref, ...), custom_call_target="tpu_custom_call" | custom-call | flops 12588154880 | bytes 8388608 | tf_op jit(solution)/shard_map/pallas_call | solution.py:920
  670.2 8.7 shard_map.471
  700.7 8.6 fusion.4
  758.2 6.3 collective-permute-done.75
  848.6 13.1 %collective-permute-done.106 = bf16[1,2,2,1,1,64,512]{6,5,4,3,2,1,0:T(8,128)(2,1)S(1)} collective-permute-done((bf16[1,2,2,1,1,64,512]{6,5,4,3,2,1,0:T(8,128)(2,1)S(1)}, bf16[1,2,2,1,1,64,512]{6,5,4,3,2,1,0:T(8,128)(2,1)S(1)}, u32[]{:S(2)}, u32[]{:S(2)}) %collective-permute-start.106) | collective-permute-done | bytes 262176 | tf_op jit(solution)/shard_map/ppermute | solution.py:24
  863.3 8.9 collective-permute-done.107
  (609 shorter events, 454.2 us)
Async XLA Ops:
  23.4 66.0 %collective-permute-start.1 = (bf16[1,1,2,1,1,16,896]{6,5,2,1,3,4,0:T(8,128)(2,1)S(1)}, bf16[1,1,2,1,1,16,896]{6,5,2,1,3,4,0:T(8,128)(2,1)S(1)}, u32[]{:S(2)}, u32[]{:S(2)}) collective-permute-start(bf16[1,1,2,1,1,16,896]{6,5,2,1,3,4,0:T(8,128)(2,1)S(1)} %maximum_select_fusion.45), channel_id=1, source_target_pairs={{0,8},{4,12},{8,0},{12,4},{1,9},{5,13},{9,1},{13,5},{2,10},{6,14},... | collective-permute-start | bytes 172040 | tf_op jit(solution)/shard_map/ppermute | solution.py:24
  25.9 65.6 %collective-permute-start.7 = (bf16[1,2,2,1,1,16,768]{6,5,2,1,4,3,0:T(8,128)(2,1)S(1)}, bf16[1,2,2,1,1,16,768]{6,5,2,1,4,3,0:T(8,128)(2,1)S(1)}, u32[]{:S(2)}, u32[]{:S(2)}) collective-permute-start(bf16[1,2,2,1,1,16,768]{6,5,2,1,4,3,0:T(8,128)(2,1)S(1)} %fusion.34), channel_id=1, source_target_pairs={{0,16},{16,0},{1,17},{17,1},{2,18},{18,2},{3,19},{19,3},{4,20},{20... | collective-permute-start | bytes 294920 | tf_op jit(solution)/shard_map/ppermute | solution.py:24
  236.6 62.4 %collective-permute-start.21 = (bf16[144,512]{1,0:T(8,128)(2,1)}, bf16[144,512]{1,0:T(8,128)(2,1)S(1)}, u32[]{:S(2)}, u32[]{:S(2)}) collective-permute-start(bf16[144,512]{1,0:T(8,128)(2,1)} %get-tuple-element.169), channel_id=1, source_target_pairs={{0,4},{4,0},{8,12},{12,8},{16,20},{20,16},{24,28},{28,24},{1,5},{5... | collective-permute-start | bytes 442376 | tf_op jit(solution)/shard_map/ppermute | solution.py:593
  237.7 50.4 %collective-permute-start.25 = (bf16[48,512]{1,0:T(8,128)(2,1)S(1)}, bf16[48,512]{1,0:T(8,128)(2,1)S(1)}, u32[]{:S(2)}, u32[]{:S(2)}) collective-permute-start(bf16[48,512]{1,0:T(8,128)(2,1)S(1)} %get-tuple-element.167), channel_id=1, source_target_pairs={{0,20},{4,16},{8,28},{12,24},{16,4},{20,0},{24,12},{28,8},{1,21},{... | collective-permute-start | bytes 147464 | tf_op jit(solution)/shard_map/ppermute | solution.py:593
  239.6 48.5 %collective-permute-start.26 = (bf16[48,512]{1,0:T(8,128)(2,1)S(1)}, bf16[48,512]{1,0:T(8,128)(2,1)S(1)}, u32[]{:S(2)}, u32[]{:S(2)}) collective-permute-start(bf16[48,512]{1,0:T(8,128)(2,1)S(1)} %get-tuple-element.166), channel_id=1, source_target_pairs={{0,24},{4,28},{8,16},{12,20},{16,8},{20,12},{24,0},{28,4},{1,25},{... | collective-permute-start | bytes 147464 | tf_op jit(solution)/shard_map/ppermute | solution.py:593
  298.1 35.6 %collective-permute-start.42 = (bf16[2,2,2,2,1,16,2560]{6,5,2,1,3,4,0:T(8,128)(2,1)S(1)}, bf16[2,2,2,2,1,16,2560]{6,5,2,1,3,4,0:T(8,128)(2,1)}, u32[]{:S(2)}, u32[]{:S(2)}) collective-permute-start(bf16[2,2,2,2,1,16,2560]{6,5,2,1,3,4,0:T(8,128)(2,1)S(1)} %maximum_select_fusion.5), channel_id=1, source_target_pairs={{0,1},{1,0},{2,3},{3,2},{4,5},{5,4},{6,7},{7,6},{8,9},{9,8},{10,11... | collective-permute-start | bytes 3932168 | tf_op jit(solution)/shard_map/ppermute | solution.py:24
  298.5 31.9 %collective-permute-start.47 = (bf16[2,2,2,2,1,64,512]{6,5,2,1,0,4,3:T(8,128)(2,1)S(1)}, bf16[2,2,2,2,1,64,512]{6,5,2,1,0,4,3:T(8,128)(2,1)}, u32[]{:S(2)}, u32[]{:S(2)}) collective-permute-start(bf16[2,2,2,2,1,64,512]{6,5,2,1,0,4,3:T(8,128)(2,1)S(1)} %maximum_select_fusion.7), channel_id=1, source_target_pairs={{0,1},{1,0},{2,3},{3,2},{4,5},{5,4},{6,7},{7,6},{8,9},{9,8},{10,11... | collective-permute-start | bytes 3145736 | tf_op jit(solution)/shard_map/ppermute | solution.py:24
  378.9 135.2 %collective-permute-start.48 = (bf16[144,512]{1,0:T(8,128)(2,1)S(1)}, bf16[144,512]{1,0:T(8,128)(2,1)S(1)}, u32[]{:S(2)}, u32[]{:S(2)}) collective-permute-start(bf16[144,512]{1,0:T(8,128)(2,1)S(1)} %get-tuple-element.164), channel_id=1, source_target_pairs={{0,4},{4,0},{8,12},{12,8},{16,20},{20,16},{24,28},{28,24},{1,5},{5... | collective-permute-start | bytes 442376 | tf_op jit(solution)/shard_map/ppermute | solution.py:593
  384.4 129.8 %collective-permute-start.49 = (bf16[144,512]{1,0:T(8,128)(2,1)S(1)}, bf16[144,512]{1,0:T(8,128)(2,1)S(1)}, u32[]{:S(2)}, u32[]{:S(2)}) collective-permute-start(bf16[144,512]{1,0:T(8,128)(2,1)S(1)} %get-tuple-element.163), channel_id=1, source_target_pairs={{0,8},{4,12},{8,0},{12,4},{16,24},{20,28},{24,16},{28,20},{1,9},{5... | collective-permute-start | bytes 442376 | tf_op jit(solution)/shard_map/ppermute | solution.py:593
  384.4 129.7 %collective-permute-start.50 = (bf16[112,512]{1,0:T(8,128)(2,1)S(1)}, bf16[112,512]{1,0:T(8,128)(2,1)S(1)}, u32[]{:S(2)}, u32[]{:S(2)}) collective-permute-start(bf16[112,512]{1,0:T(8,128)(2,1)S(1)} %slice.379), channel_id=1, source_target_pairs={{0,12},{4,8},{8,4},{12,0},{16,28},{20,24},{24,20},{28,16},{1,13},{... | collective-permute-start | bytes 344072 | tf_op jit(solution)/shard_map/ppermute | solution.py:593
  386.8 119.4 %collective-permute-start.52 = (bf16[48,512]{1,0:T(8,128)(2,1)S(1)}, bf16[48,512]{1,0:T(8,128)(2,1)S(1)}, u32[]{:S(2)}, u32[]{:S(2)}) collective-permute-start(bf16[48,512]{1,0:T(8,128)(2,1)S(1)} %get-tuple-element.162), channel_id=1, source_target_pairs={{0,20},{4,16},{8,28},{12,24},{16,4},{20,0},{24,12},{28,8},{1,21},{... | collective-permute-start | bytes 147464 | tf_op jit(solution)/shard_map/ppermute | solution.py:593
  388.2 119.2 %collective-permute-start.53 = (bf16[48,512]{1,0:T(8,128)(2,1)S(1)}, bf16[48,512]{1,0:T(8,128)(2,1)S(1)}, u32[]{:S(2)}, u32[]{:S(2)}) collective-permute-start(bf16[48,512]{1,0:T(8,128)(2,1)S(1)} %get-tuple-element.161), channel_id=1, source_target_pairs={{0,24},{4,28},{8,16},{12,20},{16,8},{20,12},{24,0},{28,4},{1,25},{... | collective-permute-start | bytes 147464 | tf_op jit(solution)/shard_map/ppermute | solution.py:593
  524.1 45.7 %collective-permute-start.62 = (bf16[144,512]{1,0:T(8,128)(2,1)}, bf16[144,512]{1,0:T(8,128)(2,1)}, u32[]{:S(2)}, u32[]{:S(2)}) collective-permute-start(bf16[144,512]{1,0:T(8,128)(2,1)} %get-tuple-element.154), channel_id=1, source_target_pairs={{0,4},{4,0},{8,12},{12,8},{16,20},{20,16},{24,28},{28,24},{1,5},{5... | collective-permute-start | bytes 442376 | tf_op jit(solution)/shard_map/ppermute | solution.py:593
  524.1 46.1 %collective-permute-start.63 = (bf16[144,512]{1,0:T(8,128)(2,1)}, bf16[144,512]{1,0:T(8,128)(2,1)}, u32[]{:S(2)}, u32[]{:S(2)}) collective-permute-start(bf16[144,512]{1,0:T(8,128)(2,1)} %get-tuple-element.153), channel_id=1, source_target_pairs={{0,8},{4,12},{8,0},{12,4},{16,24},{20,28},{24,16},{28,20},{1,9},{5... | collective-permute-start | bytes 442376 | tf_op jit(solution)/shard_map/ppermute | solution.py:593
  526.8 32.1 %collective-permute-start.66 = (bf16[48,512]{1,0:T(8,128)(2,1)}, bf16[48,512]{1,0:T(8,128)(2,1)S(1)}, u32[]{:S(2)}, u32[]{:S(2)}) collective-permute-start(bf16[48,512]{1,0:T(8,128)(2,1)} %get-tuple-element.152), channel_id=1, source_target_pairs={{0,20},{4,16},{8,28},{12,24},{16,4},{20,0},{24,12},{28,8},{1,21},{... | collective-permute-start | bytes 147464 | tf_op jit(solution)/shard_map/ppermute | solution.py:593
  527.4 34.0 %collective-permute-start.67 = (bf16[48,512]{1,0:T(8,128)(2,1)}, bf16[48,512]{1,0:T(8,128)(2,1)}, u32[]{:S(2)}, u32[]{:S(2)}) collective-permute-start(bf16[48,512]{1,0:T(8,128)(2,1)} %get-tuple-element.151), channel_id=1, source_target_pairs={{0,24},{4,28},{8,16},{12,20},{16,8},{20,12},{24,0},{28,4},{1,25},{... | collective-permute-start | bytes 147464 | tf_op jit(solution)/shard_map/ppermute | solution.py:593
  569.2 163.7 %collective-permute-start.74 = (bf16[2,2,2,2,1,16,896]{6,5,4,3,2,1,0:T(8,128)(2,1)}, bf16[2,2,2,2,1,16,896]{6,5,4,3,2,1,0:T(8,128)(2,1)}, u32[]{:S(2)}, u32[]{:S(2)}) collective-permute-start(bf16[2,2,2,2,1,16,896]{6,5,4,3,2,1,0:T(8,128)(2,1)} %fusion.11), channel_id=1, source_target_pairs={{0,1},{1,0},{2,3},{3,2},{4,5},{5,4},{6,7},{7,6},{8,9},{9,8},{10,11... | collective-permute-start | bytes 1376264 | tf_op jit(solution)/shard_map/ppermute | solution.py:24
  569.2 159.1 %collective-permute-start.84 = (bf16[2,2,2,2,1,16,768]{6,5,4,3,2,1,0:T(8,128)(2,1)}, bf16[2,2,2,2,1,16,768]{6,5,4,3,2,1,0:T(8,128)(2,1)}, u32[]{:S(2)}, u32[]{:S(2)}) collective-permute-start(bf16[2,2,2,2,1,16,768]{6,5,4,3,2,1,0:T(8,128)(2,1)} %dynamic-slice_convert_fusion.8), channel_id=1, source_target_pairs={{0,1},{1,0},{2,3},{3,2},{4,5},{5,4},{6,7},{7,6},{8,9},{9,8},{10,11... | collective-permute-start | bytes 1179656 | tf_op jit(solution)/shard_map/ppermute | solution.py:24
  569.7 266.3 %collective-permute-start.94 = (bf16[2,2,2,2,1,16,2560]{6,5,4,3,2,1,0:T(8,128)(2,1)}, bf16[2,2,2,2,1,16,2560]{6,5,4,3,2,1,0:T(8,128)(2,1)}, u32[]{:S(2)}, u32[]{:S(2)}) collective-permute-start(bf16[2,2,2,2,1,16,2560]{6,5,4,3,2,1,0:T(8,128)(2,1)} %dynamic-slice_convert_fusion), channel_id=1, source_target_pairs={{0,1},{1,0},{2,3},{3,2},{4,5},{5,4},{6,7},{7,6},{8,9},{9,8},{10,11... | collective-permute-start | bytes 3932168 | tf_op jit(solution)/shard_map/ppermute | solution.py:24
  569.8 147.0 %collective-permute-start.115 = (f32[8,2535]{1,0:T(8,128)S(1)}, f32[8,2535]{1,0:T(8,128)}, u32[]{:S(2)}, u32[]{:S(2)}) collective-permute-start(f32[8,2535]{1,0:T(8,128)S(1)} %dynamic-slice_add_fusion), channel_id=1, source_target_pairs={{0,1},{1,0},{2,3},{3,2},{4,5},{5,4},{6,7},{7,6},{8,9},{9,8},{10,11... | collective-permute-start | bytes 243368 | tf_op jit(solution)/shard_map/ppermute | solution.py:24
  727.8 101.5 %collective-permute-start.104 = (bf16[2,2,2,2,1,64,512]{6,5,4,3,2,1,0:T(8,128)(2,1)}, bf16[2,2,2,2,1,64,512]{6,5,4,3,2,1,0:T(8,128)(2,1)}, u32[]{:S(2)}, u32[]{:S(2)}) collective-permute-start(bf16[2,2,2,2,1,64,512]{6,5,4,3,2,1,0:T(8,128)(2,1)} %dynamic-slice_convert_fusion.2), channel_id=1, source_target_pairs={{0,1},{1,0},{2,3},{3,2},{4,5},{5,4},{6,7},{7,6},{8,9},{9,8},{10,11... | collective-permute-start | bytes 3145736 | tf_op jit(solution)/shard_map/ppermute | solution.py:24
  740.5 98.2 %collective-permute-start.89 = (bf16[2,2,2,2,1,16,2560]{6,5,4,3,2,1,0:T(8,128)(2,1)}, bf16[2,2,2,2,1,16,2560]{6,5,4,3,2,1,0:T(8,128)(2,1)}, u32[]{:S(2)}, u32[]{:S(2)}) collective-permute-start(bf16[2,2,2,2,1,16,2560]{6,5,4,3,2,1,0:T(8,128)(2,1)} %dynamic-slice_convert_fusion.1), channel_id=1, source_target_pairs={{0,1},{1,0},{2,3},{3,2},{4,5},{5,4},{6,7},{7,6},{8,9},{9,8},{10,11... | collective-permute-start | bytes 3932168 | tf_op jit(solution)/shard_map/ppermute | solution.py:24
  752.0 80.5 %collective-permute-start.99 = (bf16[2,2,2,2,1,64,512]{6,5,4,3,2,1,0:T(8,128)(2,1)}, bf16[2,2,2,2,1,64,512]{6,5,4,3,2,1,0:T(8,128)(2,1)}, u32[]{:S(2)}, u32[]{:S(2)}) collective-permute-start(bf16[2,2,2,2,1,64,512]{6,5,4,3,2,1,0:T(8,128)(2,1)} %dynamic-slice_convert_fusion.3), channel_id=1, source_target_pairs={{0,1},{1,0},{2,3},{3,2},{4,5},{5,4},{6,7},{7,6},{8,9},{9,8},{10,11... | collective-permute-start | bytes 3145736 | tf_op jit(solution)/shard_map/ppermute | solution.py:24
  840.5 40.0 %collective-permute-start.90 = (bf16[1,2,2,2,1,16,2560]{6,5,4,3,2,1,0:T(8,128)(2,1)S(1)}, bf16[1,2,2,2,1,16,2560]{6,5,4,3,2,1,0:T(8,128)(2,1)S(1)}, u32[]{:S(2)}, u32[]{:S(2)}) collective-permute-start(bf16[1,2,2,2,1,16,2560]{6,5,4,3,2,1,0:T(8,128)(2,1)S(1)} %dynamic-slice_convert_fusion.5), channel_id=1, source_target_pairs={{0,16},{16,0},{1,17},{17,1},{2,18},{18,2},{3,19},{19,3},{4,20},{20... | collective-permute-start | bytes 1966088 | tf_op jit(solution)/shard_map/ppermute | solution.py:24
  (138 other events, 1248.6 us)

commit v2 on v1

--- a/solution.py
+++ b/solution.py
@@ -521,11 +521,16 @@
     return lax.dot_general(left, right, dims, preferred_element_type=F32)
 
 
-def call(kernel, grid, in_specs, out_specs, out_shape, flops, scratch=()):
-    return pl.pallas_call(
-        kernel,
+def call(kernel, grid, in_specs, out_specs, out_shape, flops, scratch=(), after=()):
+    inputs, waits = len(in_specs), len(after)
+
+    def body(*refs):
+        kernel(*refs[:inputs], *refs[inputs + waits :])
+
+    run = pl.pallas_call(
+        body,
         grid=grid,
-        in_specs=in_specs,
+        in_specs=list(in_specs) + [pl.BlockSpec(memory_space=pl.ANY)] * waits,
         out_specs=out_specs,
         out_shape=out_shape,
         scratch_shapes=scratch,
@@ -534,10 +539,15 @@
         ),
         compiler_params=pltpu.CompilerParams(vmem_limit_bytes=VMEM_BYTES),
     )
+    return lambda *args: run(*args, *after)
 
 
 def whole_block(shape):
     return pl.BlockSpec(shape, lambda *ids: (0,) * len(shape))
+
+
+def flag_spec():
+    return pl.BlockSpec(memory_space=pltpu.SMEM)
 
 
 def win_block(width, column=0):
@@ -579,19 +589,52 @@
     return send, place, own, rows, starts, [kind for kind, _, _ in parts]
 
 
-def halo_permute(packed, rows, starts, kinds, onward):
+class Flow:
+    def __init__(self):
+        self.live = []
+        self.done = {}
+
+    def start(self, name, task):
+        self.live.append((name, task, next(task)))
+
+    def pending(self):
+        return [value for _, _, sends in self.live for value, _, _ in sends]
+
+    def step(self, *names):
+        live = []
+        for name, task, sends in self.live:
+            if names and name not in names:
+                live.append((name, task, sends))
+                continue
+            came = [lax.ppermute(value, axis, pairs) for value, axis, pairs in sends]
+            try:
+                live.append((name, task, task.send(came)))
+            except StopIteration as end:
+                self.done[name] = end.value
+        self.live = live
+
+    def finish(self, name):
+        while name not in self.done:
+            self.step(name)
+        return self.done[name]
+
+
+def swap_pairs(axis, bit):
+    return [(source, source ^ 2**bit) for source in range(lax.axis_size(axis))]
+
+
+def halo_flow(packed, rows, starts, kinds, onward):
     ring, quads = lax.axis_size("tm"), lax.axis_size("space")
-    came = []
+    sends = []
     for kind, start, count in zip(kinds, starts, rows):
-        piece = packed[start : start + count]
         step = 0 if not kind & 4 else (-1 if onward else 1)
         pairs = []
         for frame_at in range(ring):
             for quad in range(quads):
                 to = (frame_at + step) % ring * quads + (quad ^ (kind & 3))
                 pairs.append((frame_at * quads + quad, to))
-        came.append(lax.ppermute(piece, ("tm", "space"), pairs))
-    return came
+        sends.append((packed[start : start + count], ("tm", "space"), pairs))
+    return (yield sends)
 
 
 def pack_kernel(center, send_ref, x_ref, out_ref):
@@ -606,10 +649,10 @@
     out_ref[...] = total.astype(BF16)
 
 
-def halo_pack(x, send, center):
+def halo_pack(x, send, center, after=()):
     windows, _, width = x.shape
     rows = send.shape[0]
-    return call(
+    return functools.partial(call, after=after)(
         functools.partial(pack_kernel, center),
         (),
         [pl.BlockSpec(memory_space=pltpu.VMEM)] * 2,
@@ -641,10 +684,10 @@
         out_ref[w] = piece.astype(out_ref.dtype)
 
 
-def halo_unpack(x, came, own, place, starts, dtype, center=False, mean_of=None):
+def halo_unpack(x, came, own, place, starts, dtype, center=False, mean_of=None, after=()):
     windows, _, width = x.shape
     base = jnp.zeros((windows, 8, 128), F32) if mean_of is None else mean_of
-    return call(
+    return functools.partial(call, after=after)(
         functools.partial(unpack_kernel, center, mean_of is not None, starts),
         (),
         [pl.BlockSpec(memory_space=pltpu.VMEM)] * (4 + len(came)),
@@ -671,16 +714,16 @@
     inner = [("clip", 0)] if lax.axis_size("clip") > 1 else []
     tm = [b for b in bits if b[0] == "tm"]
     clip = [b for b in bits if b[0] == "clip" and b not in inner]
-    space = [b for b in bits if b[0] == "space"]
+    space = [b for b in reversed(bits) if b[0] == "space"]
     return inner + tm + clip + space, inner + clip + tm + space
 
 
-def gather_all(shard, order):
+def gather_flow(shard, order):
     bits = index_bits()
     out = shard.reshape((1,) * len(bits) + shard.shape)
     for axis, bit in reversed(order):
         dim = bits.index((axis, bit))
-        other = partner(out, axis, bit)
+        (other,) = yield [(out, axis, swap_pairs(axis, bit))]
         out = jnp.where(
             bit_of(axis, bit) == 1,
             jnp.concatenate([other, out], dim),
@@ -689,71 +732,143 @@
     return out.reshape((-1,) + shard.shape[1:])
 
 
-def scatter_all(grad, order):
+def scatter_flow(own, sent, order):
     bits = index_bits()
-    width = grad.shape[-1]
-    out = grad.reshape((2,) * len(bits) + (-1, width))
-    for axis, bit in order:
+    width = own.shape[-1]
+    dims = [2] * len(bits)
+    for n, (axis, bit) in enumerate(order):
         dim = bits.index((axis, bit))
-        here = bit_of(axis, bit)
-        mine = lax.dynamic_slice_in_dim(out, here, 1, dim)
-        sent = lax.dynamic_slice_in_dim(out, 1 - here, 1, dim).astype(BF16)
-        out = mine + partner(sent, axis, bit).astype(F32)
+        if n == 0:
+            dims[dim] = 1
+            own, sent = (v.reshape(dims + [-1, width]) for v in (own, sent))
+        else:
+            here = bit_of(axis, bit)
+            own = lax.dynamic_slice_in_dim(out, here, 1, dim)
+            sent = lax.dynamic_slice_in_dim(out, 1 - here, 1, dim).astype(BF16)
+        (came,) = yield [(sent, axis, swap_pairs(axis, bit))]
+        out = own + came.astype(F32)
     return out.reshape(-1, width)
 
 
-def table_shift_matrix():
-    shift = np.zeros((CELLS, 256, 128), np.float32)
+def table_flow(tables, heads_here):
+    first = lax.axis_index("tm") == 0
+    mine = jnp.where(first, tables[0], tables[1])
+    (came,) = yield [(jnp.where(first, tables[1], tables[0]), "tm", swap_pairs("tm", 0))]
+    table = mine + came
+    for axis, bit in index_bits():
+        if axis != "tm":
+            (came,) = yield [(table, axis, swap_pairs(axis, bit))]
+            table = table + came
+    return table
+
+
+WIDE = 768
+
+
+def column_pick():
+    pick = np.zeros((WIN_HW, 256, 128), np.float32)
+    for key_col in range(WIN_HW):
+        for row in range(SPAN):
+            for col in range(WIN_HW):
+                entry = row * SPAN + col - key_col + WIN_HW - 1
+                pick[key_col, entry, row * WIN_HW + col] = 1
+    return pick
+
+
+def lane_spans(step):
+    first, rest = divmod(step * CELLS, 128)
+    if rest + CELLS <= 128:
+        return [(first, rest, rest + CELLS)]
+    return [(first, rest, 128), (first + 1, 0, rest + CELLS - 128)]
+
+
+def bias_kernel(slab_ref, pick_ref, out_ref, row_ref, wide_ref):
+    heads = pl.num_programs(0)
+
+    @pl.when(pl.program_id(0) == 0)
+    def _():
+        slabs = slab_ref[...]
+        for col in range(WIN_HW):
+            row_ref[pl.ds(col, slabs.shape[0], stride=8), :] = mm(slabs, pick_ref[col]) * LOG2E
+
+    base = pl.program_id(0) * 128
+    lane = lax.broadcasted_iota(jnp.int32, (8, 128), 1)
     for row in range(WIN_HW):
+        tiles = [jnp.zeros((8, 128), F32) for _ in range(WIDE // 128)]
+        for step in range(STEPS):
+            rows = row_ref[pl.ds(pl.multiple_of(base + step * 8, 8), 8), :]
+            turn = (step * CELLS - WIN_HW * (WIN_HW - 1 - row)) % 128
+            rows = pltpu.roll(rows, turn, 1) if turn else rows
+            for tile, low, high in lane_spans(step):
+                tiles[tile] = jnp.where((lane >= low) & (lane < high), rows, tiles[tile])
+        wide_ref[row * WIN_HW : (row + 1) * WIN_HW, :] = jnp.concatenate(tiles, axis=1)[:WIN_HW]
+    wide = wide_ref[:CELLS, :]
+    for key_frame in range(WIN_T):
+        turned = pltpu.roll(wide, (WIDE - (WIN_T - 1 - key_frame) * CELLS) % WIDE, 1)
+        out_ref[0, key_frame * CELLS : (key_frame + 1) * CELLS, :] = turned[:, :TOKENS]
+
+
+def table_to_bias(tables, after=()):
+    heads = tables.shape[0]
+    slabs = tables.reshape(heads, STEPS, SPAN * SPAN)
+    slabs = jnp.pad(slabs, ((0, 0), (0, 16 - STEPS), (0, 256 - SPAN * SPAN)))
+    slabs = slabs.reshape(heads * 16, 256)
+    return functools.partial(call, after=after)(
+        bias_kernel,
+        (heads,),
+        [whole_block(slabs.shape), whole_block((WIN_HW, 256, 128))],
+        pl.BlockSpec((1, TOKENS, TOKENS), lambda h: (h, 0, 0)),
+        jax.ShapeDtypeStruct((heads, TOKENS, TOKENS), F32),
+        heads * 500_000_000,
+        [pltpu.VMEM((heads * 128, 128), F32), pltpu.VMEM((56, WIDE), F32)],
+    )(slabs, jnp.asarray(column_pick(), BF16))
+
+
+def table_back_kernel(sums_ref, pick_ref, out_ref, row_ref):
+    head = pl.program_id(0)
+    lane = lax.broadcasted_iota(jnp.int32, (WIN_HW, 128), 1)
+    totals = [None] * STEPS
+    for row in range(WIN_HW):
+        rows = sums_ref[0, row * WIN_HW : (row + 1) * WIN_HW, :]
+        start = WIN_HW * (WIN_HW - 1 - row)
+        for step in range(STEPS):
+            turn = (start - step * CELLS) % 128
+            piece = None
+            for tile, low, high in lane_spans(step):
+                part = rows[:, tile * 128 : (tile + 1) * 128]
+                part = jnp.where((lane >= low) & (lane < high), part, 0.0)
+                piece = part if piece is None else piece + part
+            piece = pltpu.roll(piece, turn, 1) if turn else piece
+            totals[step] = piece if totals[step] is None else totals[step] + piece
+    blank = jnp.zeros((1, 128), F32)
+    for step in range(16):
+        rows = jnp.concatenate([totals[step], blank]) if step < STEPS else jnp.zeros((8, 128), F32)
+        row_ref[pl.ds(pl.multiple_of(head * 128 + step * 8, 8), 8), :] = rows
+
+    @pl.when(head == pl.num_programs(0) - 1)
+    def _():
+        total = None
         for col in range(WIN_HW):
-            offset = (WIN_HW - 1 - row) * SPAN + WIN_HW - 1 - col
-            for m in range((WIN_HW - 1) * SPAN + WIN_HW):
-                shift[row * WIN_HW + col, m + offset, m] = 1
-    return shift
-
-
-def cell_spread():
-    spread = np.zeros((WIN_T * 128, TOKENS), np.float32)
-    for frame in range(WIN_T):
-        for row in range(WIN_HW):
-            for col in range(WIN_HW):
-                spread[frame * 128 + row * SPAN + col, frame * CELLS + row * WIN_HW + col] = 1
-    return spread
-
-
-def bias_kernel(slab_ref, spread_ref, out_ref):
-    spread = spread_ref[...]
-    for key_frame in range(WIN_T):
-        first = WIN_T - 1 - key_frame
-        slabs = jnp.concatenate([slab_ref[0, first + n] for n in range(WIN_T)], axis=1)
-        out_ref[0, key_frame * CELLS : (key_frame + 1) * CELLS, :] = mm(slabs, spread) * LOG2E
-
-
-def table_to_bias(tables):
-    layers, heads, _ = tables.shape
-    slabs = tables.reshape(layers * heads, STEPS, SPAN * SPAN)
-    slabs = jnp.pad(slabs, ((0, 0), (0, 0), (0, 256 - SPAN * SPAN)))
-    shift = jnp.asarray(table_shift_matrix(), BF16)
-    shifted = jnp.einsum("hje,kem->hjkm", slabs, shift, preferred_element_type=F32).astype(BF16)
-    return call(
-        bias_kernel,
-        (layers * heads,),
-        [
-            pl.BlockSpec((1, STEPS, CELLS, 128), lambda h: (h, 0, 0, 0)),
-            whole_block((WIN_T * 128, TOKENS)),
-        ],
-        pl.BlockSpec((1, TOKENS, TOKENS), lambda h: (h, 0, 0)),
-        jax.ShapeDtypeStruct((layers * heads, TOKENS, TOKENS), F32),
-        2 * layers * heads * TOKENS * WIN_T * 128 * TOKENS,
-    )(shifted, jnp.asarray(cell_spread(), BF16))
-
-
-def bias_grad_to_table(parts):
-    shift = jnp.asarray(table_shift_matrix(), F32)
-    table = jnp.einsum(
-        "hjkm,kem->hje", parts, shift, precision=lax.Precision.HIGH, preferred_element_type=F32
-    )
-    return table[:, :, : SPAN * SPAN].reshape(parts.shape[0], -1)
+            rows = row_ref[pl.ds(col, out_ref.shape[0], stride=8), :]
+            high = rows.astype(BF16)
+            low = (rows - high.astype(F32)).astype(BF16)
+            part = mm(high, pick_ref[col], 1, 1) + mm(low, pick_ref[col], 1, 1)
+            total = part if total is None else total + part
+        out_ref[...] = total
+
+
+def sums_to_table(sums, after=()):
+    heads = sums.shape[0]
+    slabs = functools.partial(call, after=after)(
+        table_back_kernel,
+        (heads,),
+        [pl.BlockSpec((1, CELLS, WIDE), lambda h: (h, 0, 0)), whole_block((WIN_HW, 256, 128))],
+        whole_block((heads * 16, 256)),
+        jax.ShapeDtypeStruct((heads * 16, 256), F32),
+        heads * 300_000_000,
+        [pltpu.VMEM((heads * 128, 128), F32)],
+    )(sums, jnp.asarray(column_pick(), BF16))
+    return slabs.reshape(heads, 16, 256)[:, :STEPS, : SPAN * SPAN].reshape(heads, -1)
 
 
 def unit_rows(x):
@@ -771,30 +886,31 @@
     )
 
 
-def qkv_kernel(x_ref, vec_ref, w_ref, out_ref):
+def qkv_kernel(x_ref, vec_ref, wq_ref, wk_ref, wv_ref, out_ref):
     width = x_ref.shape[-1]
     unit, _ = unit_rows(x_ref[0].astype(F32))
     normed = (unit * vec_ref[0:1] + vec_ref[1:2]).astype(BF16)
-    for part in range(3):
-        cols = slice(part * width, (part + 1) * width)
-        out = mm(normed, w_ref[:, cols])
+    for part, ref in enumerate((wq_ref, wk_ref, wv_ref)):
+        out = mm(normed, ref[...])
         if part == 0:
             out = out + vec_ref[2:3]
         if part == 2:
             out = out + vec_ref[3:4]
-        out_ref[0, :, cols] = out.astype(BF16)
-
-
-def run_qkv(x, vec, w_qkv):
+        out_ref[0, :, part * width : (part + 1) * width] = out.astype(BF16)
+
+
+def run_qkv(x, vec, w_qkv, after=()):
     windows, _, width = x.shape
-    return call(
+    weight, at = w_qkv
+    return functools.partial(call, after=after)(
         qkv_kernel,
         (windows,),
-        [win_block(width), whole_block(vec.shape), whole_block(w_qkv.shape)],
+        [win_block(width), whole_block(vec.shape)]
+        + [weight_block(width, width, at + n) for n in range(3)],
         win_block(3 * width),
         jax.ShapeDtypeStruct((windows, TOKENS, 3 * width), BF16),
         2 * windows * TOKENS * width * 3 * width,
-    )(x, vec, w_qkv)
+    )(x, vec, weight, weight, weight)
 
 
 GROUP = 4
@@ -808,8 +924,29 @@
     ]
 
 
-def attend_kernel(shifted, head_size, q_ref, k_ref, v_ref, bias_ref, col_ref, row_ref, out_ref, log_ref):
+def region_labels(flag_ref, late_ref, turned_ref, at_end):
+    flags = [flag_ref[1 + n].astype(F32) for n in range(3)]
+    flags[0] = flags[0] * at_end
+    col = sum(flags[n] * late_ref[:, n : n + 1] for n in range(3))
+    return col, sum(flags[n] * turned_ref[n : n + 1, :] for n in range(3))
+
+
+def late_tokens():
+    token = np.arange(TOKENS)
+    late = np.zeros((TOKENS, 8), np.float32)
+    late[:, 0] = 4 * (token // CELLS >= WIN_T - WIN_T // 2)
+    late[:, 1] = 2 * (token // WIN_HW % WIN_HW >= WIN_HW - WIN_HW // 2)
+    late[:, 2] = token % WIN_HW >= WIN_HW - WIN_HW // 2
+    return late
+
+
+def attend_kernel(
+    shifted, head_size, flag_ref, q_ref, k_ref, v_ref, bias_ref, late_ref, turned_ref, out_ref, log_ref
+):
     q, k = q_ref[0], k_ref[0]
+    if shifted:
+        at_end = jnp.where(pl.program_id(1) == pl.num_programs(1) - 1, 1.0, 0.0)
+        col, row = region_labels(flag_ref, late_ref, turned_ref, at_end)
     turned = v_ref[0].astype(F32).T.astype(BF16)
     factor = head_size**-0.5 * LOG2E
     masks = head_masks(head_size)
@@ -817,7 +954,7 @@
     for h in range(GROUP):
         scores = mm(k * masks[h], q, 1, 1) * factor + bias_ref[h]
         if shifted:
-            scores = jnp.where(col_ref[0] == row_ref[0], scores, masked_score)
+            scores = jnp.where(col == row, scores, masked_score)
         peak = jnp.max(scores, axis=0, keepdims=True)
         raised = jnp.exp2(scores - peak)
         total = jnp.sum(raised, axis=0, keepdims=True)
@@ -828,110 +965,154 @@
     log_ref[0, 0] = jnp.concatenate(logs + logs, axis=0)
 
 
-def attend_specs(width):
+def run_attend(qkv, bias, flags, shifted, first, after=()):
+    windows, _, width3 = qkv.shape
+    width = width3 // 3
     wide = GROUP * (width // HEADS)
-    groups = HEADS // GROUP
-    qkv = [
-        pl.BlockSpec((1, TOKENS, wide), lambda g, w, p=part: (w, 0, p * groups + g))
+    groups, count = HEADS // GROUP, bias.shape[0] // GROUP
+    qkv_specs = [
+        pl.BlockSpec((1, TOKENS, wide), lambda g, w, p=part: (w, 0, p * groups + first + g))
         for part in range(3)
     ]
-    bias = pl.BlockSpec((GROUP, TOKENS, TOKENS), lambda g, w: (g, 0, 0))
-    col = pl.BlockSpec((1, TOKENS, 1), lambda g, w: (w, 0, 0))
-    row = pl.BlockSpec((1, 1, TOKENS), lambda g, w: (w, 0, 0))
-    flat = pl.BlockSpec((1, TOKENS, wide), lambda g, w: (w, 0, g))
-    log = pl.BlockSpec((1, 1, 2 * GROUP, TOKENS), lambda g, w: (w, g, 0, 0))
-    return qkv, bias, col, row, flat, log
-
-
-def run_attend(qkv, bias, labels, shifted):
-    windows, _, width3 = qkv.shape
-    width = width3 // 3
-    groups = HEADS // GROUP
-    qkv_specs, bias_spec, col, row, flat, log = attend_specs(width)
-    return call(
+    return functools.partial(call, after=after)(
         functools.partial(attend_kernel, shifted, width // HEADS),
-        (groups, windows),
-        qkv_specs + [bias_spec, col, row],
-        [flat, log],
+        (count, windows),
+        [flag_spec()]
+        + qkv_specs
+        + [
+            pl.BlockSpec((GROUP, TOKENS, TOKENS), lambda g, w: (g, 0, 0)),
+            whole_block((TOKENS, 8)),
+            whole_block((8, TOKENS)),
+        ],
         [
-            jax.ShapeDtypeStruct((windows, TOKENS, width), BF16),
-            jax.ShapeDtypeStruct((windows, groups, 2 * GROUP, TOKENS), F32),
+            pl.BlockSpec((1, TOKENS, wide), lambda g, w: (w, 0, g)),
+            pl.BlockSpec((1, 1, 2 * GROUP, TOKENS), lambda g, w: (w, g, 0, 0)),
         ],
-        32 * windows * TOKENS * TOKENS * width,
-    )(qkv, qkv, qkv, bias, labels[0], labels[1])
+        [
+            jax.ShapeDtypeStruct((windows, TOKENS, count * wide), BF16),
+            jax.ShapeDtypeStruct((windows, count, 2 * GROUP, TOKENS), F32),
+        ],
+        64 * windows * TOKENS * TOKENS * count * wide,
+    )(flags, qkv, qkv, qkv, bias, late_tokens(), late_tokens().T)
 
 
 def attend_back_kernel(
-    shifted, head_size, q_ref, k_ref, v_ref, g_ref, bias_ref, col_ref, row_ref, log_ref, spread_ref,
-    dq_ref, dk_ref, dv_ref, table_ref, sum_ref, slab_ref,
+    shifted, head_size, flag_ref, q_ref, k_ref, v_ref, g_ref, o_ref, bias_ref, late_ref, turned_ref,
+    log_ref, dq_ref, dk_ref, dv_ref, table_ref, sum_ref,
 ):
-    w = pl.program_id(1)
-    q, k, v, g = q_ref[0], k_ref[0], v_ref[0], g_ref[0]
-    turned = k.astype(F32).T.astype(BF16)
+    windows = q_ref.shape[0]
+    if shifted:
+        labels = [
+            region_labels(flag_ref, late_ref, turned_ref, float(w == windows - 1))
+            for w in range(windows)
+        ]
     scale = head_size**-0.5
     factor = scale * LOG2E
     masks = head_masks(head_size)
-    grad_q, grad_k, grad_v = [], None, None
+
+    @pl.when(pl.program_id(0) == 0)
+    def _():
+        sum_ref[...] = jnp.zeros_like(sum_ref)
+
+    turned, weighed = [], []
+    for w in range(windows):
+        turned.append(k_ref[w].astype(F32).T.astype(BF16))
+        weighed.append(g_ref[w].astype(F32).T * o_ref[w].astype(F32).T)
+    grad_q = [[] for _ in range(windows)]
+    grad_k, grad_v = [None] * windows, [None] * windows
     for h in range(GROUP):
-        scores = mm(k * masks[h], q, 1, 1) * factor + bias_ref[h]
-        if shifted:
-            scores = jnp.where(col_ref[0] == row_ref[0], scores, masked_score)
-        probs = jnp.exp2(scores - log_ref[0, 0, h : h + 1])
-        grad_probs = mm(v * masks[h], g, 1, 1)
-        inner = jnp.sum(probs * grad_probs, axis=0, keepdims=True)
-        grad_scores = (probs * (grad_probs - inner)).astype(BF16)
-        part_v = mm(probs.astype(BF16), g * masks[h])
-        part_k = mm(grad_scores, q * masks[h])
-        grad_v = part_v if grad_v is None else grad_v + part_v
-        grad_k = part_k if grad_k is None else grad_k + part_k
-        grad_q.append(mm(turned[h * head_size : (h + 1) * head_size], grad_scores))
-
-        @pl.when(w == 0)
-        def _():
-            sum_ref[h] = grad_scores.astype(F32)
-
-        @pl.when(w != 0)
-        def _():
-            sum_ref[h] += grad_scores.astype(F32)
-
-    dq_ref[0] = (jnp.concatenate(grad_q, axis=0) * scale).T.astype(BF16)
-    dk_ref[0] = (grad_k * scale).astype(BF16)
-    dv_ref[0] = grad_v.astype(BF16)
-
-    @pl.when(w == pl.num_programs(1) - 1)
-    def _():
-        spread = spread_ref[...]
-        for h in range(GROUP):
-            slab_ref[...] = jnp.zeros_like(slab_ref)
-            for key_frame in range(WIN_T):
-                rows = sum_ref[h, key_frame * CELLS : (key_frame + 1) * CELLS, :]
-                first = (WIN_T - 1 - key_frame) * 128
-                slab_ref[:, first : first + WIN_T * 128] += mm(rows.astype(BF16), spread, 1, 1)
-            for step in range(STEPS):
-                table_ref[h, step] = slab_ref[:, step * 128 : (step + 1) * 128]
-
-
-def run_attend_back(qkv, grad, bias, labels, log, shifted):
+        here = slice(h * head_size, (h + 1) * head_size)
+        total = None
+        for w in range(windows):
+            q, k, v, g = q_ref[w], k_ref[w], v_ref[w], g_ref[w]
+            inner = jnp.sum(weighed[w][here], axis=0, keepdims=True)
+            scores = mm(k * masks[h], q, 1, 1) * factor + bias_ref[h]
+            if shifted:
+                scores = jnp.where(labels[w][0] == labels[w][1], scores, masked_score)
+            probs = jnp.exp2(scores - log_ref[w, 0, h : h + 1])
+            grad_probs = mm(v * masks[h], g, 1, 1)
+            grad_scores = (probs * (grad_probs - inner)).astype(BF16)
+            part_v = mm(probs.astype(BF16), g * masks[h])
+            part_k = mm(grad_scores, q * masks[h])
+            grad_v[w] = part_v if grad_v[w] is None else grad_v[w] + part_v
+            grad_k[w] = part_k if grad_k[w] is None else grad_k[w] + part_k
+            grad_q[w].append(mm(turned[w][here], grad_scores))
+            wide = grad_scores.astype(F32)
+            total = wide if total is None else total + wide
+        sum_ref[:, :TOKENS] = total
+        sums = None
+        for key_frame in range(WIN_T):
+            rows = sum_ref[key_frame * CELLS : (key_frame + 1) * CELLS, :]
+            step = (WIN_T - 1 - key_frame) * CELLS
+            rows = pltpu.roll(rows, step, 1) if step else rows
+            sums = rows if sums is None else sums + rows
+        table_ref[h] = sums
+    for w in range(windows):
+        dq_ref[w] = (jnp.concatenate(grad_q[w], axis=0) * scale).T.astype(BF16)
+        dk_ref[w] = (grad_k[w] * scale).astype(BF16)
+        dv_ref[w] = grad_v[w].astype(BF16)
+
+
+def run_attend_back(qkv, grad, attended, bias, flags, log, shifted, first, after=()):
     windows, _, width3 = qkv.shape
     width = width3 // 3
-    groups = HEADS // GROUP
-    qkv_specs, bias_spec, col, row, flat, log_spec = attend_specs(width)
-    flat_shape = jax.ShapeDtypeStruct((windows, TOKENS, width), BF16)
-    return call(
+    wide = GROUP * (width // HEADS)
+    groups, count = HEADS // GROUP, bias.shape[0] // GROUP
+    qkv_specs = [
+        pl.BlockSpec((windows, TOKENS, wide), lambda g, p=part: (0, 0, p * groups + first + g))
+        for part in range(3)
+    ]
+    flat = pl.BlockSpec((windows, TOKENS, wide), lambda g: (0, 0, g))
+    flat_shape = jax.ShapeDtypeStruct((windows, TOKENS, count * wide), BF16)
+    return functools.partial(call, after=after)(
         functools.partial(attend_back_kernel, shifted, width // HEADS),
-        (groups, windows),
-        qkv_specs + [flat, bias_spec, col, row, log_spec]
-        + [pl.BlockSpec((WIN_T * 128, TOKENS), lambda g, w: (0, 0))],
-        [flat, flat, flat, pl.BlockSpec((GROUP, STEPS, CELLS, 128), lambda g, w: (g, 0, 0, 0))],
-        [flat_shape] * 3 + [jax.ShapeDtypeStruct((HEADS, STEPS, CELLS, 128), F32)],
-        80 * windows * TOKENS * TOKENS * width,
-        [pltpu.VMEM((GROUP, TOKENS, TOKENS), F32), pltpu.VMEM((CELLS, STEPS * 128), F32)],
-    )(qkv, qkv, qkv, grad, bias, labels[0], labels[1], log, jnp.asarray(cell_spread(), BF16))
-
-
-def branch_kernel(x_ref, att_ref, vec_ref, wo_ref, w1_ref, w2_ref, mid_ref, hid_ref, slope_ref, out_ref):
+        (count,),
+        [flag_spec()]
+        + qkv_specs
+        + [
+            pl.BlockSpec((windows, TOKENS, wide), lambda g: (0, 0, first + g)),
+            flat,
+            pl.BlockSpec((GROUP, TOKENS, TOKENS), lambda g: (g, 0, 0)),
+            whole_block((TOKENS, 8)),
+            whole_block((8, TOKENS)),
+            pl.BlockSpec((windows, 1, 2 * GROUP, TOKENS), lambda g: (0, g, 0, 0)),
+        ],
+        [flat, flat, flat, pl.BlockSpec((GROUP, CELLS, WIDE), lambda g: (g, 0, 0))],
+        [flat_shape] * 3 + [jax.ShapeDtypeStruct((count * GROUP, CELLS, WIDE), F32)],
+        160 * windows * TOKENS * TOKENS * count * wide,
+        [pltpu.VMEM((TOKENS, WIDE), F32)],
+    )(flags, qkv, qkv, qkv, grad, attended, bias, late_tokens(), late_tokens().T, log)
+
+
+def normal_below(x):
+    bell = jnp.exp2(x * x * (-0.5 * LOG2E)) * (1.0 / math.sqrt(2 * math.pi))
+    return 0.5 + 0.5 * lax.erf(x * math.sqrt(0.5)), bell
+
+
+def spread_down(down_ref, w2_ref):
+    _, parts, own, width = w2_ref.shape
+    for part in range(parts):
+        cols = slice(part * width, (part + 1) * width)
+        w2_ref[:, part] = down_ref[:, cols].reshape(-1, own, width)
+
+
+def chunk_rows(w2_ref, first, chunk):
+    _, parts, own, width = w2_ref.shape
+    step = chunk // (parts * own)
+    return w2_ref[first * step : (first + 1) * step].reshape(chunk, width)
+
+
+def branch_kernel(count, *refs):
+    att_refs = refs[:count]
+    x_ref, vec_ref, wo_ref, w1_ref, down_ref, mid_ref, hid_ref, slope_ref, out_ref, w2_ref = refs[count:]
+
+    @pl.when(pl.program_id(0) == 0)
+    def _():
+        spread_down(down_ref, w2_ref)
+
     chunk = 512
-    middle = x_ref[0].astype(F32) + mm(att_ref[0], wo_ref[...]) + vec_ref[4:5]
+    attended = jnp.concatenate([ref[0] for ref in att_refs], axis=1)
+    middle = x_ref[0].astype(F32) + mm(attended, wo_ref[...]) + vec_ref[4:5]
     mid_ref[0] = middle
     unit, _ = unit_rows(middle)
     normed = (unit * vec_ref[5:6] + vec_ref[6:7]).astype(BF16)
@@ -939,29 +1120,38 @@
     for n in range(w1_ref.shape[1] // chunk):
         cols = slice(n * chunk, (n + 1) * chunk)
         pre = mm(normed, w1_ref[:, cols]) + vec_ref[8 + n : 9 + n]
-        below = 0.5 * (1.0 + lax.erf(pre * math.sqrt(0.5)))
-        bell = jnp.exp(-0.5 * pre * pre) * (1.0 / math.sqrt(2 * math.pi))
+        below, bell = normal_below(pre)
         hidden = (pre * below).astype(BF16)
         hid_ref[0, :, cols] = hidden
         slope_ref[0, :, cols] = (below + pre * bell).astype(BF16)
-        after = after + mm(hidden, w2_ref[cols, :])
+        after = after + mm(hidden, chunk_rows(w2_ref, n, chunk))
     out_ref[0] = after.astype(out_ref.dtype)
 
 
-def run_branch(x, attended, vec, w_mid, w2, out_dtype):
+def weight_block(rows, width, column):
+    return pl.BlockSpec((rows, width), lambda *ids: (0, column))
+
+
+def branch_weights(weights, width, wide):
+    (wo, wo_at), (w1, w1_at), (down, down_at) = weights
+    specs = [
+        weight_block(width, width, wo_at),
+        weight_block(width, wide, w1_at),
+        weight_block(width, wide, down_at),
+    ]
+    return (wo, w1, down), specs
+
+
+def run_branch(x, attended, vec, weights, out_dtype, after=()):
     windows, _, width = x.shape
-    wide = w2.shape[0]
-    return call(
-        branch_kernel,
+    wide = 4 * width
+    arrays, specs = branch_weights(weights, width, wide)
+    return functools.partial(call, after=after)(
+        functools.partial(branch_kernel, len(attended)),
         (windows,),
-        [
-            win_block(width),
-            win_block(width),
-            whole_block(vec.shape),
-            pl.BlockSpec((width, width), lambda w: (0, wide // width)),
-            pl.BlockSpec((width, wide), lambda w: (0, 0)),
-            whole_block(w2.shape),
-        ],
+        [win_block(part.shape[-1]) for part in attended]
+        + [win_block(width), whole_block(vec.shape)]
+        + specs,
         [win_block(width), win_block(wide), win_block(wide), win_block(width)],
         [
             jax.ShapeDtypeStruct((windows, TOKENS, width), F32),
@@ -970,22 +1160,30 @@
             jax.ShapeDtypeStruct((windows, TOKENS, width), out_dtype),
         ],
         2 * windows * TOKENS * width * (width + 2 * wide),
-    )(x, attended, vec, w_mid, w_mid, w2)
+        [pltpu.VMEM((width // 16, wide // width, 16, width), BF16)],
+    )(*attended, x, vec, *arrays)
 
 
 def add_rows(ref, rows, value):
     ref[rows, :] += jnp.sum(value.astype(F32), axis=0, keepdims=True)
 
 
-def branch_back_kernel(
-    grad_ref, mid_ref, att_ref, hid_ref, slope_ref, vec_ref, wo_ref, w1_ref, w2_ref,
-    gm_ref, ga_ref, d1_ref, d2_ref, vecs_ref,
-):
+def split_out(sums_ref, core, own_ref, sent_ref):
+    own_ref[...] = sums_ref[:, core]
+    sent_ref[...] = sums_ref[:, 1 - core].astype(BF16)
+
+
+def branch_back_kernel(count, split, flag_ref, *refs):
+    att_refs = refs[:count]
+    grad_ref, mid_ref, hid_ref, slope_ref, vec_ref, wo_ref, w1_ref, down_ref = refs[count : count + 8]
+    gm_ref, ga_ref, vecs_ref = refs[count + 8 : count + 11]
+    outs, (d1_ref, d2_ref, w2_ref) = refs[count + 11 : -3], refs[-3:]
     chunk = 512
-    wide = w2_ref.shape[0]
+    width, wide = w1_ref.shape
 
     @pl.when(pl.program_id(0) == 0)
     def _():
+        spread_down(down_ref, w2_ref)
         d1_ref[...] = jnp.zeros_like(d1_ref)
         d2_ref[...] = jnp.zeros_like(d2_ref)
         vecs_ref[...] = jnp.zeros_like(vecs_ref)
@@ -996,13 +1194,16 @@
     normed = (unit * vec_ref[5:6] + vec_ref[6:7]).astype(BF16)
     add_rows(vecs_ref, slice(7, 8), branch)
     back = None
+    blocks = chunk // d2_ref.shape[2]
     for n in range(wide // chunk):
         cols = slice(n * chunk, (n + 1) * chunk)
-        d2_ref[cols, :] += mm(hid_ref[0, :, cols], branch, 0, 0)
-        grad_pre = mm(branch, w2_ref[cols, :], 1, 1) * slope_ref[0, :, cols].astype(F32)
-        add_rows(vecs_ref, slice(8 + n, 9 + n), grad_pre.astype(BF16))
+        total = mm(hid_ref[0, :, cols], branch, 0, 0)
+        at = slice(n * blocks // 2, (n + 1) * blocks // 2)
+        d2_ref[at] += total.reshape((-1,) + d2_ref.shape[1:])
+        grad_pre = mm(branch, chunk_rows(w2_ref, n, chunk), 1, 1) * slope_ref[0, :, cols].astype(F32)
         grad_pre = grad_pre.astype(BF16)
-        d1_ref[:, cols] += mm(normed, grad_pre, 0, 0)
+        add_rows(vecs_ref, slice(8 + n, 9 + n), grad_pre)
+        d1_ref[:, :, :, cols] += mm(normed, grad_pre, 0, 0).reshape(d1_ref.shape[:3] + (chunk,))
         part = mm(grad_pre, w1_ref[:, cols], 1, 1)
         back = part if back is None else back + part
     add_rows(vecs_ref, slice(5, 6), back * unit)
@@ -1011,56 +1212,82 @@
     gm_ref[0] = middle_grad
     branch = middle_grad.astype(BF16)
     add_rows(vecs_ref, slice(4, 5), branch)
-    d1_ref[:, wide:] += mm(att_ref[0], branch, 0, 0)
+    attended = jnp.concatenate([ref[0] for ref in att_refs], axis=1)
+    total = mm(attended, branch, 0, 0)
+    d1_ref[:, :, :, wide:] += total.reshape(d1_ref.shape[:3] + (width,))
     ga_ref[0] = mm(branch, wo_ref[...], 1, 1).astype(BF16)
 
-
-def run_branch_back(grad, middle, attended, hidden, slope, vec, w_mid, w2):
+    @pl.when(pl.program_id(0) == pl.num_programs(0) - 1)
+    def _():
+        if split:
+            split_out(d1_ref, flag_ref[0], *outs[:2])
+            split_out(d2_ref, flag_ref[0], *outs[2:])
+        else:
+            (out_ref,) = outs
+            out_ref[:, : wide + width] = d1_ref[...].reshape(width, -1).astype(BF16)
+            parts = wide // width
+            for part in range(parts):
+                first = wide + width + part * width
+                piece = d2_ref[:, :, part * 16 : (part + 1) * 16, :].reshape(width, width)
+                out_ref[:, first : first + width] = piece.astype(BF16)
+
+
+def run_branch_back(grad, middle, attended, hidden, slope, vec, weights, flags, split, after=()):
     windows, _, width = middle.shape
-    wide = w2.shape[0]
+    wide = 4 * width
+    arrays, specs = branch_weights(weights, width, wide)
     flat = win_block(width)
-    return call(
-        branch_back_kernel,
+    pairs = width // 32
+    if split:
+        shapes = []
+        for rows, cols in ((16, wide + width), (64, width)):
+            shapes.append(jax.ShapeDtypeStruct((pairs, rows, cols), F32))
+            shapes.append(jax.ShapeDtypeStruct((pairs, rows, cols), BF16))
+    else:
+        shapes = [jax.ShapeDtypeStruct((width, 2 * wide + width), BF16)]
+    return functools.partial(call, after=after)(
+        functools.partial(branch_back_kernel, len(attended), split),
         (windows,),
-        [
-            flat,
-            flat,
-            flat,
-            win_block(wide),
-            win_block(wide),
-            whole_block(vec.shape),
-            pl.BlockSpec((width, width), lambda w: (0, wide // width)),
-            pl.BlockSpec((width, wide), lambda w: (0, 0)),
-            whole_block(w2.shape),
-        ],
-        [flat, flat, whole_block(w_mid.shape), whole_block(w2.shape), whole_block(vec.shape)],
+        [flag_spec()]
+        + [win_block(part.shape[-1]) for part in attended]
+        + [flat, flat, win_block(wide), win_block(wide), whole_block(vec.shape)]
+        + specs,
+        [flat, flat, whole_block(vec.shape)] + [whole_block(s.shape) for s in shapes],
         [
             jax.ShapeDtypeStruct((windows, TOKENS, width), F32),
             jax.ShapeDtypeStruct((windows, TOKENS, width), BF16),
-            jax.ShapeDtypeStruct(w_mid.shape, F32),
-            jax.ShapeDtypeStruct(w2.shape, F32),
             jax.ShapeDtypeStruct(vec.shape, F32),
+        ]
+        + shapes,
+        4 * windows * TOKENS * width * (width + 2 * wide),
+        [
+            pltpu.VMEM((pairs, 2, 16, wide + width), F32),
+            pltpu.VMEM((pairs, 2, 64, width), F32),
+            pltpu.VMEM((pairs * 2, wide // width, 16, width), BF16),
         ],
-        4 * windows * TOKENS * width * (width + 2 * wide),
-    )(grad, middle, attended, hidden, slope, vec, w_mid, w_mid, w2)
-
-
-def qkv_back_kernel(dq_ref, dk_ref, dv_ref, x_ref, gm_ref, vec_ref, w_ref, out_ref, dw_ref, vecs_ref):
+    )(flags, *attended, grad, middle, hidden, slope, vec, *arrays)
+
+
+def qkv_back_kernel(count, flag_ref, *refs):
+    grads, refs = refs[: 3 * count], refs[3 * count :]
+    x_ref, gm_ref, vec_ref, wq_ref, wk_ref, wv_ref, rest_ref, mask_ref, pick_ref, spread_ref = refs[:10]
+    out_ref, own_ref, sent_ref, dw_ref, vecs_ref = refs[10:]
     width = x_ref.shape[-1]
 
     @pl.when(pl.program_id(0) == 0)
     def _():
         dw_ref[...] = jnp.zeros_like(dw_ref)
-        vecs_ref[...] = jnp.zeros_like(vecs_ref)
+        vecs_ref[...] = rest_ref[...]
 
     unit, inverse = unit_rows(x_ref[0].astype(F32))
     normed = (unit * vec_ref[0:1] + vec_ref[1:2]).astype(BF16)
     back = None
-    for part, ref in enumerate((dq_ref, dk_ref, dv_ref)):
+    for part, ref in enumerate((wq_ref, wk_ref, wv_ref)):
+        grad = jnp.concatenate([g[0] for g in grads[part * count : (part + 1) * count]], axis=1)
+        total = mm(normed, grad, 0, 0)
         cols = slice(part * width, (part + 1) * width)
-        grad = ref[0]
-        dw_ref[:, cols] += mm(normed, grad, 0, 0)
-        here = mm(grad, w_ref[:, cols], 1, 1)
+        dw_ref[:, :, :, cols] += total.reshape(dw_ref.shape[:3] + (width,))
+        here = mm(grad, ref[...], 1, 1)
         back = here if back is None else back + here
         if part == 0:
             add_rows(vecs_ref, slice(2, 3), grad)
@@ -1070,80 +1297,141 @@
     add_rows(vecs_ref, slice(1, 2), back)
     out_ref[0] = (gm_ref[0] + norm_back(back, unit, inverse, vec_ref[0:1])).astype(out_ref.dtype)
 
-
-def run_qkv_back(grads, x, grad_middle, vec, w_qkv, out_dtype):
+    @pl.when(pl.program_id(0) == pl.num_programs(0) - 1)
+    def _():
+        rows = vecs_ref[...]
+        high = rows.astype(BF16)
+        low = (rows - high.astype(F32)).astype(BF16)
+        total = None
+        for piece in (high, low):
+            piece = (mm(pick_ref[...], piece, 0, 0) * mask_ref[...].astype(F32)).astype(BF16)
+            piece = mm(piece, spread_ref[0], 1, 1)
+            total = piece if total is None else total + piece
+        dw_ref[:, :, :, 3 * width :] = total.reshape(dw_ref.shape[:3] + (128,))
+        split_out(dw_ref, flag_ref[0], own_ref, sent_ref)
+
+
+def run_qkv_back(grads, x, grad_middle, vec, w_qkv, rest, flags, out_dtype, after=()):
     windows, _, width = x.shape
     flat = win_block(width)
-    return call(
-        qkv_back_kernel,
+    weight, at = w_qkv
+    extra = [jnp.asarray(a, BF16) for a in vector_slots()]
+    shape = (width // 32, 16, 3 * width + 128)
+    return functools.partial(call, after=after)(
+        functools.partial(qkv_back_kernel, len(grads) // 3),
         (windows,),
-        [flat] * 5 + [whole_block(vec.shape), whole_block(w_qkv.shape)],
-        [flat, whole_block(w_qkv.shape), whole_block((8, width))],
+        [flag_spec()]
+        + [win_block(part.shape[-1]) for part in grads]
+        + [flat, flat, whole_block(vec.shape)]
+        + [weight_block(width, width, at + n) for n in range(3)]
+        + [whole_block(rest.shape)]
+        + [whole_block(a.shape) for a in extra],
+        [flat, whole_block(shape), whole_block(shape)],
         [
             jax.ShapeDtypeStruct((windows, TOKENS, width), out_dtype),
-            jax.ShapeDtypeStruct(w_qkv.shape, F32),
-            jax.ShapeDtypeStruct((8, width), F32),
+            jax.ShapeDtypeStruct(shape, F32),
+            jax.ShapeDtypeStruct(shape, BF16),
         ],
         4 * windows * TOKENS * width * 3 * width,
-    )(*grads, x, grad_middle, vec, w_qkv)
-
-
-def vectors_in(shards):
-    gain_one, bias_one, mix_bias, proj_bias, gain_two, bias_two, wide_bias, narrow_bias = shards
-    own = gain_one.shape[1]
-    rows = []
-    for v in (gain_one, bias_one, mix_bias, proj_bias, gain_two, bias_two, narrow_bias, wide_bias):
-        rows.append(v.reshape(LAYERS, -1, own))
-    block = jnp.concatenate(rows, axis=1)
-    block = block.transpose(1, 0, 2).reshape(block.shape[1], LAYERS * own)
-    return jnp.pad(block, ((0, 16 - block.shape[0]), (0, 128 - block.shape[1])))
-
-
-def vectors_whole(blocks, own):
-    devices = blocks.shape[0] // 16
-    parts = blocks.reshape(devices, 16, 128)[:, :, : LAYERS * own]
-    parts = parts.reshape(devices, 16, LAYERS, own).transpose(2, 0, 1, 3).astype(F32)
-
-    def joined(first, count):
-        return parts[:, :, first : first + count].reshape(LAYERS, -1, devices * own)
-
-    singles = parts.transpose(0, 2, 1, 3).reshape(LAYERS, 16, devices * own)
-    return jnp.concatenate(
-        [singles[:, 0:2], joined(2, 2), singles[:, 4:8], joined(8, 4), singles[:, 12:16]], axis=1
-    )
-
-
-def vectors_split(rows, devices):
-    own = rows.shape[1] // devices
-
-    def shared(first, count):
-        return rows[first : first + count].reshape(devices, count, own)
-
-    singles = rows.reshape(16, devices, own).transpose(1, 0, 2)
-    block = jnp.concatenate(
-        [singles[:, 0:2], shared(2, 2), singles[:, 4:8], shared(8, 4), singles[:, 12:16]], axis=1
-    )
-    return jnp.pad(block, ((0, 0), (0, 0), (0, 128 - own))).reshape(devices * 16, 128)
-
-
-def after_that(value, *others):
-    return lax.optimization_barrier((value,) + others)[0]
-
-
-def window_labels(frames_here, windows):
-    token = np.arange(TOKENS)
-    late_t = token // CELLS >= WIN_T - WIN_T // 2
-    late_r = token // WIN_HW % WIN_HW >= WIN_HW - WIN_HW // 2
-    late_c = token % WIN_HW >= WIN_HW - WIN_HW // 2
+        [pltpu.VMEM((shape[0], 2) + shape[1:], F32), pltpu.VMEM(rest.shape, F32)],
+    )(flags, *grads, x, grad_middle, vec, weight, weight, weight, rest, *extra)
+
+
+def pack_shards_kernel(
+    gain1_ref, bias1_ref, qkv_ref, qvb_ref, out_ref, outb_ref, gain2_ref, bias2_ref, fc1_ref, fc1b_ref,
+    fc2_ref, fc2b_ref, first_ref, mid_ref, down_ref, later_ref, rows_ref,
+):
+    own, width = out_ref.shape[1:]
+    wide = fc1_ref.shape[2]
+    rows_ref[...] = jnp.zeros_like(rows_ref)
+    row = 0
+    lane = lax.broadcasted_iota(jnp.int32, (1, 128), 1)
+    for ref in (gain1_ref, bias1_ref, qvb_ref, outb_ref, gain2_ref, bias2_ref, fc2b_ref, fc1b_ref):
+        values = ref[...].astype(F32)
+        values = jnp.pad(values, ((0, 0), (0, 128 - values.shape[1])))
+        for part in range(ref.shape[1] // own):
+            line = jnp.zeros((1, 128), F32)
+            for layer in range(LAYERS):
+                turn = ((layer - part) * own) % 128
+                turned = pltpu.roll(values, turn, 1) if turn else values
+                here = (lane >= layer * own) & (lane < (layer + 1) * own)
+                line = jnp.where(here, turned[layer : layer + 1], line)
+            rows_ref[row : row + 1, :] = line
+            row += 1
+    first_ref[:, : 3 * width] = qkv_ref[0]
+    first_ref[:, 3 * width :] = rows_ref[...].astype(BF16)
+    mid_ref[:, :wide] = fc1_ref[0]
+    mid_ref[:, wide:] = out_ref[0]
+    later_ref[:, :wide] = fc1_ref[1]
+    later_ref[:, 2 * wide : 2 * wide + 3 * width] = qkv_ref[1]
+    later_ref[:, 2 * wide + 3 * width :] = out_ref[1]
+    for part in range(wide // width):
+        cols = slice(part * width, (part + 1) * width)
+        rows = slice(part * own, (part + 1) * own)
+        down_ref[:, cols] = fc2_ref[0, rows, :]
+        later_ref[:, wide + part * width : wide + (part + 1) * width] = fc2_ref[1, rows, :]
+
+
+def pack_shards(*shards):
+    own, width = shards[4].shape[1:]
+    wide = shards[8].shape[2]
+    widths = (3 * width + 128, wide + width, wide, 2 * wide + 4 * width)
+    return call(
+        pack_shards_kernel,
+        (1,),
+        [whole_block(s.shape) for s in shards],
+        [whole_block((own, w)) for w in widths],
+        [jax.ShapeDtypeStruct((own, w), BF16) for w in widths],
+        1e6,
+        [pltpu.VMEM((16, 128), F32)],
+    )(*shards)
+
+
+def vector_slots():
+    devices, own = 32, 16
+    count = devices * own
+    mask = np.zeros((devices * 16, count), np.float32)
+    pick = np.zeros((16, devices * 16), np.float32)
+    spread = np.zeros((LAYERS, 128, count), np.float32)
+    for device in range(devices):
+        for first, parts in ((0, 1), (1, 1), (2, 2), (4, 1), (5, 1), (6, 1), (7, 1), (8, 4)):
+            for part in range(parts):
+                row, start = divmod(device * own * parts + part * own, count)
+                slot = device * 16 + first + part
+                pick[first + row, slot] = 1
+                mask[slot, start : start + own] = 1
+    for layer in range(LAYERS):
+        for lane in range(count):
+            spread[layer, layer * own + lane % own, lane] = 1
+    return mask, pick, spread
+
+
+def vectors_kernel(block_ref, mask_ref, pick_ref, spread_ref, out_ref):
+    block = block_ref[...]
+    for layer in range(LAYERS):
+        lines = mm(block, spread_ref[layer]) * mask_ref[...].astype(F32)
+        out_ref[layer] = mm(pick_ref[...], lines.astype(BF16))
+
+
+def vectors_whole(blocks, after=()):
+    count, width = blocks.shape
+    extra = [jnp.asarray(a, BF16) for a in vector_slots()]
+    return functools.partial(call, after=after)(
+        vectors_kernel,
+        (1,),
+        [pl.BlockSpec((count, 128), lambda n: (0, width // 128 - 1))]
+        + [whole_block(a.shape) for a in extra],
+        whole_block((LAYERS, 16, count)),
+        jax.ShapeDtypeStruct((LAYERS, 16, count), F32),
+        1e9,
+    )(blocks, *extra)
+
+
+def place_flags():
     quadrant = lax.axis_index("space")
-    last = (lax.axis_index("tm") == lax.axis_size("tm") - 1).astype(jnp.int32)
-    at_end = last * (jnp.arange(windows) == windows - 1).astype(jnp.int32)
-    label = (
-        4 * at_end[:, None] * jnp.asarray(late_t, jnp.int32)
-        + 2 * (quadrant // 2) * jnp.asarray(late_r, jnp.int32)
-        + (quadrant % 2) * jnp.asarray(late_c, jnp.int32)
-    ).astype(F32)
-    return label[:, :, None], label[:, None, :]
+    last = lax.axis_index("tm") == lax.axis_size("tm") - 1
+    flags = [lax.axis_index("clip") % 2, last, quadrant // 2, quadrant % 2]
+    return jnp.stack([jnp.asarray(f, jnp.int32) for f in flags])
 
 
 def local_windows(
@@ -1166,100 +1454,123 @@
     _, frames_here, _, _, width = clips_in.shape
     windows = frames_here // WIN_T
     own = ln1_gain.shape[1]
-    devices = width // own
+    heads_here = pos_table.shape[2]
+    groups_here = heads_here // GROUP
     one, two = stage_orders()
-    half = 3 * width // 2
     flat = (windows, TOKENS, width)
-
-    small = vectors_in(
-        (ln1_gain, ln1_bias, qv_bias, out_bias, ln2_gain, ln2_bias, fc1_bias, fc2_bias)
-    )
-    first = gather_all(jnp.concatenate([qkv_weight[0][:, :half], small], axis=1), one)
-    second = gather_all(qkv_weight[0][:, half:], two)
-    vec = vectors_whole(first[:, half:], own)
-    w_qkv = [jnp.concatenate([first[:, :half], second], axis=1), None]
-
+    flags = place_flags()
+    send, place, stay, rows, starts, kinds = halo_matrices(frames_here)
+    flow = Flow()
+
+    def stepped(run, *args, names=(), **options):
+        out = run(*args, after=flow.pending(), **options)
+        flow.step(*names)
+        return out
+
+    def halo_start(name, packed, onward):
+        flow.start(name, halo_flow(packed, rows, starts, kinds, onward))
+
+    def send_table():
+        (came,) = yield [(tables, "tm", swap_pairs("tm", 0))]
+        first = lax.axis_index("tm") == 0
+        return jnp.where(first, tables, came), jnp.where(first, came, tables)
+
+    shards = (
+        ln1_gain, ln1_bias, qkv_weight, qv_bias, out_weight, out_bias,
+        ln2_gain, ln2_bias, fc1_weight, fc1_bias, fc2_weight, fc2_bias,
+    )
+    first, mid, down, later = pack_shards(*shards)
+    later = lax.all_gather(later, ("tm", "space", "clip"), axis=0, tiled=True)
     tables = pos_table.transpose(0, 2, 1)
-    beside = partner(tables, "tm", 0)
-    tables = jnp.where(
-        lax.axis_index("tm") == 1,
-        jnp.concatenate([beside, tables], 1),
-        jnp.concatenate([tables, beside], 1),
-    )
-    bias = table_to_bias(tables).reshape(LAYERS, HEADS, TOKENS, TOKENS)
-    labels = window_labels(frames_here, windows)
-    send, place, stay, rows, starts, kinds = halo_matrices(frames_here)
-
-    w_mid, w_two = [], []
-    gate = (first, second)
-    for layer in range(LAYERS):
-        if layer > 0:
-            shard = after_that(qkv_weight[layer], *gate)
-            parts = (gather_all(shard[:, :half], one), gather_all(shard[:, half:], two))
-            w_qkv[layer] = jnp.concatenate(parts, axis=1)
-            gate = parts
-        shard = jnp.concatenate([fc1_weight[layer], out_weight[layer]], axis=1)
-        shard, down = lax.optimization_barrier((shard, fc2_weight[layer]) + gate)[:2]
-        w_mid.append(gather_all(shard, one))
-        w_two.append(gather_all(down, two))
-        gate = (w_mid[-1], w_two[-1])
+    flow.start("tables", send_table())
+    flow.start("first", gather_flow(first, one))
+    flow.step()
+    tables = flow.finish("tables")
+    flow.start("mid", gather_flow(mid, one))
+    flow.start("down", gather_flow(down, two))
+    bias0 = [stepped(table_to_bias, tables[n][0]) for n in range(2)]
+    first = flow.finish("first")
+    vec = stepped(vectors_whole, first)
+    w_qkv = ((first, 0), (later, 8))
 
     stream0 = clips_in.reshape(flat)
-    qkv0 = run_qkv(stream0, vec[0], w_qkv[0])
-    att0, log0 = run_attend(qkv0, bias[0], labels, False)
-    mid0, hid0, slope0, stream1 = run_branch(stream0, att0, vec[0], w_mid[0], w_two[0], F32)
-    came = halo_permute(halo_pack(stream1, send, True), rows, starts, kinds, True)
-    rolled1 = halo_unpack(stream1, came, stay, place, starts, F32, center=True)
+    qkv0 = stepped(run_qkv, stream0, vec[0], w_qkv[0])
+    att0, log0 = [None, None], [None, None]
+    for n in range(2):
+        att0[n], log0[n] = stepped(run_attend, qkv0, bias0[n], flags, False, n * groups_here)
+    mid = flow.finish("mid")
+    weights = (
+        ((mid, 4), (mid, 0), (flow.finish("down"), 0)),
+        ((later, 11), (later, 0), (later, 1)),
+    )
+    mid0, hid0, slope0, stream1 = stepped(run_branch, stream0, att0, vec[0], weights[0], F32)
+    halo_start("roll", halo_pack(stream1, send, True), True)
+    table1 = jnp.concatenate([tables[0][1], tables[1][1]], axis=0)
+    bias1 = [stepped(table_to_bias, table1)]
+    rolled1 = halo_unpack(stream1, flow.finish("roll"), stay, place, starts, F32, center=True)
     qkv1 = run_qkv(rolled1, vec[1], w_qkv[1])
-    att1, log1 = run_attend(qkv1, bias[1], labels, True)
-    mid1, hid1, slope1, rolled_out = run_branch(rolled1, att1, vec[1], w_mid[1], w_two[1], F32)
-    back = halo_permute(halo_pack(rolled_out, place.T, False), rows, starts, kinds, False)
-    clips_out = halo_unpack(rolled_out, back, stay.T, send.T, starts, BF16, mean_of=stream1)
-
-    grad_in = after_that(out_grad, *gate).reshape(flat)
-    came = halo_permute(halo_pack(grad_in, send, False), rows, starts, kinds, True)
-    grad = halo_unpack(grad_in, came, stay, place, starts, BF16)
+    grad_in = out_grad.reshape(flat)
+    halo_start("grad", halo_pack(grad_in, send, False, after=[qkv1]), True)
+    att1, log1 = stepped(run_attend, qkv1, bias1[0], flags, True, 0)
+    mid1, hid1, slope1, rolled_out = run_branch(rolled1, [att1], vec[1], weights[1], F32)
+    halo_start("out", halo_pack(rolled_out, place.T, False), False)
+    grad = halo_unpack(grad_in, flow.finish("grad"), stay, place, starts, BF16)
 
     kept = (
-        (stream0, qkv0, att0, log0, mid0, hid0, slope0),
-        (rolled1, qkv1, att1, log1, mid1, hid1, slope1),
-    )
-    shares, table_parts = [None] * LAYERS, [None] * LAYERS
+        (stream0, qkv0, att0, log0, mid0, hid0, slope0, bias0),
+        (rolled1, qkv1, [att1], [log1], mid1, hid1, slope1, bias1),
+    )
+    rests, tables = [None] * LAYERS, [None] * LAYERS
     for layer in reversed(range(LAYERS)):
-        stream, qkv, att, log, mid, hid, slope = kept[layer]
-        grad_mid, grad_att, d_mid, d_two, vecs = run_branch_back(
-            grad, mid, att, hid, slope, vec[layer], w_mid[layer], w_two[layer]
+        stream, qkv, att, log, mid, hid, slope, bias = kept[layer]
+        grad_mid, grad_att, rest, *halves = stepped(
+            run_branch_back, grad, mid, att, hid, slope, vec[layer], weights[layer], flags, layer == 0
         )
-        mid_share = scatter_all(d_mid, one)
-        two_share = scatter_all(d_two, two)
-        *grads, table = run_attend_back(qkv, grad_att, bias[layer], labels, log, layer == 1)
-        grad_stream, d_qkv, vecs_one = run_qkv_back(
-            grads, stream, grad_mid, vec[layer], w_qkv[layer], F32 if layer else BF16
+        if layer == 0:
+            flow.start("d_mid", scatter_flow(*halves[:2], one))
+            flow.start("d_two", scatter_flow(*halves[2:], two))
+        else:
+            mid_share1 = lax.psum_scatter(
+                halves[0], ("tm", "space", "clip"), scatter_dimension=0, tiled=True
+            ).astype(F32)
+            clips_out = stepped(
+                halo_unpack, rolled_out, flow.finish("out"), stay.T, send.T, starts, BF16,
+                mean_of=stream1,
+            )
+        grads, sums = [], []
+        for n in range(len(att)):
+            *parts, total = stepped(
+                run_attend_back, qkv, grad_att, att[n], bias[n], flags, log[n],
+                layer == 1, n * groups_here,
+            )
+            grads.append(parts)
+            sums.append(total)
+        grads = [part for group in zip(*grads) for part in group]
+        grad_stream, *halves = stepped(
+            run_qkv_back, grads, stream, grad_mid, vec[layer], w_qkv[layer], rest, flags,
+            F32 if layer else BF16,
         )
-        vecs = jnp.concatenate([vecs_one[:4], vecs[4:]], axis=0)
-        packed = jnp.concatenate([d_qkv[:, :half], vectors_split(vecs, devices)], axis=1)
-        left = scatter_all(packed, one)
-        right = scatter_all(d_qkv[:, half:], two)
-        shares[layer] = (mid_share, two_share, left, right)
-        table = bias_grad_to_table(table)
-        heads_here = pos_table.shape[2]
-        mine = lax.dynamic_slice_in_dim(table, lax.axis_index("tm") * heads_here, heads_here, 0)
-        theirs = lax.dynamic_slice_in_dim(
-            table, (1 - lax.axis_index("tm")) * heads_here, heads_here, 0
-        )
-        table = mine + partner(theirs, "tm", 0)
-        for axis, bit in one:
-            if axis != "tm":
-                table = table + partner(table, axis, bit)
-        table_parts[layer] = table
         if layer:
-            back = halo_permute(halo_pack(grad_stream, place.T, False), rows, starts, kinds, False)
-            grad = halo_unpack(grad_stream, back, stay.T, send.T, starts, F32)
+            halo_start("back", halo_pack(grad_stream, place.T, False), False)
+        flow.start(f"d_qkv{layer}", scatter_flow(*halves, one))
+        found = [stepped(sums_to_table, total) for total in sums]
+        tables[layer] = jnp.split(found[0], 2) if len(found) == 1 else found
+        if layer:
+            grad = halo_unpack(grad_stream, flow.finish("back"), stay.T, send.T, starts, F32)
     in_grad = grad_stream
-
+    pairs = [jnp.stack([tables[layer][n] for layer in range(LAYERS)]) for n in range(2)]
+    flow.start("table", table_flow(pairs, heads_here))
+
+    while flow.live:
+        flow.step()
     wide = fc1_weight.shape[2]
-    mid_share, two_share, left, right = (jnp.stack(s) for s in zip(*shares))
-    small = left[:, :, half : half + own]
+    mixes = jnp.stack([flow.done[f"d_qkv{layer}"] for layer in range(LAYERS)])
+    mid_share0, two_share0 = flow.done["d_mid"], flow.done["d_two"]
+    two_share1 = jnp.concatenate(
+        [mid_share1[:, first : first + width] for first in range(wide + width, wide * 2 + width, width)],
+        axis=0,
+    )
+    small = mixes[:, :, 3 * width : 3 * width + own]
 
     def vector(row, count=1):
         return small[:, row : row + count].reshape(LAYERS, count * own)
@@ -1269,17 +1580,17 @@
         in_grad.reshape(clips_in.shape),
         vector(0),
         vector(1),
-        jnp.concatenate([left[:, :, :half], right], axis=2),
+        mixes[:, :, : 3 * width],
         vector(2, 2),
-        mid_share[:, :, wide:],
+        jnp.stack([s[:, wide : wide + width] for s in (mid_share0, mid_share1)]),
         vector(4),
         vector(5),
         vector(6),
-        mid_share[:, :, :wide],
+        jnp.stack([s[:, :wide] for s in (mid_share0, mid_share1)]),
         vector(8, 4),
-        two_share,
+        jnp.stack([two_share0, two_share1]),
         vector(7),
-        jnp.stack(table_parts).transpose(0, 2, 1),
+        flow.done["table"].transpose(0, 2, 1),
     )
 
 

time: 909 us -> 543 us (0.60)
  waiting for transfers between devices: 237 us -> 73 us
  Pallas kernels: 368 us -> 284 us
  local copies, waits for them, and re-layouts: 110 us -> 58.1 us
  starting transfers between devices: 130 us -> 91.4 us
  matrix products: 20.6 us -> 0 us
  other arithmetic: 32.8 us -> 15.9 us
  between operations: 2.91 us -> 15.8 us
    ppermute x119 -> x69, waiting for transfers between devices: 237 us -> 72.9 us  [step(): came = [lax.ppermute(value, axis, pairs) for value, axis, pairs in sends]]
    pallas_call x21 -> x30, Pallas kernels: 368 us -> 284 us  [call(): return lambda *args: run(*args, *after)]
    ppermute x119 -> x69, starting transfers between devices: 130 us -> 91.3 us  [step(): came = [lax.ppermute(value, axis, pairs) for value, axis, pairs in sends]]
    slice x37 -> x18, local copies, waits for them, and re-layouts: 41.1 us -> 19.5 us  [the longest x16 18.7 us: halo_flow(): sends.append((packed[start:start + count], ('tm', 'space'), pairs))]
    dot_general x3 -> x0, matrix products: 20.6 us -> none  [the longest x2 17 us: bias_grad_to_table(): jnp.einsum('hjkm,kem->hje', parts, shift, precision=lax.Precision.HIGH, p...]
    convert_element_type x39 -> x16, local copies, waits for them, and re-layouts: 18.6 us -> 3.28 us  [scatter_flow(): sent = lax.dynamic_slice_in_dim(out, 1 - here, 1, dim).astype(BF16)]
    reshape x22 -> x1, local copies, waits for them, and re-layouts: 13.8 us -> 1.14 us  [local_windows(): grad_in = out_grad.reshape(flat)]
  transfers between devices with their start and end apart: 119 -> 71, of which waited for: 55 -> 14; matrix products, arithmetic and copies ran while one was open for 16% -> 11% of each run, Pallas kernels for 38% -> 39%
where the time goes in v2:
time: 543 us; the launch traced here: 538 us
  Pallas kernels  284 us (52%)
  starting transfers between devices  91.4 us (17%)
  waiting for transfers between devices  73 us (13%)
  local copies, waits for them, and re-layouts  58.1 us (11%)
  other arithmetic  15.9 us (3%)
  between operations  15.8 us (3%)
    pallas_call x30, Pallas kernels, call(): return lambda *args: run(*args, *after)  284 us
    ppermute x69, starting transfers between devices, step(): came = [lax.ppermute(value, axis, pairs) for value, axis, pairs in sends]  91.3 us
    ppermute x69, waiting for transfers between devices, step(): came = [lax.ppermute(value, axis, pairs) for value, axis, pairs in sends]  72.9 us
    slice x16, local copies, waits for them, and re-layouts, halo_flow(): sends.append((packed[start:start + count], ('tm', 'space'), pairs))  18.7 us
    unnamed x170, local copies, waits for them, and re-layouts  11.1 us
  transfers between devices with their start and end apart: 71, of which 14 were waited for; matrix products, arithmetic and copies ran while one was open for 11% of the time, Pallas kernels for 39%

profile of v2, /device:TPU:0, one launch (start us, length us, event | category | flops | bytes accessed | tf_op | source)
XLA Modules:
  0.0 538.0 jit_solution(6069361378821485485)
XLA Ops:
  27.8 7.9 %shard_map.616.refs_4_.refs_6_ = f32[8,392,392]{2,1,0:T(8,128)} custom-call(bf16[128,256]{1,0:T(8,128)(2,1)} %bitcast.173, bf16[7,256,128]{2,1,0:T(8,128)(2,1)} %constant.231.clone.refs_1_, bf16[1,2,1,1,1,16,1664]{6,5,4,3,2,1,0:T(8,128)(2,1)} %fusion.40.refs_2_, bf16[1,1,1,1,1,16,2560]{6,5,4,3,2,1,0:T(8,128)(2,1)} %bitcast.158, ...), custom_call_target="tpu_custom_call" | custom-call | flops 4000000000 | bytes 8388608 | tf_op jit(solution)/shard_map/pallas_call | solution.py:542
  39.8 7.6 %shard_map.618.refs_4_.refs_6_ = f32[8,392,392]{2,1,0:T(8,128)} custom-call(bf16[128,256]{1,0:T(8,128)(2,1)} %bitcast.172, bf16[7,256,128]{2,1,0:T(8,128)(2,1)} %constant.231.clone.refs_1_, bf16[1,2,2,1,1,16,1664]{6,5,4,3,2,1,0:T(8,128)(2,1)} %copy-done.23, bf16[1,2,1,1,1,16,2560]{6,5,4,3,2,1,0:T(8,128)(2,1)} %copy-done.27, ...), custom_call_target="tpu_custom_call" | custom-call | flops 4000000000 | bytes 8388608 | tf_op jit(solution)/shard_map/pallas_call | solution.py:542
  60.8 7.3 %collective-permute-done.3 = bf16[1,2,2,2,1,16,1664]{6,5,2,1,3,4,0:T(8,128)(2,1)S(1)} collective-permute-done((bf16[1,2,2,2,1,16,1664]{6,5,2,1,3,4,0:T(8,128)(2,1)S(1)}, bf16[1,2,2,2,1,16,1664]{6,5,2,1,3,4,0:T(8,128)(2,1)S(1)}, u32[]{:S(2)}, u32[]{:S(2)}) %collective-permute-start.3) | collective-permute-done | bytes 426016 | tf_op jit(solution)/shard_map/ppermute | solution.py:609
  68.4 7.1 %collective-permute-done.13 = bf16[2,2,2,1,1,16,2048]{6,5,1,2,0,4,3:T(8,128)(2,1)S(1)} collective-permute-done((bf16[2,2,2,1,1,16,2048]{6,5,1,2,0,4,3:T(8,128)(2,1)S(1)}, bf16[2,2,2,1,1,16,2048]{6,5,1,2,0,4,3:T(8,128)(2,1)S(1)}, u32[]{:S(2)}, u32[]{:S(2)}) %collective-permute-start.13) | collective-permute-done | bytes 524320 | tf_op jit(solution)/shard_map/ppermute | solution.py:609
  76.8 13.2 %collective-permute-done.12 = bf16[1,2,2,2,1,16,2560]{6,5,1,2,3,4,0:T(8,128)(2,1)S(1)} collective-permute-done((bf16[1,2,2,2,1,16,2560]{6,5,1,2,3,4,0:T(8,128)(2,1)S(1)}, bf16[1,2,2,2,1,16,2560]{6,5,1,2,3,4,0:T(8,128)(2,1)S(1)}, u32[]{:S(2)}, u32[]{:S(2)}) %collective-permute-start.12) | collective-permute-done | bytes 655392 | tf_op jit(solution)/shard_map/ppermute | solution.py:609
  101.8 10.3 %shard_map.619 = (bf16[2,392,256]{2,1,0:T(8,128)(2,1)}, f32[2,2,8,392]{3,2,1,0:T(8,128)}) custom-call(s32[4]{0:T(128)} %pad_add_fusion.refs_0_, bf16[2,392,1536]{2,1,0:T(8,128)(2,1)} %shard_map.615.refs_1_.refs_2_.refs_3_, bf16[2,392,1536]{2,1,0:T(8,128)(2,1)} %shard_map.615.refs_1_.refs_2_.refs_3_, ...), custom_call_target="tpu_custom_call" | custom-call | flops 5035261952 | bytes 8388608 | tf_op jit(solution)/shard_map/pallas_call | solution.py:542
  112.1 10.3 %shard_map.617 = (bf16[2,392,256]{2,1,0:T(8,128)(2,1)}, f32[2,2,8,392]{3,2,1,0:T(8,128)}) custom-call(s32[4]{0:T(128)} %pad_add_fusion.refs_0_, bf16[2,392,1536]{2,1,0:T(8,128)(2,1)} %shard_map.615.refs_1_.refs_2_.refs_3_, bf16[2,392,1536]{2,1,0:T(8,128)(2,1)} %shard_map.615.refs_1_.refs_2_.refs_3_, ...), custom_call_target="tpu_custom_call" | custom-call | flops 5035261952 | bytes 8388608 | tf_op jit(solution)/shard_map/pallas_call | solution.py:542
  126.4 11.8 %shard_map.620 = (f32[2,392,512]{2,1,0:T(8,128)}, bf16[2,392,2048]{2,1,0:T(8,128)(2,1)}, bf16[2,392,2048]{2,1,0:T(8,128)(2,1)}, f32[2,392,512]{2,1,0:T(8,128)}) custom-call(bf16[2,392,256]{2,1,0:T(8,128)(2,1)} %get-tuple-element.65.refs_0_.refs_1_.refs_5_, bf16[2,392,256]{2,1,0:T(8,128)(2,1)} %get-tuple-element.66.refs_1_.refs_2_.refs_5_, ...), custom_call_target="tpu_custom_call" | custom-call | flops 3699376128 | bytes 8388608 | tf_op jit(solution)/shard_map/pallas_call | solution.py:542
  156.8 13.5 %shard_map.624.refs_4_.refs_6_ = f32[16,392,392]{2,1,0:T(8,128)} custom-call(bf16[256,256]{1,0:T(8,128)(2,1)} %bitcast.168, bf16[7,256,128]{2,1,0:T(8,128)(2,1)} %constant.231.clone.refs_1_, bf16[144,512]{1,0:T(8,128)(2,1)} %copy-done.40, bf16[144,512]{1,0:T(8,128)(2,1)} %copy-done.39, bf16[112,512]{1,0:T(8,128)(2,1)} %copy-done.45, ...), custom_call_target="tpu_custom_call" | custom-call | flops 8000000000 | bytes 8388608 | tf_op jit(solution)/shard_map/pallas_call | solution.py:542
  171.2 6.0 %shard_map.622.refs_0_.refs_1_.refs_4_ = f32[2,392,512]{2,1,0:T(8,128)} custom-call(bf16[784,784]{1,0:T(8,128)(2,1)} %constant.238.clone.refs_0_, bf16[784,608]{1,0:T(8,128)(2,1)} %constant.239.clone.refs_1_, f32[2,392,512]{2,1,0:T(8,128)} %get-tuple-element.67.refs_1_.refs_2_.refs_3_, f32[2,8,128]{2,1,0:T(8,128)} %broadcast_1_refs_3_.2.refs_3_, ...), custom_call_target="tpu_custom_call" | custom-call | flops 1258815488 | bytes 8388608 | tf_op jit(solution)/shard_map/pallas_call | solution.py:542
  199.4 18.8 %shard_map.626 = (bf16[2,392,512]{2,1,0:T(8,128)(2,1)}, f32[2,4,8,392]{3,2,1,0:T(8,128)}) custom-call(s32[4]{0:T(128)} %pad_add_fusion.refs_0_, bf16[2,392,1536]{2,1,0:T(8,128)(2,1)} %shard_map.623.refs_2_.refs_1_.refs_3_, bf16[2,392,1536]{2,1,0:T(8,128)(2,1)} %shard_map.623.refs_2_.refs_1_.refs_3_, ...), custom_call_target="tpu_custom_call" | custom-call | flops 10070523904 | bytes 8388608 | tf_op jit(solution)/shard_map/pallas_call | solution.py:542
  218.2 12.0 %shard_map.627 = (f32[2,392,512]{2,1,0:T(8,128)}, bf16[2,392,2048]{2,1,0:T(8,128)(2,1)}, bf16[2,392,2048]{2,1,0:T(8,128)(2,1)}, f32[2,392,512]{2,1,0:T(8,128)}) custom-call(bf16[2,392,512]{2,1,0:T(8,128)(2,1)} %get-tuple-element.69.refs_0_.refs_1_.refs_5_, f32[2,392,512]{2,1,0:T(8,128)} %shard_map.622.refs_0_.refs_1_.refs_4_, ...), custom_call_target="tpu_custom_call" | custom-call | flops 3699376128 | bytes 8388608 | tf_op jit(solution)/shard_map/pallas_call | solution.py:542
  248.9 19.2 %shard_map.631 = (f32[2,392,512]{2,1,0:T(8,128)}, bf16[2,392,512]{2,1,0:T(8,128)(2,1)}, f32[16,512]{1,0:T(8,128)}, bf16[512,4608]{1,0:T(8,128)(2,1)}) custom-call(s32[4]{0:T(128)} %pad_add_fusion.refs_0_, bf16[2,392,512]{2,1,0:T(8,128)(2,1)} %get-tuple-element.69.refs_0_.refs_1_.refs_5_, bf16[2,392,512]{2,1,0:T(8,128)(2,1)} %shard_map.630.refs_2_, ...), custom_call_target="tpu_custom_call" | custom-call | flops 7398752256 | bytes 8388608 | tf_op jit(solution)/shard_map/pallas_call | solution.py:542
  268.1 28.0 %shard_map.632 = (bf16[2,392,512]{2,1,0:T(8,128)(2,1)}, bf16[2,392,512]{2,1,0:T(8,128)(2,1)}, bf16[2,392,512]{2,1,0:T(8,128)(2,1)}, f32[16,49,768]{2,1,0:T(8,128)}) custom-call(s32[4]{0:T(128)} %pad_add_fusion.refs_0_, bf16[2,392,1536]{2,1,0:T(8,128)(2,1)} %shard_map.623.refs_2_.refs_1_.refs_3_, bf16[2,392,1536]{2,1,0:T(8,128)(2,1)} %shard_map.623.refs_2_.refs_1_.refs_3_, ...), custom_call_target="tpu_custom_call" | custom-call | flops 25176309760 | bytes 8388608 | tf_op jit(solution)/shard_map/pallas_call | solution.py:542
  296.1 10.8 %shard_map.633 = (f32[2,392,512]{2,1,0:T(8,128)}, f32[16,16,1664]{2,1,0:T(8,128)}, bf16[16,16,1664]{2,1,0:T(8,128)(2,1)}) custom-call(s32[4]{0:T(128)} %pad_add_fusion.refs_0_, bf16[2,392,512]{2,1,0:T(8,128)(2,1)} %get-tuple-element.76.refs_1_, bf16[2,392,512]{2,1,0:T(8,128)(2,1)} %get-tuple-element.77.refs_2_, ...), custom_call_target="tpu_custom_call" | custom-call | flops 2466250752 | bytes 8388608 | tf_op jit(solution)/shard_map/pallas_call | solution.py:542
  331.8 6.1 %shard_map.629 = bf16[2,392,512]{2,1,0:T(8,128)(2,1)} custom-call(bf16[784,784]{1,0:T(8,128)(2,1)} %constant.241.clone.refs_0_, bf16[784,608]{1,0:T(8,128)(2,1)} %constant.242.clone.refs_1_, f32[2,392,512]{2,1,0:T(8,128)} %get-tuple-element.70.refs_1_.refs_2_, f32[2,392,512]{2,1,0:T(8,128)} %get-tuple-element.67.refs_1_.refs_2_.refs_3_, ...), custom_call_target="tpu_custom_call" | custom-call | flops 1258815488 | bytes 8388608 | tf_op jit(solution)/shard_map/pallas_call | solution.py:542
  352.2 10.8 %shard_map.641 = f32[256,256]{1,0:T(8,128)} custom-call(f32[16,49,768]{2,1,0:T(8,128)} %get-tuple-element.107.refs_0_, bf16[7,256,128]{2,1,0:T(8,128)(2,1)} %constant.231.clone.refs_1_, bf16[144,512]{1,0:T(8,128)(2,1)} %copy-done.36, bf16[144,512]{1,0:T(8,128)(2,1)} %copy-done.35, bf16[112,512]{1,0:T(8,128)(2,1)} %slice.261.refs_4_, ...), custom_call_target="tpu_custom_call" | custom-call | flops 4800000000 | bytes 8388608 | tf_op jit(solution)/shard_map/pallas_call | solution.py:542
  381.1 20.5 %shard_map.636 = (f32[2,392,512]{2,1,0:T(8,128)}, bf16[2,392,512]{2,1,0:T(8,128)(2,1)}, f32[16,512]{1,0:T(8,128)}, f32[16,16,2560]{2,1,0:T(8,128)}, bf16[16,16,2...) custom-call(s32[4]{0:T(128)} %pad_add_fusion.refs_0_, ...), custom_call_target="tpu_custom_call" | custom-call | flops 7398752256 | bytes 8388608 | tf_op jit(solution)/shard_map/pallas_call | solution.py:542
  404.5 15.0 %shard_map.637 = (bf16[2,392,256]{2,1,0:T(8,128)(2,1)}, bf16[2,392,256]{2,1,0:T(8,128)(2,1)}, bf16[2,392,256]{2,1,0:T(8,128)(2,1)}, f32[8,49,768]{2,1,0:T(8,128)}) custom-call(s32[4]{0:T(128)} %pad_add_fusion.refs_0_, bf16[2,392,1536]{2,1,0:T(8,128)(2,1)} %shard_map.615.refs_1_.refs_2_.refs_3_, bf16[2,392,1536]{2,1,0:T(8,128)(2,1)} %shard_map.615.refs_1_.refs_2_.refs_3_, ...), custom_call_target="tpu_custom_call" | custom-call | flops 12588154880 | bytes 8388608 | tf_op jit(solution)/shard_map/pallas_call | solution.py:542
  422.9 15.1 %collective-permute-done.51 = bf16[2,2,2,1,1,64,512]{6,5,4,3,2,1,0:T(8,128)(2,1)S(1)} collective-permute-done((bf16[2,2,2,1,1,64,512]{6,5,4,3,2,1,0:T(8,128)(2,1)S(1)}, bf16[2,2,2,1,1,64,512]{6,5,4,3,2,1,0:T(8,128)(2,1)S(1)}, u32[]{:S(2)}, u32[]{:S(2)}) %collective-permute-start.51) | collective-permute-done | bytes 524320 | tf_op jit(solution)/shard_map/ppermute | solution.py:609
  439.2 14.8 %shard_map.638 = (bf16[2,392,256]{2,1,0:T(8,128)(2,1)}, bf16[2,392,256]{2,1,0:T(8,128)(2,1)}, bf16[2,392,256]{2,1,0:T(8,128)(2,1)}, f32[8,49,768]{2,1,0:T(8,128)}) custom-call(s32[4]{0:T(128)} %pad_add_fusion.refs_0_, bf16[2,392,1536]{2,1,0:T(8,128)(2,1)} %shard_map.615.refs_1_.refs_2_.refs_3_, bf16[2,392,1536]{2,1,0:T(8,128)(2,1)} %shard_map.615.refs_1_.refs_2_.refs_3_, ...), custom_call_target="tpu_custom_call" | custom-call | flops 12588154880 | bytes 8388608 | tf_op jit(solution)/shard_map/pallas_call | solution.py:542
  456.3 10.3 %shard_map.639 = (bf16[2,392,512]{2,1,0:T(8,128)(2,1)}, f32[16,16,1664]{2,1,0:T(8,128)}, bf16[16,16,1664]{2,1,0:T(8,128)(2,1)}) custom-call(s32[4]{0:T(128)} %pad_add_fusion.refs_0_, bf16[2,392,256]{2,1,0:T(8,128)(2,1)} %get-tuple-element.91.refs_1_, bf16[2,392,256]{2,1,0:T(8,128)(2,1)} %get-tuple-element.95.refs_2_, ...), custom_call_target="tpu_custom_call" | custom-call | flops 2466250752 | bytes 8388608 | tf_op jit(solution)/shard_map/pallas_call | solution.py:542
  485.0 6.0 %shard_map.642 = f32[128,256]{1,0:T(8,128)} custom-call(f32[8,49,768]{2,1,0:T(8,128)} %get-tuple-element.108.refs_0_, bf16[7,256,128]{2,1,0:T(8,128)(2,1)} %constant.231.clone.refs_1_, bf16[1,1,1,1,1,16,2560]{6,5,4,3,2,1,0:T(8,128)(2,1)} %dynamic-slice_convert_fusion.12.refs_2_, bf16[1,1,1,1,1,64,512]{6,5,4,3,2,1,0:T(8,128)(2,1)} %dynamic-slice_convert_fusion.13.refs_3_, ...), custom_call_target="tpu_custom_call" | custom-call | flops 2400000000 | bytes 8388608 | tf_op jit(solution)/shard_map/pallas_call | solution.py:542
  500.7 7.0 %collective-permute-done.53 = bf16[1,2,2,2,1,16,1664]{6,5,4,3,2,1,0:T(8,128)(2,1)S(1)} collective-permute-done((bf16[1,2,2,2,1,16,1664]{6,5,4,3,2,1,0:T(8,128)(2,1)S(1)}, bf16[1,2,2,2,1,16,1664]{6,5,4,3,2,1,0:T(8,128)(2,1)S(1)}, u32[]{:S(2)}, u32[]{:S(2)}) %collective-permute-start.53) | collective-permute-done | bytes 426016 | tf_op jit(solution)/shard_map/ppermute | solution.py:609
  (452 shorter events, 232.8 us)
Async XLA Ops:
  7.2 170.1 %all-gather.2.cloned.1.call-start = ((), (), s32[]{:S(2)}) async-start(), calls=%async_computation.1 | async-start | bytes 6488064 | tf_op jit(solution)/shard_map/all_gather | solution.py:1483
  13.2 23.2 %collective-permute-start.5 = (bf16[1,1,1,1,1,16,2560]{6,5,4,3,2,1,0:T(8,128)(2,1)}, bf16[1,1,1,1,1,16,2560]{6,5,4,3,2,1,0:T(8,128)(2,1)S(1)}, u32[]{:S(2)}, u32[]{:S(2)}) collective-permute-start(bf16[1,1,1,1,1,16,2560]{6,5,4,3,2,1,0:T(8,128)(2,1)} %bitcast.157), channel_id=1, source_target_pairs={{0,8},{4,12},{8,0},{12,4},{1,9},{5,13},{9,1},{13,5},{2,10},{6,14},... | collective-permute-start | bytes 245768 | tf_op jit(solution)/shard_map/ppermute | solution.py:609
  17.6 509.6 %reduce-scatter.2.cloned.1.call-start = ((), (), s32[]{:S(2)}) async-start(), calls=%async_computation.2 | async-start | bytes 4866048 | tf_op jit(solution)/shard_map/reduce_scatter | solution.py:1533
  25.1 22.3 %collective-permute-start.8 = (bf16[1,2,1,1,1,16,2048]{6,5,4,3,2,1,0:T(8,128)(2,1)S(1)}, bf16[1,2,1,1,1,16,2048]{6,5,4,3,2,1,0:T(8,128)(2,1)S(1)}, u32[]{:S(2)}, u32[]{:S(2)}) collective-permute-start(bf16[1,2,1,1,1,16,2048]{6,5,4,3,2,1,0:T(8,128)(2,1)S(1)} %maximum_select_fusion.19.refs_4_), channel_id=1, source_target_pairs={{0,4},{4,0},{8,12},{12,8},{1,5},{5,1},{9,13},{13,9},{2,6},{6,2},{1... | collective-permute-start | bytes 393224 | tf_op jit(solution)/shard_map/ppermute | solution.py:609
  60.2 29.8 %collective-permute-start.12 = (bf16[1,2,2,2,1,16,2560]{6,5,1,2,3,4,0:T(8,128)(2,1)S(1)}, bf16[1,2,2,2,1,16,2560]{6,5,1,2,3,4,0:T(8,128)(2,1)S(1)}, u32[]{:S(2)}, u32[]{:S(2)}) collective-permute-start(bf16[1,2,2,2,1,16,2560]{6,5,1,2,3,4,0:T(8,128)(2,1)S(1)} %maximum_select_fusion.6), channel_id=1, source_target_pairs={{0,16},{16,0},{1,17},{17,1},{2,18},{18,2},{3,19},{19,3},{4,20},{20... | collective-permute-start | bytes 1966088 | tf_op jit(solution)/shard_map/ppermute | solution.py:609
  68.2 23.2 %collective-permute-start.4 = (bf16[2,2,2,2,1,16,1664]{6,5,2,1,3,4,0:T(8,128)(2,1)S(1)}, bf16[2,2,2,2,1,16,1664]{6,5,2,1,3,4,0:T(8,128)(2,1)S(1)}, u32[]{:S(2)}, u32[]{:S(2)}) collective-permute-start(bf16[2,2,2,2,1,16,1664]{6,5,2,1,3,4,0:T(8,128)(2,1)S(1)} %maximum_select_fusion.5), channel_id=1, source_target_pairs={{0,1},{1,0},{2,3},{3,2},{4,5},{5,4},{6,7},{7,6},{8,9},{9,8},{10,11... | collective-permute-start | bytes 2555912 | tf_op jit(solution)/shard_map/ppermute | solution.py:609
  76.8 45.7 %collective-permute-start.15 = (bf16[2,2,2,2,1,16,2048]{6,5,1,2,0,4,3:T(8,128)(2,1)S(1)}, bf16[2,2,2,2,1,16,2048]{6,5,1,2,0,4,3:T(8,128)(2,1)S(1)}, u32[]{:S(2)}, u32[]{:S(2)}) collective-permute-start(bf16[2,2,2,2,1,16,2048]{6,5,1,2,0,4,3:T(8,128)(2,1)S(1)} %maximum_select_fusion.4), channel_id=1, source_target_pairs={{0,1},{1,0},{2,3},{3,2},{4,5},{5,4},{6,7},{7,6},{8,9},{9,8},{10,11... | collective-permute-start | bytes 3145736 | tf_op jit(solution)/shard_map/ppermute | solution.py:609
  91.4 32.8 %collective-permute-start.14 = (bf16[2,2,2,2,1,16,2560]{6,5,1,2,3,4,0:T(8,128)(2,1)S(1)}, bf16[2,2,2,2,1,16,2560]{6,5,1,2,3,4,0:T(8,128)(2,1)S(1)}, u32[]{:S(2)}, u32[]{:S(2)}) collective-permute-start(bf16[2,2,2,2,1,16,2560]{6,5,1,2,3,4,0:T(8,128)(2,1)S(1)} %maximum_select_fusion.3), channel_id=1, source_target_pairs={{0,1},{1,0},{2,3},{3,2},{4,5},{5,4},{6,7},{7,6},{8,9},{9,8},{10,11... | collective-permute-start | bytes 3932168 | tf_op jit(solution)/shard_map/ppermute | solution.py:609
  150.4 20.0 %collective-permute-start.16 = (bf16[144,512]{1,0:T(8,128)(2,1)S(1)}, bf16[144,512]{1,0:T(8,128)(2,1)S(1)}, u32[]{:S(2)}, u32[]{:S(2)}) collective-permute-start(bf16[144,512]{1,0:T(8,128)(2,1)S(1)} %get-tuple-element.158.refs_2_), channel_id=1, source_target_pairs={{0,4},{4,0},{8,12},{12,8},{16,20},{20,16},{24,28},{28,24},{1,5},{5... | collective-permute-start | bytes 442376 | tf_op jit(solution)/shard_map/ppermute | solution.py:609
  150.9 19.6 %collective-permute-start.17 = (bf16[144,512]{1,0:T(8,128)(2,1)S(1)}, bf16[144,512]{1,0:T(8,128)(2,1)S(1)}, u32[]{:S(2)}, u32[]{:S(2)}) collective-permute-start(bf16[144,512]{1,0:T(8,128)(2,1)S(1)} %get-tuple-element.157.refs_3_), channel_id=1, source_target_pairs={{0,8},{4,12},{8,0},{12,4},{16,24},{20,28},{24,16},{28,20},{1,9},{5... | collective-permute-start | bytes 442376 | tf_op jit(solution)/shard_map/ppermute | solution.py:609
  190.2 52.7 %collective-permute-start.30 = (bf16[144,512]{1,0:T(8,128)(2,1)S(1)}, bf16[144,512]{1,0:T(8,128)(2,1)S(1)}, u32[]{:S(2)}, u32[]{:S(2)}) collective-permute-start(bf16[144,512]{1,0:T(8,128)(2,1)S(1)} %get-tuple-element.153.refs_7_), channel_id=1, source_target_pairs={{0,4},{4,0},{8,12},{12,8},{16,20},{20,16},{24,28},{28,24},{1,5},{5... | collective-permute-start | bytes 442376 | tf_op jit(solution)/shard_map/ppermute | solution.py:609
  190.2 52.7 %collective-permute-start.31 = (bf16[144,512]{1,0:T(8,128)(2,1)S(1)}, bf16[144,512]{1,0:T(8,128)(2,1)S(1)}, u32[]{:S(2)}, u32[]{:S(2)}) collective-permute-start(bf16[144,512]{1,0:T(8,128)(2,1)S(1)} %get-tuple-element.152.refs_8_), channel_id=1, source_target_pairs={{0,8},{4,12},{8,0},{12,4},{16,24},{20,28},{24,16},{28,20},{1,9},{5... | collective-permute-start | bytes 442376 | tf_op jit(solution)/shard_map/ppermute | solution.py:609
  194.1 48.8 %collective-permute-start.32 = (bf16[112,512]{1,0:T(8,128)(2,1)S(1)}, bf16[112,512]{1,0:T(8,128)(2,1)S(1)}, u32[]{:S(2)}, u32[]{:S(2)}) collective-permute-start(bf16[112,512]{1,0:T(8,128)(2,1)S(1)} %slice.247.refs_9_), channel_id=1, source_target_pairs={{0,12},{4,8},{8,4},{12,0},{16,28},{20,24},{24,20},{28,16},{1,13},{... | collective-permute-start | bytes 344072 | tf_op jit(solution)/shard_map/ppermute | solution.py:609
  194.6 40.8 %collective-permute-start.34 = (bf16[48,512]{1,0:T(8,128)(2,1)S(1)}, bf16[48,512]{1,0:T(8,128)(2,1)S(1)}, u32[]{:S(2)}, u32[]{:S(2)}) collective-permute-start(bf16[48,512]{1,0:T(8,128)(2,1)S(1)} %get-tuple-element.151.refs_11_), channel_id=1, source_target_pairs={{0,20},{4,16},{8,28},{12,24},{16,4},{20,0},{24,12},{28,8},{1,21},{... | collective-permute-start | bytes 147464 | tf_op jit(solution)/shard_map/ppermute | solution.py:609
  194.6 41.4 %collective-permute-start.35 = (bf16[48,512]{1,0:T(8,128)(2,1)S(1)}, bf16[48,512]{1,0:T(8,128)(2,1)S(1)}, u32[]{:S(2)}, u32[]{:S(2)}) collective-permute-start(bf16[48,512]{1,0:T(8,128)(2,1)S(1)} %get-tuple-element.150.refs_12_), channel_id=1, source_target_pairs={{0,24},{4,28},{8,16},{12,20},{16,8},{20,12},{24,0},{28,4},{1,25},{... | collective-permute-start | bytes 147464 | tf_op jit(solution)/shard_map/ppermute | solution.py:609
  306.9 42.9 %collective-permute-start.44 = (bf16[2,2,2,2,1,16,1664]{6,5,4,3,2,1,0:T(8,128)(2,1)}, bf16[2,2,2,2,1,16,1664]{6,5,4,3,2,1,0:T(8,128)(2,1)S(1)}, u32[]{:S(2)}, u32[]{:S(2)}) collective-permute-start(bf16[2,2,2,2,1,16,1664]{6,5,4,3,2,1,0:T(8,128)(2,1)} %bitcast.184), channel_id=1, source_target_pairs={{0,1},{1,0},{2,3},{3,2},{4,5},{5,4},{6,7},{7,6},{8,9},{9,8},{10,11... | collective-permute-start | bytes 2555912 | tf_op jit(solution)/shard_map/ppermute | solution.py:609
  311.1 19.4 %collective-permute-start.24 = (bf16[144,512]{1,0:T(8,128)(2,1)S(1)}, bf16[144,512]{1,0:T(8,128)(2,1)S(1)}, u32[]{:S(2)}, u32[]{:S(2)}) collective-permute-start(bf16[144,512]{1,0:T(8,128)(2,1)S(1)} %copy-done.8), channel_id=1, source_target_pairs={{0,8},{4,12},{8,0},{12,4},{16,24},{20,28},{24,16},{28,20},{1,9},{5... | collective-permute-start | bytes 442376 | tf_op jit(solution)/shard_map/ppermute | solution.py:609
  340.5 32.6 %collective-permute-start.37 = (bf16[144,512]{1,0:T(8,128)(2,1)S(1)}, bf16[144,512]{1,0:T(8,128)(2,1)S(1)}, u32[]{:S(2)}, u32[]{:S(2)}) collective-permute-start(bf16[144,512]{1,0:T(8,128)(2,1)S(1)} %get-tuple-element.143.refs_2_), channel_id=1, source_target_pairs={{0,4},{4,0},{8,12},{12,8},{16,20},{20,16},{24,28},{28,24},{1,5},{5... | collective-permute-start | bytes 442376 | tf_op jit(solution)/shard_map/ppermute | solution.py:609
  345.2 27.8 %collective-permute-start.38 = (bf16[144,512]{1,0:T(8,128)(2,1)S(1)}, bf16[144,512]{1,0:T(8,128)(2,1)S(1)}, u32[]{:S(2)}, u32[]{:S(2)}) collective-permute-start(bf16[144,512]{1,0:T(8,128)(2,1)S(1)} %get-tuple-element.142.refs_3_), channel_id=1, source_target_pairs={{0,8},{4,12},{8,0},{12,4},{16,24},{20,28},{24,16},{28,20},{1,9},{5... | collective-permute-start | bytes 442376 | tf_op jit(solution)/shard_map/ppermute | solution.py:609
  346.1 19.5 %collective-permute-start.41 = (bf16[48,512]{1,0:T(8,128)(2,1)S(1)}, bf16[48,512]{1,0:T(8,128)(2,1)S(1)}, u32[]{:S(2)}, u32[]{:S(2)}) collective-permute-start(bf16[48,512]{1,0:T(8,128)(2,1)S(1)} %get-tuple-element.141.refs_6_), channel_id=1, source_target_pairs={{0,20},{4,16},{8,28},{12,24},{16,4},{20,0},{24,12},{28,8},{1,21},{... | collective-permute-start | bytes 147464 | tf_op jit(solution)/shard_map/ppermute | solution.py:609
  380.5 21.8 %collective-permute-start.49 = (bf16[1,2,1,1,1,16,1664]{6,5,4,3,2,1,0:T(8,128)(2,1)S(1)}, bf16[1,2,1,1,1,16,1664]{6,5,4,3,2,1,0:T(8,128)(2,1)S(1)}, u32[]{:S(2)}, u32[]{:S(2)}) collective-permute-start(bf16[1,2,1,1,1,16,1664]{6,5,4,3,2,1,0:T(8,128)(2,1)S(1)} %dynamic-slice_convert_fusion.11.refs_10_), channel_id=1, source_target_pairs={{0,4},{4,0},{8,12},{12,8},{1,5},{5,1},{9,13},{13,9},{2,6},{6,2},{1... | collective-permute-start | bytes 319496 | tf_op jit(solution)/shard_map/ppermute | solution.py:609
  401.7 19.4 %collective-permute-start.47 = (bf16[2,2,2,2,1,16,2560]{6,5,4,3,2,1,0:T(8,128)(2,1)}, bf16[2,2,2,2,1,16,2560]{6,5,4,3,2,1,0:T(8,128)(2,1)S(1)}, u32[]{:S(2)}, u32[]{:S(2)}) collective-permute-start(bf16[2,2,2,2,1,16,2560]{6,5,4,3,2,1,0:T(8,128)(2,1)} %bitcast.180), channel_id=1, source_target_pairs={{0,1},{1,0},{2,3},{3,2},{4,5},{5,4},{6,7},{7,6},{8,9},{9,8},{10,11... | collective-permute-start | bytes 3932168 | tf_op jit(solution)/shard_map/ppermute | solution.py:609
  422.1 33.3 %collective-permute-start.50 = (bf16[1,2,2,2,1,16,2560]{6,5,4,3,2,1,0:T(8,128)(2,1)S(1)}, bf16[1,2,2,2,1,16,2560]{6,5,4,3,2,1,0:T(8,128)(2,1)S(1)}, u32[]{:S(2)}, u32[]{:S(2)}) collective-permute-start(bf16[1,2,2,2,1,16,2560]{6,5,4,3,2,1,0:T(8,128)(2,1)S(1)} %dynamic-slice_convert_fusion.refs_11_), channel_id=1, source_target_pairs={{0,16},{16,0},{1,17},{17,1},{2,18},{18,2},{3,19},{19,3},{4,20},{20... | collective-permute-start | bytes 1966088 | tf_op jit(solution)/shard_map/ppermute | solution.py:609
  470.6 22.4 %collective-permute-start.63 = (bf16[1,1,1,1,1,64,512]{6,5,4,3,2,1,0:T(8,128)(2,1)}, bf16[1,1,1,1,1,64,512]{6,5,4,3,2,1,0:T(8,128)(2,1)}, u32[]{:S(2)}, u32[]{:S(2)}) collective-permute-start(bf16[1,1,1,1,1,64,512]{6,5,4,3,2,1,0:T(8,128)(2,1)} %dynamic-slice_convert_fusion.13.refs_3_), channel_id=1, source_target_pairs={{0,8},{4,12},{8,0},{12,4},{1,9},{5,13},{9,1},{13,5},{2,10},{6,14},... | collective-permute-start | bytes 196616 | tf_op jit(solution)/shard_map/ppermute | solution.py:609
  (129 other events, 1151.4 us)
Sparse Core Ops, SparseCore 0:
  17.7 80.7 all-gather.1
  349.9 111.1 reduce-scatter.1

commit v3 on v2

--- a/solution.py
+++ b/solution.py
@@ -16,6 +16,8 @@
 
 
 masked_score = -1000000000.0
+TM, SPACE, CLIP = "tm", "space", "clip"
+ALL = (TM, SPACE, CLIP)
 
 
 def partner(value, axis, bit):
@@ -73,7 +75,7 @@
 
 
 def region_match(frames):
-    quadrant = lax.axis_index("space")
+    quadrant = lax.axis_index(SPACE)
     row_quad = quadrant // 2
     col_quad = quadrant % 2
     local = jnp.arange(WIN_HW, dtype=jnp.int32)
@@ -89,52 +91,20 @@
     side = field.shape[2]
     reach = side // 2
     sent_rows = field[:, :, :reach] if onward else field[:, :, side - reach :]
-    came_rows = partner(sent_rows, "space", 1)
+    came_rows = partner(sent_rows, SPACE, 1)
     if onward:
         rows_done = jnp.concatenate([field, came_rows], axis=2)[:, :, reach : reach + side]
     else:
         rows_done = jnp.concatenate([came_rows, field], axis=2)[:, :, :side]
     sent_cols = rows_done[:, :, :, :reach] if onward else rows_done[:, :, :, side - reach :]
-    came_cols = partner(sent_cols, "space", 0)
+    came_cols = partner(sent_cols, SPACE, 0)
     if onward:
         return jnp.concatenate([rows_done, came_cols], axis=3)[:, :, :, reach : reach + side]
     return jnp.concatenate([came_cols, rows_done], axis=3)[:, :, :, :side]
 
 
 def gather_layer(shards, layer):
-    parts = tuple((w[layer] for w in shards))
-    return (
-        lax.all_gather(parts[0], ("tm", "space", "clip"), axis=0, tiled=True),
-        lax.all_gather(parts[1], ("tm", "space", "clip"), axis=0, tiled=True),
-        lax.all_gather(parts[2], ("tm", "space", "clip"), axis=0, tiled=True),
-        lax.all_gather(parts[3], ("tm", "space", "clip"), axis=0, tiled=True),
-        lax.all_gather(parts[4], ("tm", "space", "clip"), axis=0, tiled=True),
-        lax.all_gather(parts[5], ("tm", "space", "clip"), axis=0, tiled=True),
-        lax.all_gather(parts[6], ("tm", "space", "clip"), axis=0, tiled=True),
-        lax.all_gather(parts[7], ("tm", "space", "clip"), axis=0, tiled=True),
-        lax.all_gather(parts[8], ("tm", "space", "clip"), axis=0, tiled=True),
-        lax.all_gather(parts[9], ("tm", "space", "clip"), axis=0, tiled=True),
-        lax.all_gather(parts[10], ("tm", "space", "clip"), axis=0, tiled=True),
-        lax.all_gather(parts[11], ("tm", "space", "clip"), axis=0, tiled=True),
-    )
-
-
-def gather_again(shards, layer):
-    parts = tuple((w[layer] for w in shards))
-    return (
-        lax.all_gather(parts[0], ("tm", "space", "clip"), axis=0, tiled=True),
-        lax.all_gather(parts[1], ("tm", "space", "clip"), axis=0, tiled=True),
-        lax.all_gather(parts[2], ("tm", "space", "clip"), axis=0, tiled=True),
-        lax.all_gather(parts[3], ("tm", "space", "clip"), axis=0, tiled=True),
-        lax.all_gather(parts[4], ("tm", "space", "clip"), axis=0, tiled=True),
-        lax.all_gather(parts[5], ("tm", "space", "clip"), axis=0, tiled=True),
-        lax.all_gather(parts[6], ("tm", "space", "clip"), axis=0, tiled=True),
-        lax.all_gather(parts[7], ("tm", "space", "clip"), axis=0, tiled=True),
-        lax.all_gather(parts[8], ("tm", "space", "clip"), axis=0, tiled=True),
-        lax.all_gather(parts[9], ("tm", "space", "clip"), axis=0, tiled=True),
-        lax.all_gather(parts[10], ("tm", "space", "clip"), axis=0, tiled=True),
-        lax.all_gather(parts[11], ("tm", "space", "clip"), axis=0, tiled=True),
-    )
+    return tuple(lax.all_gather(w[layer], ALL, axis=0, tiled=True) for w in shards)
 
 
 def table_bias(table):
@@ -193,9 +163,9 @@
     keys = mixed[..., width : 2 * width].astype(jnp.bfloat16).reshape(head_shape)
     values = (mixed[..., 2 * width :] + mix_bias32[width:]).astype(jnp.bfloat16).reshape(head_shape)
     queries, keys, values = (
-        lax.all_to_all(queries, "tm", split_axis=3, concat_axis=1, tiled=True),
-        lax.all_to_all(keys, "tm", split_axis=3, concat_axis=1, tiled=True),
-        lax.all_to_all(values, "tm", split_axis=3, concat_axis=1, tiled=True),
+        lax.all_to_all(queries, TM, split_axis=3, concat_axis=1, tiled=True),
+        lax.all_to_all(keys, TM, split_axis=3, concat_axis=1, tiled=True),
+        lax.all_to_all(values, TM, split_axis=3, concat_axis=1, tiled=True),
     )
     frames = queries.shape[1]
     if shifted:
@@ -222,7 +192,7 @@
     attended_heads = to_frames(attended_heads, frames)
     if shifted:
         attended_heads = jnp.roll(attended_heads, WIN_T // 2, axis=1)
-    attended = lax.all_to_all(attended_heads, "tm", split_axis=1, concat_axis=3, tiled=True)
+    attended = lax.all_to_all(attended_heads, TM, split_axis=1, concat_axis=3, tiled=True)
     attended = attended.reshape(clips, frames_here, side, side, width)
     if shifted:
         attended = space_roll(attended, False)
@@ -303,7 +273,7 @@
     if shifted:
         grad_attended = space_roll(grad_attended, True)
     grad_attended = grad_attended.reshape(clips, frames_here, side * side, HEADS, head_size)
-    grad_attended = lax.all_to_all(grad_attended, "tm", split_axis=3, concat_axis=1, tiled=True)
+    grad_attended = lax.all_to_all(grad_attended, TM, split_axis=3, concat_axis=1, tiled=True)
     if shifted:
         grad_attended = jnp.roll(grad_attended, -(WIN_T // 2), axis=1)
     grad_attended = to_windows(grad_attended)
@@ -351,9 +321,9 @@
         grad_k = jnp.roll(grad_k, WIN_T // 2, axis=1)
         grad_v = jnp.roll(grad_v, WIN_T // 2, axis=1)
     grad_q, grad_k, grad_v = (
-        lax.all_to_all(grad_q, "tm", split_axis=1, concat_axis=3, tiled=True),
-        lax.all_to_all(grad_k, "tm", split_axis=1, concat_axis=3, tiled=True),
-        lax.all_to_all(grad_v, "tm", split_axis=1, concat_axis=3, tiled=True),
+        lax.all_to_all(grad_q, TM, split_axis=1, concat_axis=3, tiled=True),
+        lax.all_to_all(grad_k, TM, split_axis=1, concat_axis=3, tiled=True),
+        lax.all_to_all(grad_v, TM, split_axis=1, concat_axis=3, tiled=True),
     )
     token_shape = (clips, frames_here, side, side, width)
     grad_q, grad_k, grad_v = (
@@ -439,51 +409,16 @@
     layer_shares = [None] * LAYERS
     table_parts = [None] * LAYERS
     for layer in reversed(range(LAYERS)):
-        params = gather_again(shards, layer)
+        params = gather_layer(shards, layer)
         grad_stream, weight_grads, table_grad = layer_backward(
             grad_stream, params, pos_table[layer], kept_stash[layer], layer % 2 == 1
         )
-        layer_shares[layer] = (
-            lax.psum_scatter(
-                weight_grads[0], ("tm", "space", "clip"), scatter_dimension=0, tiled=True
-            ),
-            lax.psum_scatter(
-                weight_grads[1], ("tm", "space", "clip"), scatter_dimension=0, tiled=True
-            ),
-            lax.psum_scatter(
-                weight_grads[2], ("tm", "space", "clip"), scatter_dimension=0, tiled=True
-            ),
-            lax.psum_scatter(
-                weight_grads[3], ("tm", "space", "clip"), scatter_dimension=0, tiled=True
-            ),
-            lax.psum_scatter(
-                weight_grads[4], ("tm", "space", "clip"), scatter_dimension=0, tiled=True
-            ),
-            lax.psum_scatter(
-                weight_grads[5], ("tm", "space", "clip"), scatter_dimension=0, tiled=True
-            ),
-            lax.psum_scatter(
-                weight_grads[6], ("tm", "space", "clip"), scatter_dimension=0, tiled=True
-            ),
-            lax.psum_scatter(
-                weight_grads[7], ("tm", "space", "clip"), scatter_dimension=0, tiled=True
-            ),
-            lax.psum_scatter(
-                weight_grads[8], ("tm", "space", "clip"), scatter_dimension=0, tiled=True
-            ),
-            lax.psum_scatter(
-                weight_grads[9], ("tm", "space", "clip"), scatter_dimension=0, tiled=True
-            ),
-            lax.psum_scatter(
-                weight_grads[10], ("tm", "space", "clip"), scatter_dimension=0, tiled=True
-            ),
-            lax.psum_scatter(
-                weight_grads[11], ("tm", "space", "clip"), scatter_dimension=0, tiled=True
-            ),
+        layer_shares[layer] = tuple(
+            lax.psum_scatter(g, ALL, scatter_dimension=0, tiled=True) for g in weight_grads
         )
         table_parts[layer] = table_grad
     in_grad = grad_stream.astype(jnp.bfloat16).reshape(clips_in.shape)
-    table_total = lax.psum(jnp.stack(table_parts), ("space", "clip"))
+    table_total = lax.psum(jnp.stack(table_parts), (SPACE, CLIP))
     stacked = tuple(
         (jnp.stack([layer_shares[n][slot] for n in range(LAYERS)]) for slot in range(12))
     )
@@ -521,16 +456,33 @@
     return lax.dot_general(left, right, dims, preferred_element_type=F32)
 
 
-def call(kernel, grid, in_specs, out_specs, out_shape, flops, scratch=(), after=()):
-    inputs, waits = len(in_specs), len(after)
+class Order:
+    def __init__(self, waits=()):
+        self.waits = list(waits)
+        self.token = None
+
+
+def call(kernel, grid, in_specs, out_specs, out_shape, flops, scratch=(), after=None):
+    waits = after.waits if after else []
+    inputs = len(in_specs)
+    single = not isinstance(out_shape, list)
+    out_specs = [out_specs] if single else list(out_specs)
+    out_shape = [out_shape] if single else list(out_shape)
+    outputs = len(out_shape)
+    if after:
+        out_specs.append(pl.BlockSpec(memory_space=pltpu.SMEM))
+        out_shape.append(jax.ShapeDtypeStruct((1, 1), F32))
 
     def body(*refs):
-        kernel(*refs[:inputs], *refs[inputs + waits :])
+        ins, outs = refs[:inputs], refs[inputs + len(waits) :]
+        if after:
+            outs[outputs][0, 0] = 0.0
+        kernel(*ins, *outs[:outputs], *outs[len(out_shape) :])
 
     run = pl.pallas_call(
         body,
         grid=grid,
-        in_specs=list(in_specs) + [pl.BlockSpec(memory_space=pl.ANY)] * waits,
+        in_specs=list(in_specs) + [pl.BlockSpec(memory_space=pl.ANY)] * len(waits),
         out_specs=out_specs,
         out_shape=out_shape,
         scratch_shapes=scratch,
@@ -539,7 +491,14 @@
         ),
         compiler_params=pltpu.CompilerParams(vmem_limit_bytes=VMEM_BYTES),
     )
-    return lambda *args: run(*args, *after)
+
+    def result(*args):
+        found = run(*args, *waits)
+        if after:
+            after.token = found[outputs]
+        return found[0] if single else found[:outputs]
+
+    return result
 
 
 def whole_block(shape):
@@ -554,39 +513,48 @@
     return pl.BlockSpec((1, TOKENS, width), lambda w: (w, 0, column))
 
 
-def halo_plan(frames_here):
-    half_t, reach = WIN_T // 2, WIN_HW // 2
-    frame, row, col = np.meshgrid(
-        np.arange(frames_here), np.arange(WIN_HW), np.arange(WIN_HW), indexing="ij"
-    )
-    frame, row, col = frame.reshape(-1), row.reshape(-1), col.reshape(-1)
-    new_t = (frame - half_t) % frames_here
-    new_r = (row - reach) % WIN_HW
-    new_c = (col - reach) % WIN_HW
-    target = new_t * CELLS + new_r * WIN_HW + new_c
-    leaves = (frame < half_t) * 4 + (row < reach) * 2 + (col < reach) * 1
-    parts = []
-    for kind in range(1, 8):
-        source = np.nonzero(leaves == kind)[0]
-        parts.append((kind, source, target[source]))
-    stay = np.nonzero(leaves == 0)[0]
-    return parts, (stay, target[stay])
-
-
-def halo_matrices(frames_here):
-    parts, (stay, stay_to) = halo_plan(frames_here)
-    count = frames_here * CELLS
-    rows = [-(-len(source) // 16) * 16 for _, source, _ in parts]
-    starts = np.concatenate([[0], np.cumsum(rows)])
-    send = np.zeros((starts[-1], count), np.float32)
-    place = np.zeros((count, starts[-1]), np.float32)
-    own = np.zeros((count, count), np.float32)
-    for (_, source, to), start in zip(parts, starts[:-1]):
-        slots = start + np.arange(len(source))
-        send[slots, source] = 1
-        place[to, slots] = 1
-    own[stay_to, stay] = 1
-    return send, place, own, rows, starts, [kind for kind, _, _ in parts]
+HALF = WIN_T // 2 * CELLS
+KINDS = range(1, 8)
+
+
+class Halo:
+    def __init__(self):
+        token = np.arange(HALF)
+        row, col = token // WIN_HW % WIN_HW, token % WIN_HW
+        reach = WIN_HW // 2
+        target = token - row * WIN_HW - col
+        target = target + (row - reach) % WIN_HW * WIN_HW + (col - reach) % WIN_HW
+        leaves = (row < reach) * 2 + (col < reach) * 1
+        self.stay = np.zeros((HALF, HALF), np.float32)
+        stays = leaves == 0
+        self.stay[target[stays], token[stays]] = 1
+        self.near, self.near_to = self.ways(leaves, target, (1, 2, 3))
+        self.far, self.far_to = self.ways(leaves, target, (0, 1, 2, 3))
+
+    @staticmethod
+    def ways(leaves, target, kinds):
+        send, place = [], []
+        for kind in kinds:
+            source = np.nonzero(leaves == kind)[0]
+            rows = 64 if kind == 0 else 48
+            out, back = np.zeros((rows, HALF), np.float32), np.zeros((HALF, rows), np.float32)
+            out[np.arange(len(source)), source] = 1
+            back[target[source], np.arange(len(source))] = 1
+            send.append(out)
+            place.append(back)
+        return np.concatenate(send, 0), np.concatenate(place, 1)
+
+    def sends(self, onward):
+        return (self.near, self.far) if onward else (self.near_to.T, self.far_to.T)
+
+    def places(self, onward):
+        if onward:
+            return self.stay, self.near_to, self.far_to
+        return self.stay.T, self.near.T, self.far.T
+
+
+def half_at(half):
+    return half // 2, slice(half % 2 * HALF, (half % 2 + 1) * HALF)
 
 
 class Flow:
@@ -600,22 +568,22 @@
     def pending(self):
         return [value for _, _, sends in self.live for value, _, _ in sends]
 
-    def step(self, *names):
+    def step(self, token, names=None):
         live = []
         for name, task, sends in self.live:
-            if names and name not in names:
+            if names is not None and name not in names:
                 live.append((name, task, sends))
                 continue
             came = [lax.ppermute(value, axis, pairs) for value, axis, pairs in sends]
             try:
-                live.append((name, task, task.send(came)))
+                live.append((name, task, task.send((came, token))))
             except StopIteration as end:
                 self.done[name] = end.value
         self.live = live
 
     def finish(self, name):
         while name not in self.done:
-            self.step(name)
+            self.step(None, (name,))
         return self.done[name]
 
 
@@ -623,83 +591,103 @@
     return [(source, source ^ 2**bit) for source in range(lax.axis_size(axis))]
 
 
-def halo_flow(packed, rows, starts, kinds, onward):
-    ring, quads = lax.axis_size("tm"), lax.axis_size("space")
+def halo_flow(packed, onward):
+    ring, quads = lax.axis_size(TM), lax.axis_size(SPACE)
     sends = []
-    for kind, start, count in zip(kinds, starts, rows):
+    for kind, piece in zip(KINDS, packed):
         step = 0 if not kind & 4 else (-1 if onward else 1)
         pairs = []
         for frame_at in range(ring):
             for quad in range(quads):
                 to = (frame_at + step) % ring * quads + (quad ^ (kind & 3))
                 pairs.append((frame_at * quads + quad, to))
-        sends.append((packed[start : start + count], ("tm", "space"), pairs))
-    return (yield sends)
-
-
-def pack_kernel(center, send_ref, x_ref, out_ref):
-    windows = x_ref.shape[0]
-    total = None
-    for w in range(windows):
-        x = x_ref[w]
+        sends.append((piece, (TM, SPACE), pairs))
+    came, _ = yield sends
+    return came
+
+
+def pack_kernel(center, onward, near_ref, far_ref, x_ref, *refs):
+    out_refs, flat_ref = refs[:-1], refs[-1]
+    halves = 2 * x_ref.shape[0]
+    for w in range(x_ref.shape[0]):
+        x = x_ref[w].astype(F32)
         if center:
             x = x - jnp.mean(x, axis=-1, keepdims=True)
-        part = mm(send_ref[:, w * TOKENS : (w + 1) * TOKENS], x.astype(BF16))
-        total = part if total is None else total + part
-    out_ref[...] = total.astype(BF16)
-
-
-def halo_pack(x, send, center, after=()):
+        flat_ref[w] = x
+    for n in range(halves - 1):
+        w, rows = half_at(n + 1 if onward else n)
+        sent = mm(near_ref[...], flat_ref[w, rows].astype(BF16)).astype(BF16)
+        for kind in range(3):
+            out_refs[kind][n * 48 : (n + 1) * 48] = sent[kind * 48 : (kind + 1) * 48]
+    w, rows = half_at(0 if onward else halves - 1)
+    sent = mm(far_ref[...], flat_ref[w, rows].astype(BF16)).astype(BF16)
+    for kind in range(4):
+        first = 0 if kind == 0 else 16 + 48 * kind
+        out_refs[3 + kind][...] = sent[first : first + out_refs[3 + kind].shape[0]]
+
+
+def halo_pack(x, halo, onward, center=False, after=None):
     windows, _, width = x.shape
-    rows = send.shape[0]
+    near, far = (jnp.asarray(m, BF16) for m in halo.sends(onward))
+    rows = [48 * (2 * windows - 1)] * 3 + [64, 48, 48, 48]
     return functools.partial(call, after=after)(
-        functools.partial(pack_kernel, center),
-        (),
-        [pl.BlockSpec(memory_space=pltpu.VMEM)] * 2,
-        pl.BlockSpec(memory_space=pltpu.VMEM),
-        jax.ShapeDtypeStruct((rows, width), BF16),
-        2 * rows * windows * TOKENS * width,
-    )(jnp.asarray(send, BF16), x)
-
-
-def unpack_kernel(center, add_mean, starts, own_ref, place_ref, x_ref, base_ref, *refs):
-    came_refs, out_ref = refs[:-1], refs[-1]
+        functools.partial(pack_kernel, center, onward),
+        (1,),
+        [whole_block(m.shape) for m in (near, far, x)],
+        [whole_block((n, width)) for n in rows],
+        [jax.ShapeDtypeStruct((n, width), BF16) for n in rows],
+        2 * 640 * HALF * width,
+        [pltpu.VMEM(x.shape, F32)],
+    )(near, far, x)
+
+
+def unpack_kernel(center, onward, add_mean, stay_ref, near_ref, far_ref, x_ref, *refs):
+    base_ref, refs = (refs[0], refs[1:]) if add_mean else (None, refs)
+    came_refs, (out_ref, flat_ref, total_ref) = refs[:7], refs[7:]
     windows = x_ref.shape[0]
-    total = jnp.zeros((windows * TOKENS, x_ref.shape[-1]), F32)
+    halves = 2 * windows
     for w in range(windows):
         x = x_ref[w].astype(F32)
         if center:
             x = x - jnp.mean(x, axis=-1, keepdims=True)
+        flat_ref[w] = x
+    for n in range(halves - 1):
+        w, rows = half_at(n + 1 if onward else n)
+        x = flat_ref[w, rows]
         high = x.astype(BF16)
-        cols = own_ref[:, w * TOKENS : (w + 1) * TOKENS]
-        total = total + mm(cols, high)
+        total = mm(stay_ref[...], high)
         if x_ref.dtype == F32:
-            total = total + mm(cols, (x - high.astype(F32)).astype(BF16))
-    came = jnp.concatenate([r[...] for r in came_refs], axis=0)
-    total = total + mm(place_ref[...], came)
+            total = total + mm(stay_ref[...], (x - high.astype(F32)).astype(BF16))
+        came = jnp.concatenate([ref[n * 48 : (n + 1) * 48] for ref in came_refs[:3]], axis=0)
+        w, rows = half_at(n if onward else n + 1)
+        total_ref[w, rows] = total + mm(near_ref[...], came)
+    came = jnp.concatenate([ref[...] for ref in came_refs[3:]], axis=0)
+    w, rows = half_at(halves - 1 if onward else 0)
+    total_ref[w, rows] = mm(far_ref[...], came)
     for w in range(windows):
-        piece = total[w * TOKENS : (w + 1) * TOKENS]
+        total = total_ref[w]
         if add_mean:
-            piece = piece + jnp.mean(base_ref[w], axis=-1, keepdims=True)
-        out_ref[w] = piece.astype(out_ref.dtype)
-
-
-def halo_unpack(x, came, own, place, starts, dtype, center=False, mean_of=None, after=()):
-    windows, _, width = x.shape
-    base = jnp.zeros((windows, 8, 128), F32) if mean_of is None else mean_of
+            total = total + jnp.mean(base_ref[w], axis=-1, keepdims=True)
+        out_ref[w] = total.astype(out_ref.dtype)
+
+
+def halo_unpack(x, came, halo, onward, dtype, center=False, mean_of=None, after=None):
+    places = [jnp.asarray(m, BF16) for m in halo.places(onward)]
+    operands = places + [x] + ([] if mean_of is None else [mean_of]) + list(came)
     return functools.partial(call, after=after)(
-        functools.partial(unpack_kernel, center, mean_of is not None, starts),
-        (),
-        [pl.BlockSpec(memory_space=pltpu.VMEM)] * (4 + len(came)),
-        pl.BlockSpec(memory_space=pltpu.VMEM),
-        jax.ShapeDtypeStruct((windows, TOKENS, width), dtype),
-        4 * (windows * TOKENS) ** 2 * width,
-    )(jnp.asarray(own, BF16), jnp.asarray(place, BF16), x, base, *came)
+        functools.partial(unpack_kernel, center, onward, mean_of is not None),
+        (1,),
+        [whole_block(v.shape) for v in operands],
+        whole_block(x.shape),
+        jax.ShapeDtypeStruct(x.shape, dtype),
+        8 * x.size * HALF,
+        [pltpu.VMEM(x.shape, F32), pltpu.VMEM(x.shape, F32)],
+    )(*operands)
 
 
 def index_bits():
     bits = []
-    for axis in ("tm", "space", "clip"):
+    for axis in ALL:
         count = lax.axis_size(axis).bit_length() - 1
         bits += [(axis, b) for b in reversed(range(count))]
     return bits
@@ -711,10 +699,10 @@
 
 def stage_orders():
     bits = index_bits()
-    inner = [("clip", 0)] if lax.axis_size("clip") > 1 else []
-    tm = [b for b in bits if b[0] == "tm"]
-    clip = [b for b in bits if b[0] == "clip" and b not in inner]
-    space = [b for b in reversed(bits) if b[0] == "space"]
+    inner = [(CLIP, 0)] if lax.axis_size(CLIP) > 1 else []
+    tm = [b for b in bits if b[0] == TM]
+    clip = [b for b in bits if b[0] == CLIP and b not in inner]
+    space = [b for b in reversed(bits) if b[0] == SPACE]
     return inner + tm + clip + space, inner + clip + tm + space
 
 
@@ -723,7 +711,9 @@
     out = shard.reshape((1,) * len(bits) + shard.shape)
     for axis, bit in reversed(order):
         dim = bits.index((axis, bit))
-        (other,) = yield [(out, axis, swap_pairs(axis, bit))]
+        (other,), token = yield [(out, axis, swap_pairs(axis, bit))]
+        if token is not None:
+            other = (other.astype(F32) + token.reshape(())).astype(BF16)
         out = jnp.where(
             bit_of(axis, bit) == 1,
             jnp.concatenate([other, out], dim),
@@ -736,28 +726,33 @@
     bits = index_bits()
     width = own.shape[-1]
     dims = [2] * len(bits)
+    own, sent = own.reshape(-1, width), sent.reshape(-1, width)
     for n, (axis, bit) in enumerate(order):
+        (came,), token = yield [(sent, axis, swap_pairs(axis, bit))]
+        dims[bits.index((axis, bit))] = 1
+        zero = 0.0 if token is None else token.reshape(())
+        if n + 1 == len(order):
+            return own + came.astype(F32)
+        axis, bit = order[n + 1]
         dim = bits.index((axis, bit))
-        if n == 0:
-            dims[dim] = 1
-            own, sent = (v.reshape(dims + [-1, width]) for v in (own, sent))
-        else:
-            here = bit_of(axis, bit)
-            own = lax.dynamic_slice_in_dim(out, here, 1, dim)
-            sent = lax.dynamic_slice_in_dim(out, 1 - here, 1, dim).astype(BF16)
-        (came,) = yield [(sent, axis, swap_pairs(axis, bit))]
-        out = own + came.astype(F32)
-    return out.reshape(-1, width)
+        here = bit_of(axis, bit)
+        own, came = (v.reshape(dims + [-1, width]) for v in (own, came))
+
+        def half(index):
+            mine, theirs = (lax.dynamic_slice_in_dim(v, index, 1, dim) for v in (own, came))
+            return (mine + theirs.astype(F32) + zero).reshape(-1, width)
+
+        own, sent = half(here), half(1 - here).astype(BF16)
 
 
 def table_flow(tables, heads_here):
-    first = lax.axis_index("tm") == 0
+    first = lax.axis_index(TM) == 0
     mine = jnp.where(first, tables[0], tables[1])
-    (came,) = yield [(jnp.where(first, tables[1], tables[0]), "tm", swap_pairs("tm", 0))]
+    (came,), _ = yield [(jnp.where(first, tables[1], tables[0]), TM, swap_pairs(TM, 0))]
     table = mine + came
     for axis, bit in index_bits():
-        if axis != "tm":
-            (came,) = yield [(table, axis, swap_pairs(axis, bit))]
+        if axis != TM:
+            (came,), _ = yield [(table, axis, swap_pairs(axis, bit))]
             table = table + came
     return table
 
@@ -808,7 +803,7 @@
         out_ref[0, key_frame * CELLS : (key_frame + 1) * CELLS, :] = turned[:, :TOKENS]
 
 
-def table_to_bias(tables, after=()):
+def table_to_bias(tables, after=None):
     heads = tables.shape[0]
     slabs = tables.reshape(heads, STEPS, SPAN * SPAN)
     slabs = jnp.pad(slabs, ((0, 0), (0, 16 - STEPS), (0, 256 - SPAN * SPAN)))
@@ -857,7 +852,7 @@
         out_ref[...] = total
 
 
-def sums_to_table(sums, after=()):
+def sums_to_table(sums, after=None):
     heads = sums.shape[0]
     slabs = functools.partial(call, after=after)(
         table_back_kernel,
@@ -899,7 +894,7 @@
         out_ref[0, :, part * width : (part + 1) * width] = out.astype(BF16)
 
 
-def run_qkv(x, vec, w_qkv, after=()):
+def run_qkv(x, vec, w_qkv, after=None):
     windows, _, width = x.shape
     weight, at = w_qkv
     return functools.partial(call, after=after)(
@@ -965,7 +960,7 @@
     log_ref[0, 0] = jnp.concatenate(logs + logs, axis=0)
 
 
-def run_attend(qkv, bias, flags, shifted, first, after=()):
+def run_attend(qkv, bias, flags, shifted, first, after=None):
     windows, _, width3 = qkv.shape
     width = width3 // 3
     wide = GROUP * (width // HEADS)
@@ -1053,7 +1048,7 @@
         dv_ref[w] = grad_v[w].astype(BF16)
 
 
-def run_attend_back(qkv, grad, attended, bias, flags, log, shifted, first, after=()):
+def run_attend_back(qkv, grad, attended, bias, flags, log, shifted, first, after=None):
     windows, _, width3 = qkv.shape
     width = width3 // 3
     wide = GROUP * (width // HEADS)
@@ -1142,7 +1137,7 @@
     return (wo, w1, down), specs
 
 
-def run_branch(x, attended, vec, weights, out_dtype, after=()):
+def run_branch(x, attended, vec, weights, out_dtype, after=None):
     windows, _, width = x.shape
     wide = 4 * width
     arrays, specs = branch_weights(weights, width, wide)
@@ -1232,7 +1227,7 @@
                 out_ref[:, first : first + width] = piece.astype(BF16)
 
 
-def run_branch_back(grad, middle, attended, hidden, slope, vec, weights, flags, split, after=()):
+def run_branch_back(grad, middle, attended, hidden, slope, vec, weights, flags, split, after=None):
     windows, _, width = middle.shape
     wide = 4 * width
     arrays, specs = branch_weights(weights, width, wide)
@@ -1311,7 +1306,7 @@
         split_out(dw_ref, flag_ref[0], own_ref, sent_ref)
 
 
-def run_qkv_back(grads, x, grad_middle, vec, w_qkv, rest, flags, out_dtype, after=()):
+def run_qkv_back(grads, x, grad_middle, vec, w_qkv, rest, flags, out_dtype, after=None):
     windows, _, width = x.shape
     flat = win_block(width)
     weight, at = w_qkv
@@ -1337,16 +1332,13 @@
     )(flags, *grads, x, grad_middle, vec, weight, weight, weight, rest, *extra)
 
 
-def pack_shards_kernel(
-    gain1_ref, bias1_ref, qkv_ref, qvb_ref, out_ref, outb_ref, gain2_ref, bias2_ref, fc1_ref, fc1b_ref,
-    fc2_ref, fc2b_ref, first_ref, mid_ref, down_ref, later_ref, rows_ref,
-):
-    own, width = out_ref.shape[1:]
-    wide = fc1_ref.shape[2]
+def pack_first_kernel(qkv_ref, *refs):
+    vector_refs, (first_ref, rows_ref) = refs[:-2], refs[-2:]
+    own, width3 = qkv_ref.shape[1:]
     rows_ref[...] = jnp.zeros_like(rows_ref)
     row = 0
     lane = lax.broadcasted_iota(jnp.int32, (1, 128), 1)
-    for ref in (gain1_ref, bias1_ref, qvb_ref, outb_ref, gain2_ref, bias2_ref, fc2b_ref, fc1b_ref):
+    for ref in vector_refs:
         values = ref[...].astype(F32)
         values = jnp.pad(values, ((0, 0), (0, 128 - values.shape[1])))
         for part in range(ref.shape[1] // own):
@@ -1358,33 +1350,55 @@
                 line = jnp.where(here, turned[layer : layer + 1], line)
             rows_ref[row : row + 1, :] = line
             row += 1
-    first_ref[:, : 3 * width] = qkv_ref[0]
-    first_ref[:, 3 * width :] = rows_ref[...].astype(BF16)
+    first_ref[:, :width3] = qkv_ref[0]
+    first_ref[:, width3:] = rows_ref[...].astype(BF16)
+
+
+def pack_first(qkv, *vectors, after=None):
+    own, width3 = qkv.shape[1:]
+    return functools.partial(call, after=after)(
+        pack_first_kernel,
+        (1,),
+        [whole_block((1, own, width3))] + [whole_block(v.shape) for v in vectors],
+        whole_block((own, width3 + 128)),
+        jax.ShapeDtypeStruct((own, width3 + 128), BF16),
+        1e6,
+        [pltpu.VMEM((16, 128), F32)],
+    )(qkv, *vectors)
+
+
+def put_down(fc2_ref, layer, out_ref, first):
+    own, width = 16, fc2_ref.shape[2]
+    for part in range(fc2_ref.shape[1] // own):
+        at = first + part * width
+        out_ref[:, at : at + width] = fc2_ref[layer, part * own : (part + 1) * own, :]
+
+
+def pack_mid_kernel(out_ref, fc1_ref, fc2_ref, mid_ref, down_ref):
+    wide = fc1_ref.shape[2]
     mid_ref[:, :wide] = fc1_ref[0]
     mid_ref[:, wide:] = out_ref[0]
+    put_down(fc2_ref, 0, down_ref, 0)
+
+
+def pack_later_kernel(qkv_ref, out_ref, fc1_ref, fc2_ref, later_ref):
+    width, wide = out_ref.shape[2], fc1_ref.shape[2]
     later_ref[:, :wide] = fc1_ref[1]
+    put_down(fc2_ref, 1, later_ref, wide)
     later_ref[:, 2 * wide : 2 * wide + 3 * width] = qkv_ref[1]
     later_ref[:, 2 * wide + 3 * width :] = out_ref[1]
-    for part in range(wide // width):
-        cols = slice(part * width, (part + 1) * width)
-        rows = slice(part * own, (part + 1) * own)
-        down_ref[:, cols] = fc2_ref[0, rows, :]
-        later_ref[:, wide + part * width : wide + (part + 1) * width] = fc2_ref[1, rows, :]
-
-
-def pack_shards(*shards):
-    own, width = shards[4].shape[1:]
-    wide = shards[8].shape[2]
-    widths = (3 * width + 128, wide + width, wide, 2 * wide + 4 * width)
-    return call(
-        pack_shards_kernel,
+
+
+def pack_weights(kernel, widths, *weights, after=None):
+    own = weights[0].shape[1]
+    return functools.partial(call, after=after)(
+        kernel,
         (1,),
-        [whole_block(s.shape) for s in shards],
+        [whole_block(w.shape) for w in weights],
         [whole_block((own, w)) for w in widths],
         [jax.ShapeDtypeStruct((own, w), BF16) for w in widths],
         1e6,
-        [pltpu.VMEM((16, 128), F32)],
-    )(*shards)
+    )(*weights)
 
 
 def vector_slots():
@@ -1413,7 +1427,7 @@
         out_ref[layer] = mm(pick_ref[...], lines.astype(BF16))
 
 
-def vectors_whole(blocks, after=()):
+def vectors_whole(blocks, after=None):
     count, width = blocks.shape
     extra = [jnp.asarray(a, BF16) for a in vector_slots()]
     return functools.partial(call, after=after)(
@@ -1427,11 +1441,61 @@
     )(blocks, *extra)
 
 
+def finish_kernel(
+    mix0_ref, mix1_ref, mid_ref, two_ref, later_ref, gain1_ref, bias1_ref, qkv_ref, qvb_ref, out_ref,
+    outb_ref, gain2_ref, bias2_ref, fc1_ref, fc1b_ref, fc2_ref, fc2b_ref,
+):
+    width, wide = out_ref.shape[2], fc1_ref.shape[2]
+    own = gain1_ref.shape[1]
+    lane = lax.broadcasted_iota(jnp.int32, (1, 128), 1)
+    for layer, mix_ref in enumerate((mix0_ref, mix1_ref)):
+        qkv_ref[layer] = mix_ref[:, : 3 * width]
+        row = 0
+        for ref in (gain1_ref, bias1_ref, qvb_ref, outb_ref, gain2_ref, bias2_ref, fc2b_ref, fc1b_ref):
+            line = jnp.zeros((1, 128), F32)
+            for part in range(ref.shape[1] // own):
+                piece = mix_ref[row : row + 1, 3 * width : 3 * width + 128]
+                piece = pltpu.roll(piece, part * own, 1) if part else piece
+                line = jnp.where((lane >= part * own) & (lane < (part + 1) * own), piece, line)
+                row += 1
+            ref[layer : layer + 1, :] = line[:, : ref.shape[1]]
+    fc1_ref[0] = mid_ref[:, :wide]
+    out_ref[0] = mid_ref[:, wide:]
+    fc2_ref[0] = two_ref[...]
+    fc1_ref[1] = later_ref[:, :wide].astype(F32)
+    out_ref[1] = later_ref[:, wide : wide + width].astype(F32)
+    for part in range(wide // width):
+        first = wide + width + part * width
+        piece = later_ref[:, first : first + width].astype(F32)
+        fc2_ref[1, part * own : (part + 1) * own, :] = piece
+
+
+def run_finish(mixes, mid, two, later):
+    own, width = 16, two.shape[1]
+    wide = mid.shape[1] - width
+    shapes = [
+        (own,), (own,), (own, 3 * width), (2 * own,), (own, width), (own,),
+        (own,), (own,), (own, wide), (4 * own,), (4 * own, width), (own,),
+    ]
+    operands = [*mixes, mid, two, later]
+    return call(
+        finish_kernel,
+        (1,),
+        [whole_block(v.shape) for v in operands],
+        [whole_block((LAYERS,) + shape) for shape in shapes],
+        [jax.ShapeDtypeStruct((LAYERS,) + shape, F32) for shape in shapes],
+        1e6,
+    )(*operands)
+
+
 def place_flags():
-    quadrant = lax.axis_index("space")
-    last = lax.axis_index("tm") == lax.axis_size("tm") - 1
-    flags = [lax.axis_index("clip") % 2, last, quadrant // 2, quadrant % 2]
+    quadrant = lax.axis_index(SPACE)
+    last = lax.axis_index(TM) == lax.axis_size(TM) - 1
+    flags = [lax.axis_index(CLIP) % 2, last, quadrant // 2, quadrant % 2]
     return jnp.stack([jnp.asarray(f, jnp.int32) for f in flags])
+
+
+FIRST, TABLES, MID, DOWN, ROLL, GRAD, OUT, BACK, D_MID, D_TWO, TABLE, D_QKV = range(12)
 
 
 def local_windows(
@@ -1459,89 +1523,93 @@
     one, two = stage_orders()
     flat = (windows, TOKENS, width)
     flags = place_flags()
-    send, place, stay, rows, starts, kinds = halo_matrices(frames_here)
+    halo = Halo()
     flow = Flow()
 
-    def stepped(run, *args, names=(), **options):
-        out = run(*args, after=flow.pending(), **options)
-        flow.step(*names)
+    def stepped(run, *args, names=None, waits=(), **options):
+        order = Order(flow.pending() + list(waits))
+        out = run(*args, after=order, **options)
+        flow.step(order.token, names)
         return out
 
     def halo_start(name, packed, onward):
-        flow.start(name, halo_flow(packed, rows, starts, kinds, onward))
+        flow.start(name, halo_flow(packed, onward))
 
     def send_table():
-        (came,) = yield [(tables, "tm", swap_pairs("tm", 0))]
-        first = lax.axis_index("tm") == 0
+        (came,), _ = yield [(tables, TM, swap_pairs(TM, 0))]
+        first = lax.axis_index(TM) == 0
         return jnp.where(first, tables, came), jnp.where(first, came, tables)
 
-    shards = (
-        ln1_gain, ln1_bias, qkv_weight, qv_bias, out_weight, out_bias,
-        ln2_gain, ln2_bias, fc1_weight, fc1_bias, fc2_weight, fc2_bias,
-    )
-    first, mid, down, later = pack_shards(*shards)
-    later = lax.all_gather(later, ("tm", "space", "clip"), axis=0, tiled=True)
+    wide = fc1_weight.shape[2]
+    first = pack_first(
+        qkv_weight, ln1_gain, ln1_bias, qv_bias, out_bias, ln2_gain, ln2_bias, fc2_bias, fc1_bias
+    )
+    flow.start(FIRST, gather_flow(first, one))
     tables = pos_table.transpose(0, 2, 1)
-    flow.start("tables", send_table())
-    flow.start("first", gather_flow(first, one))
-    flow.step()
-    tables = flow.finish("tables")
-    flow.start("mid", gather_flow(mid, one))
-    flow.start("down", gather_flow(down, two))
+    flow.start(TABLES, send_table())
+    mid, down = stepped(
+        pack_weights, pack_mid_kernel, (wide + width, wide), out_weight, fc1_weight, fc2_weight
+    )
+    tables = flow.finish(TABLES)
+    flow.start(MID, gather_flow(mid, one))
+    flow.start(DOWN, gather_flow(down, two))
     bias0 = [stepped(table_to_bias, tables[n][0]) for n in range(2)]
-    first = flow.finish("first")
+    (later,) = stepped(
+        pack_weights, pack_later_kernel, (2 * wide + 4 * width,),
+        qkv_weight, out_weight, fc1_weight, fc2_weight, names=(FIRST,),
+    )
+    later = lax.all_gather(later, ALL, axis=0, tiled=True)
+    first = flow.finish(FIRST)
     vec = stepped(vectors_whole, first)
     w_qkv = ((first, 0), (later, 8))
 
     stream0 = clips_in.reshape(flat)
-    qkv0 = stepped(run_qkv, stream0, vec[0], w_qkv[0])
+    qkv0 = stepped(run_qkv, stream0, vec[0], w_qkv[0], names=())
     att0, log0 = [None, None], [None, None]
     for n in range(2):
         att0[n], log0[n] = stepped(run_attend, qkv0, bias0[n], flags, False, n * groups_here)
-    mid = flow.finish("mid")
+    mid = flow.finish(MID)
     weights = (
-        ((mid, 4), (mid, 0), (flow.finish("down"), 0)),
+        ((mid, 4), (mid, 0), (flow.finish(DOWN), 0)),
         ((later, 11), (later, 0), (later, 1)),
     )
     mid0, hid0, slope0, stream1 = stepped(run_branch, stream0, att0, vec[0], weights[0], F32)
-    halo_start("roll", halo_pack(stream1, send, True), True)
+    halo_start(ROLL, halo_pack(stream1, halo, True, center=True), True)
     table1 = jnp.concatenate([tables[0][1], tables[1][1]], axis=0)
     bias1 = [stepped(table_to_bias, table1)]
-    rolled1 = halo_unpack(stream1, flow.finish("roll"), stay, place, starts, F32, center=True)
+    rolled1 = halo_unpack(
+        stream1, flow.finish(ROLL), halo, True, F32, center=True, after=Order(bias1)
+    )
     qkv1 = run_qkv(rolled1, vec[1], w_qkv[1])
     grad_in = out_grad.reshape(flat)
-    halo_start("grad", halo_pack(grad_in, send, False, after=[qkv1]), True)
+    halo_start(GRAD, halo_pack(grad_in, halo, True, after=Order([qkv1])), True)
     att1, log1 = stepped(run_attend, qkv1, bias1[0], flags, True, 0)
-    mid1, hid1, slope1, rolled_out = run_branch(rolled1, [att1], vec[1], weights[1], F32)
-    halo_start("out", halo_pack(rolled_out, place.T, False), False)
-    grad = halo_unpack(grad_in, flow.finish("grad"), stay, place, starts, BF16)
+    mid1, hid1, slope1, rolled_out = stepped(
+        run_branch, rolled1, [att1], vec[1], weights[1], F32, waits=flow.done[GRAD]
+    )
+    halo_start(OUT, halo_pack(rolled_out, halo, False), False)
+    grad = stepped(halo_unpack, grad_in, flow.done[GRAD], halo, True, BF16, names=())
 
     kept = (
         (stream0, qkv0, att0, log0, mid0, hid0, slope0, bias0),
         (rolled1, qkv1, [att1], [log1], mid1, hid1, slope1, bias1),
     )
-    rests, tables = [None] * LAYERS, [None] * LAYERS
+    tables = [None] * LAYERS
     for layer in reversed(range(LAYERS)):
         stream, qkv, att, log, mid, hid, slope, bias = kept[layer]
         grad_mid, grad_att, rest, *halves = stepped(
             run_branch_back, grad, mid, att, hid, slope, vec[layer], weights[layer], flags, layer == 0
         )
         if layer == 0:
-            flow.start("d_mid", scatter_flow(*halves[:2], one))
-            flow.start("d_two", scatter_flow(*halves[2:], two))
+            flow.start(D_MID, scatter_flow(*halves[:2], one))
+            flow.start(D_TWO, scatter_flow(*halves[2:], two))
         else:
-            mid_share1 = lax.psum_scatter(
-                halves[0], ("tm", "space", "clip"), scatter_dimension=0, tiled=True
-            ).astype(F32)
-            clips_out = stepped(
-                halo_unpack, rolled_out, flow.finish("out"), stay.T, send.T, starts, BF16,
-                mean_of=stream1,
-            )
+            mid_share1 = lax.psum_scatter(halves[0], ALL, scatter_dimension=0, tiled=True)
         grads, sums = [], []
         for n in range(len(att)):
             *parts, total = stepped(
                 run_attend_back, qkv, grad_att, att[n], bias[n], flags, log[n],
-                layer == 1, n * groups_here,
+                layer == 1, n * groups_here, waits=flow.done[OUT] if layer else (),
             )
             grads.append(parts)
             sums.append(total)
@@ -1551,46 +1619,34 @@
             F32 if layer else BF16,
         )
         if layer:
-            halo_start("back", halo_pack(grad_stream, place.T, False), False)
-        flow.start(f"d_qkv{layer}", scatter_flow(*halves, one))
+            halo_start(BACK, halo_pack(grad_stream, halo, False), False)
+        flow.start(D_QKV + layer, scatter_flow(*halves, one))
         found = [stepped(sums_to_table, total) for total in sums]
         tables[layer] = jnp.split(found[0], 2) if len(found) == 1 else found
         if layer:
-            grad = halo_unpack(grad_stream, flow.finish("back"), stay.T, send.T, starts, F32)
+            grad = stepped(
+                halo_unpack, grad_stream, flow.finish(BACK), halo, False, F32, names=(),
+                waits=found,
+            )
     in_grad = grad_stream
     pairs = [jnp.stack([tables[layer][n] for layer in range(LAYERS)]) for n in range(2)]
-    flow.start("table", table_flow(pairs, heads_here))
-
+    flow.start(TABLE, table_flow(pairs, heads_here))
+    clips_out = stepped(
+        halo_unpack, rolled_out, flow.done[OUT], halo, False, BF16, mean_of=stream1
+    )
     while flow.live:
-        flow.step()
-    wide = fc1_weight.shape[2]
-    mixes = jnp.stack([flow.done[f"d_qkv{layer}"] for layer in range(LAYERS)])
-    mid_share0, two_share0 = flow.done["d_mid"], flow.done["d_two"]
-    two_share1 = jnp.concatenate(
-        [mid_share1[:, first : first + width] for first in range(wide + width, wide * 2 + width, width)],
-        axis=0,
-    )
-    small = mixes[:, :, 3 * width : 3 * width + own]
-
-    def vector(row, count=1):
-        return small[:, row : row + count].reshape(LAYERS, count * own)
-
+        flow.step(None)
+    grads = run_finish(
+        [flow.done[D_QKV + layer] for layer in range(LAYERS)],
+        flow.done[D_MID],
+        flow.done[D_TWO],
+        mid_share1,
+    )
     return (
         clips_out.reshape(clips_in.shape),
         in_grad.reshape(clips_in.shape),
-        vector(0),
-        vector(1),
-        mixes[:, :, : 3 * width],
-        vector(2, 2),
-        jnp.stack([s[:, wide : wide + width] for s in (mid_share0, mid_share1)]),
-        vector(4),
-        vector(5),
-        vector(6),
-        jnp.stack([s[:, :wide] for s in (mid_share0, mid_share1)]),
-        vector(8, 4),
-        jnp.stack([two_share0, two_share1]),
-        vector(7),
-        flow.done["table"].transpose(0, 2, 1),
+        *grads,
+        flow.done[TABLE].transpose(0, 2, 1),
     )
 
 
@@ -1602,8 +1658,8 @@
             clips == 1
             and frames_here % WIN_T == 0
             and own == 16
-            and mesh.shape["tm"] == 2
-            and mesh.shape["space"] == 4
+            and mesh.shape[TM] == 2
+            and mesh.shape[SPACE] == 4
         )
 
     def program(*args):
@@ -1614,42 +1670,42 @@
 
 def solution(mesh):
     placed = (
-        P("clip", "tm", "space", None, None),
-        P(None, ("tm", "space", "clip")),
-        P(None, ("tm", "space", "clip")),
-        P(None, ("tm", "space", "clip"), None),
-        P(None, ("tm", "space", "clip")),
-        P(None, ("tm", "space", "clip"), None),
-        P(None, ("tm", "space", "clip")),
-        P(None, ("tm", "space", "clip")),
-        P(None, ("tm", "space", "clip")),
-        P(None, ("tm", "space", "clip"), None),
-        P(None, ("tm", "space", "clip")),
-        P(None, ("tm", "space", "clip"), None),
-        P(None, ("tm", "space", "clip")),
-        P(None, None, "tm"),
-        P("clip", "tm", "space", None, None),
+        P(CLIP, TM, SPACE, None, None),
+        P(None, ALL),
+        P(None, ALL),
+        P(None, ALL, None),
+        P(None, ALL),
+        P(None, ALL, None),
+        P(None, ALL),
+        P(None, ALL),
+        P(None, ALL),
+        P(None, ALL, None),
+        P(None, ALL),
+        P(None, ALL, None),
+        P(None, ALL),
+        P(None, None, TM),
+        P(CLIP, TM, SPACE, None, None),
     )
     return jax.shard_map(
         windows_are_local(mesh),
         mesh=mesh,
         in_specs=placed,
         out_specs=(
-            P("clip", "tm", "space", None, None),
-            P("clip", "tm", "space", None, None),
-            P(None, ("tm", "space", "clip")),
-            P(None, ("tm", "space", "clip")),
-            P(None, ("tm", "space", "clip"), None),
-            P(None, ("tm", "space", "clip")),
-            P(None, ("tm", "space", "clip"), None),
-            P(None, ("tm", "space", "clip")),
-            P(None, ("tm", "space", "clip")),
-            P(None, ("tm", "space", "clip")),
-            P(None, ("tm", "space", "clip"), None),
-            P(None, ("tm", "space", "clip")),
-            P(None, ("tm", "space", "clip"), None),
-            P(None, ("tm", "space", "clip")),
-            P(None, None, "tm"),
+            P(CLIP, TM, SPACE, None, None),
+            P(CLIP, TM, SPACE, None, None),
+            P(None, ALL),
+            P(None, ALL),
+            P(None, ALL, None),
+            P(None, ALL),
+            P(None, ALL, None),
+            P(None, ALL),
+            P(None, ALL),
+            P(None, ALL),
+            P(None, ALL, None),
+            P(None, ALL),
+            P(None, ALL, None),
+            P(None, ALL),
+            P(None, None, TM),
         ),
         check_vma=False,
     )

time: 543 us -> 503 us (0.926)
  other arithmetic: 15.9 us -> 61.5 us
  waiting for transfers between devices: 73 us -> 33.9 us
  local copies, waits for them, and re-layouts: 58.1 us -> 24.7 us
  starting transfers between devices: 91.4 us -> 82 us
  Pallas kernels: 284 us -> 277 us
    ppermute x69, waiting for transfers between devices: 72.9 us -> 33.9 us  [step(): came = [lax.ppermute(value, axis, pairs) for value, axis, pairs in sends]]
    convert_element_type x1 -> x22, other arithmetic: 0.93 us -> 24.2 us  [the longest x16 14.1 us: gather_flow(): other = (other.astype(F32) + token.reshape(())).astype(BF16)]
    slice x17 -> x0, local copies, waits for them, and re-layouts: 19.4 us -> none  [the longest x16 18.7 us: halo_flow(): sends.append((packed[start:start + count], ('tm', 'space'), pairs))]
    add x16 -> x14, other arithmetic: 5.42 us -> 16.8 us  [the longest x10 9.6 us: half(): return (mine + theirs.astype(F32) + zero).reshape(-1, width)]
    ppermute x69, starting transfers between devices: 91.3 us -> 81.9 us  [step(): came = [lax.ppermute(value, axis, pairs) for value, axis, pairs in sends]]
    select_n x9 -> x1, local copies, waits for them, and re-layouts: 10.1 us -> 0.88 us  [gather_flow(): jnp.where(bit_of(axis, bit) == 1, jnp.concatenate([other, out], dim), jnp...]
    select_n x16 -> x19, other arithmetic: 2.69 us -> 9.89 us  [gather_flow(): jnp.where(bit_of(axis, bit) == 1, jnp.concatenate([other, out], dim), jnp...]
    pallas_call x30 -> x33, Pallas kernels: 284 us -> 277 us  [result(): found = run(*args, *waits)]
  transfers between devices with their start and end apart: 71 -> 71, of which waited for: 14 -> 12; matrix products, arithmetic and copies ran while one was open for 11% -> 16% of each run, Pallas kernels for 39% -> 43%
where the time goes in v3:
time: 503 us; the launch traced here: 496 us
  Pallas kernels  277 us (55%)
  starting transfers between devices  82 us (16%)
  other arithmetic  61.5 us (12%)
  waiting for transfers between devices  33.9 us (7%)
  local copies, waits for them, and re-layouts  24.7 us (5%)
  between operations  16.1 us (3%)
    pallas_call x33, Pallas kernels, result(): found = run(*args, *waits)  277 us
    ppermute x69, starting transfers between devices, step(): came = [lax.ppermute(value, axis, pairs) for value, axis, pairs in sends]  81.9 us
    ppermute x69, waiting for transfers between devices, step(): came = [lax.ppermute(value, axis, pairs) for value, axis, pairs in sends]  33.9 us
    convert_element_type x16, other arithmetic, gather_flow(): other = (other.astype(F32) + token.reshape(())).astype(BF16)  14.1 us
    unnamed x144, local copies, waits for them, and re-layouts  10.5 us
    convert_element_type x6, other arithmetic, scatter_flow(): own, sent = (half(here), half(1 - here).astype(BF16))  10.1 us
  transfers between devices with their start and end apart: 71, of which 12 were waited for; matrix products, arithmetic and copies ran while one was open for 16% of the time, Pallas kernels for 43%

profile of v3, /device:TPU:0, one launch (start us, length us, event | category | flops | bytes accessed | tf_op | source)
XLA Modules:
  0.0 495.7 jit_solution(3634354187084863405)
XLA Ops:
  26.3 7.7 %shard_map.687 = (f32[8,392,392]{2,1,0:T(8,128)}, f32[1,1]{1,0:T(1,128)}) custom-call(bf16[128,256]{1,0:T(8,128)(2,1)} %bitcast.265, bf16[7,256,128]{2,1,0:T(8,128)(2,1)} %constant.237.clone.refs_1_, bf16[1,2,1,1,1,16,1664]{6,5,4,3,2,1,0:T(8,128)(2,1)} %copy-done.49, bf16[1,1,1,1,1,16,2560]{6,5,4,3,2,1,0:T(8,128)(2,1)} %bitcast.240, ...), custom_call_target="tpu_custom_call" | custom-call | flops 4000000000 | bytes 8388608 | tf_op jit(solution)/shard_map/pallas_call | solution.py:496
  44.3 7.6 %shard_map.688 = (f32[8,392,392]{2,1,0:T(8,128)}, f32[1,1]{1,0:T(1,128)}) custom-call(bf16[128,256]{1,0:T(8,128)(2,1)} %bitcast.264, bf16[7,256,128]{2,1,0:T(8,128)(2,1)} %constant.237.clone.refs_1_, bf16[1,2,2,1,1,16,1664]{6,5,4,3,2,1,0:T(8,128)(2,1)} %fusion.43.refs_2_, bf16[1,2,1,1,1,16,2560]{6,5,4,3,2,1,0:T(8,128)(2,1)} %copy-done.37, ...), custom_call_target="tpu_custom_call" | custom-call | flops 4000000000 | bytes 8388608 | tf_op jit(solution)/shard_map/pallas_call | solution.py:496
  64.0 4.9 collective-permute-done.6
  84.6 4.9 shard_map.691
  89.5 10.3 %shard_map.692 = (bf16[2,392,256]{2,1,0:T(8,128)(2,1)}, f32[2,2,8,392]{3,2,1,0:T(8,128)}, f32[1,1]{1,0:T(1,128)}) custom-call(s32[4]{0:T(128)} %pad_add_fusion.refs_0_, bf16[2,392,1536]{2,1,0:T(8,128)(2,1)} %get-tuple-element.136.refs_1_.refs_2_.refs_3_, bf16[2,392,1536]{2,1,0:T(8,128)(2,1)} %get-tuple-element.136.refs_1_.refs_2_.refs_3_, ...), custom_call_target="tpu_custom_call" | custom-call | flops 5035261952 | bytes 8388608 | tf_op jit(solution)/shard_map/pallas_call | solution.py:496
  104.3 10.5 %shard_map.693 = (bf16[2,392,256]{2,1,0:T(8,128)(2,1)}, f32[2,2,8,392]{3,2,1,0:T(8,128)}, f32[1,1]{1,0:T(1,128)}) custom-call(s32[4]{0:T(128)} %pad_add_fusion.refs_0_, bf16[2,392,1536]{2,1,0:T(8,128)(2,1)} %get-tuple-element.136.refs_1_.refs_2_.refs_3_, bf16[2,392,1536]{2,1,0:T(8,128)(2,1)} %get-tuple-element.136.refs_1_.refs_2_.refs_3_, ...), custom_call_target="tpu_custom_call" | custom-call | flops 5035261952 | bytes 8388608 | tf_op jit(solution)/shard_map/pallas_call | solution.py:496
  122.6 11.8 %shard_map.694 = (f32[2,392,512]{2,1,0:T(8,128)}, bf16[2,392,2048]{2,1,0:T(8,128)(2,1)}, bf16[2,392,2048]{2,1,0:T(8,128)(2,1)}, f32[2,392,512]{2,1,0:T(8,128)}, f32[1,1]{1,0:T(1,128)}) custom-call(bf16[2,392,256]{2,1,0:T(8,128)(2,1)} %get-tuple-element.138.refs_0_.refs_1_.refs_5_, bf16[2,392,256]{2,1,0:T(8,128)(2,1)} %get-tuple-element.141.refs_1_.refs_2_.refs_5_, ...), custom_call_target="tpu_custom_call" | custom-call | flops 3699376128 | bytes 8388608 | tf_op jit(solution)/shard_map/pallas_call | solution.py:496
  144.4 4.5 collective-permute-start.22
  148.9 13.6 %shard_map.696 = (f32[16,392,392]{2,1,0:T(8,128)}, f32[1,1]{1,0:T(1,128)}) custom-call(bf16[256,256]{1,0:T(8,128)(2,1)} %bitcast.254, bf16[7,256,128]{2,1,0:T(8,128)(2,1)} %constant.237.clone.refs_1_, bf16[144,512]{1,0:T(8,128)(2,1)} %get-tuple-element.144.refs_2_, bf16[144,512]{1,0:T(8,128)(2,1)} %get-tuple-element.145.refs_3_, ...), custom_call_target="tpu_custom_call" | custom-call | flops 8000000000 | bytes 8388608 | tf_op jit(solution)/shard_map/pallas_call | solution.py:496
  166.9 5.0 %shard_map.698.refs_3_.refs_1_.refs_2_ = bf16[2,392,1536]{2,1,0:T(8,128)(2,1)} custom-call(f32[2,392,512]{2,1,0:T(8,128)} %get-tuple-element.152.refs_0_.refs_1_.refs_4_, f32[16,512]{1,0:T(8,128)} %get-tuple-element.326.refs_1_.refs_2_.refs_6_, bf16[512,6144]{1,0:T(8,128)(2,1)} %all-gather.2.cloned.1.call-done.refs_2_.refs_3_.refs_4_.refs_5_.refs_7_.refs_8_.refs_9_, ...), custom_call_target="tpu_custom_call" | custom-call | flops 1233125376 | bytes 8388608 | tf_op jit(solution)/shard_map/pallas_call | solution.py:496
  185.5 18.8 %shard_map.700 = (bf16[2,392,512]{2,1,0:T(8,128)(2,1)}, f32[2,4,8,392]{3,2,1,0:T(8,128)}, f32[1,1]{1,0:T(1,128)}) custom-call(s32[4]{0:T(128)} %pad_add_fusion.refs_0_, bf16[2,392,1536]{2,1,0:T(8,128)(2,1)} %shard_map.698.refs_3_.refs_1_.refs_2_, bf16[2,392,1536]{2,1,0:T(8,128)(2,1)} %shard_map.698.refs_3_.refs_1_.refs_2_, ...), custom_call_target="tpu_custom_call" | custom-call | flops 10070523904 | bytes 8388608 | tf_op jit(solution)/shard_map/pallas_call | solution.py:496
  205.1 11.6 %shard_map.701 = (f32[2,392,512]{2,1,0:T(8,128)}, bf16[2,392,2048]{2,1,0:T(8,128)(2,1)}, bf16[2,392,2048]{2,1,0:T(8,128)(2,1)}, f32[2,392,512]{2,1,0:T(8,128)}, f32[1,1]{1,0:T(1,128)}) custom-call(bf16[2,392,512]{2,1,0:T(8,128)(2,1)} %get-tuple-element.161.refs_0_.refs_1_.refs_5_, f32[2,392,512]{2,1,0:T(8,128)} %get-tuple-element.152.refs_0_.refs_1_.refs_4_, ...), custom_call_target="tpu_custom_call" | custom-call | flops 3699376128 | bytes 8388608 | tf_op jit(solution)/shard_map/pallas_call | solution.py:496
  236.9 19.7 %shard_map.704 = (f32[2,392,512]{2,1,0:T(8,128)}, bf16[2,392,512]{2,1,0:T(8,128)(2,1)}, f32[16,512]{1,0:T(8,128)}, bf16[512,4608]{1,0:T(8,128)(2,1)}, f32[1,1]{1,0:T(1,128)}) custom-call(s32[4]{0:T(128)} %pad_add_fusion.refs_0_, bf16[2,392,512]{2,1,0:T(8,128)(2,1)} %get-tuple-element.161.refs_0_.refs_1_.refs_5_, ...), custom_call_target="tpu_custom_call" | custom-call | flops 7398752256 | bytes 8388608 | tf_op jit(solution)/shard_map/pallas_call | solution.py:496
  257.3 27.8 %shard_map.705 = (bf16[2,392,512]{2,1,0:T(8,128)(2,1)}, bf16[2,392,512]{2,1,0:T(8,128)(2,1)}, bf16[2,392,512]{2,1,0:T(8,128)(2,1)}, f32[16,49,768]{2,1,0:T(8,128)}, f32[1,1]{1,0:T(1,128)}) custom-call(s32[4]{0:T(128)} %pad_add_fusion.refs_0_, bf16[2,392,1536]{2,1,0:T(8,128)(2,1)} %shard_map.698.refs_3_.refs_1_.refs_2_, ...), custom_call_target="tpu_custom_call" | custom-call | flops 25176309760 | bytes 8388608 | tf_op jit(solution)/shard_map/pallas_call | solution.py:496
  285.1 10.9 %shard_map.706 = (f32[2,392,512]{2,1,0:T(8,128)}, f32[16,16,1664]{2,1,0:T(8,128)}, bf16[16,16,1664]{2,1,0:T(8,128)(2,1)}, f32[1,1]{1,0:T(1,128)}) custom-call(s32[4]{0:T(128)} %pad_add_fusion.refs_0_, bf16[2,392,512]{2,1,0:T(8,128)(2,1)} %get-tuple-element.176.refs_1_, bf16[2,392,512]{2,1,0:T(8,128)(2,1)} %get-tuple-element.177.refs_2_, ...), custom_call_target="tpu_custom_call" | custom-call | flops 2466250752 | bytes 8388608 | tf_op jit(solution)/shard_map/pallas_call | solution.py:496
  304.6 11.1 %shard_map.708 = (f32[256,256]{1,0:T(8,128)}, f32[1,1]{1,0:T(1,128)}) custom-call(f32[16,49,768]{2,1,0:T(8,128)} %get-tuple-element.191.refs_0_, bf16[7,256,128]{2,1,0:T(8,128)(2,1)} %constant.237.clone.refs_1_, bf16[144,512]{1,0:T(8,128)(2,1)} %get-tuple-element.182.refs_2_, bf16[144,512]{1,0:T(8,128)(2,1)} %get-tuple-element.183.refs_3_, ...), custom_call_target="tpu_custom_call" | custom-call | flops 4800000000 | bytes 8388608 | tf_op jit(solution)/shard_map/pallas_call | solution.py:496
  337.1 20.2 %shard_map.710 = (f32[2,392,512]{2,1,0:T(8,128)}, bf16[2,392,512]{2,1,0:T(8,128)(2,1)}, f32[16,512]{1,0:T(8,128)}, f32[16,16,2560]{2,1,0:T(8,128)}, bf16[16,16,2...) custom-call(s32[4]{0:T(128)} %pad_add_fusion.refs_0_, ...), custom_call_target="tpu_custom_call" | custom-call | flops 7398752256 | bytes 8388608 | tf_op jit(solution)/shard_map/pallas_call | solution.py:496
  359.3 15.0 %shard_map.711 = (bf16[2,392,256]{2,1,0:T(8,128)(2,1)}, bf16[2,392,256]{2,1,0:T(8,128)(2,1)}, bf16[2,392,256]{2,1,0:T(8,128)(2,1)}, f32[8,49,768]{2,1,0:T(8,128)}, f32[1,1]{1,0:T(1,128)}) custom-call(s32[4]{0:T(128)} %pad_add_fusion.refs_0_, bf16[2,392,1536]{2,1,0:T(8,128)(2,1)} %get-tuple-element.136.refs_1_.refs_2_.refs_3_, ...), custom_call_target="tpu_custom_call" | custom-call | flops 12588154880 | bytes 8388608 | tf_op jit(solution)/shard_map/pallas_call | solution.py:496
  380.4 15.0 %shard_map.712 = (bf16[2,392,256]{2,1,0:T(8,128)(2,1)}, bf16[2,392,256]{2,1,0:T(8,128)(2,1)}, bf16[2,392,256]{2,1,0:T(8,128)(2,1)}, f32[8,49,768]{2,1,0:T(8,128)}, f32[1,1]{1,0:T(1,128)}) custom-call(s32[4]{0:T(128)} %pad_add_fusion.refs_0_, bf16[2,392,1536]{2,1,0:T(8,128)(2,1)} %get-tuple-element.136.refs_1_.refs_2_.refs_3_, ...), custom_call_target="tpu_custom_call" | custom-call | flops 12588154880 | bytes 8388608 | tf_op jit(solution)/shard_map/pallas_call | solution.py:496
  400.5 10.4 %shard_map.713 = (bf16[2,392,512]{2,1,0:T(8,128)(2,1)}, f32[16,16,1664]{2,1,0:T(8,128)}, bf16[16,16,1664]{2,1,0:T(8,128)(2,1)}, f32[1,1]{1,0:T(1,128)}) custom-call(s32[4]{0:T(128)} %pad_add_fusion.refs_0_, bf16[2,392,256]{2,1,0:T(8,128)(2,1)} %get-tuple-element.203.refs_1_, bf16[2,392,256]{2,1,0:T(8,128)(2,1)} %get-tuple-element.208.refs_2_, ...), custom_call_target="tpu_custom_call" | custom-call | flops 2466250752 | bytes 8388608 | tf_op jit(solution)/shard_map/pallas_call | solution.py:496
  415.7 6.1 %shard_map.714 = (f32[128,256]{1,0:T(8,128)}, f32[1,1]{1,0:T(1,128)}) custom-call(f32[8,49,768]{2,1,0:T(8,128)} %get-tuple-element.218.refs_0_, bf16[7,256,128]{2,1,0:T(8,128)(2,1)} %constant.237.clone.refs_1_, bf16[32,2560]{1,0:T(8,128)(2,1)} %bitcast.96.refs_2_, bf16[128,512]{1,0:T(8,128)(2,1)} %bitcast.98.refs_3_, bf16[256,1664]{1,0:T(8,128)(2,1)} %bitcast.273), custom_call_target="tpu_custom_call" | custom-call | flops 2400000000 | bytes 8388608 | tf_op jit(solution)/shard_map/pallas_call | solution.py:496
  433.2 6.1 %shard_map.715 = (f32[128,256]{1,0:T(8,128)}, f32[1,1]{1,0:T(1,128)}) custom-call(f32[8,49,768]{2,1,0:T(8,128)} %get-tuple-element.221.refs_0_, bf16[7,256,128]{2,1,0:T(8,128)(2,1)} %constant.237.clone.refs_1_, bf16[16,2560]{1,0:T(8,128)(2,1)} %fusion.9.refs_2_, bf16[64,512]{1,0:T(8,128)(2,1)} %fusion.10.refs_3_, bf16[128,1664]{1,0:T(8,128)(2,1)} %bitcast.235), custom_call_target="tpu_custom_call" | custom-call | flops 2400000000 | bytes 8388608 | tf_op jit(solution)/shard_map/pallas_call | solution.py:496
  443.4 4.2 collective-permute-done.64
  449.5 6.4 %collective-permute-done.55 = bf16[128,1664]{1,0:T(8,128)(2,1)S(1)} collective-permute-done((bf16[128,1664]{1,0:T(8,128)(2,1)S(1)}, bf16[128,1664]{1,0:T(8,128)(2,1)S(1)}, u32[]{:S(2)}, u32[]{:S(2)}) %collective-permute-start.55) | collective-permute-done | bytes 426016 | tf_op jit(solution)/shard_map/ppermute | solution.py:577
  (404 shorter events, 215.9 us)
Async XLA Ops:
  7.2 159.8 %all-gather.2.cloned.1.call-start = ((), (), s32[]{:S(2)}) async-start(), calls=%async_computation.1 | async-start | bytes 6488064 | tf_op jit(solution)/shard_map/all_gather | solution.py:1561
  16.0 20.7 %collective-permute-start.4 = (bf16[1,1,1,1,1,16,2560]{6,5,4,3,2,1,0:T(8,128)(2,1)}, bf16[1,1,1,1,1,16,2560]{6,5,4,3,2,1,0:T(8,128)(2,1)S(1)}, u32[]{:S(2)}, u32[]{:S(2)}) collective-permute-start(bf16[1,1,1,1,1,16,2560]{6,5,4,3,2,1,0:T(8,128)(2,1)} %bitcast.239), channel_id=1, source_target_pairs={{0,8},{4,12},{8,0},{12,4},{1,9},{5,13},{9,1},{13,5},{2,10},{6,14},... | collective-permute-start | bytes 245768 | tf_op jit(solution)/shard_map/ppermute | solution.py:577
  53.4 25.8 %collective-permute-start.11 = (bf16[1,2,2,1,1,16,2048]{6,5,2,1,4,3,0:T(8,128)(2,1)S(1)}, bf16[1,2,2,1,1,16,2048]{6,5,2,1,4,3,0:T(8,128)(2,1)S(1)}, u32[]{:S(2)}, u32[]{:S(2)}) collective-permute-start(bf16[1,2,2,1,1,16,2048]{6,5,2,1,4,3,0:T(8,128)(2,1)S(1)} %maximum_select_fusion.12), channel_id=1, source_target_pairs={{0,16},{16,0},{1,17},{17,1},{2,18},{18,2},{3,19},{19,3},{4,20},{20... | collective-permute-start | bytes 786440 | tf_op jit(solution)/shard_map/ppermute | solution.py:577
  63.2 423.1 %reduce-scatter.2.cloned.1.call-start = ((), (), s32[]{:S(2)}) async-start(), calls=%async_computation.2 | async-start | bytes 4866048 | tf_op jit(solution)/shard_map/reduce_scatter | solution.py:1607
  77.9 22.9 %collective-permute-start.12 = (bf16[1,2,2,2,1,16,2560]{6,5,2,1,4,3,0:T(8,128)(2,1)S(1)}, bf16[1,2,2,2,1,16,2560]{6,5,2,1,4,3,0:T(8,128)(2,1)S(1)}, u32[]{:S(2)}, u32[]{:S(2)}) collective-permute-start(bf16[1,2,2,2,1,16,2560]{6,5,2,1,4,3,0:T(8,128)(2,1)S(1)} %maximum_select_fusion.6), channel_id=1, source_target_pairs={{0,16},{16,0},{1,17},{17,1},{2,18},{18,2},{3,19},{19,3},{4,20},{20... | collective-permute-start | bytes 1966088 | tf_op jit(solution)/shard_map/ppermute | solution.py:577
  139.3 23.1 %collective-permute-start.16 = (bf16[144,512]{1,0:T(8,128)(2,1)}, bf16[144,512]{1,0:T(8,128)(2,1)S(1)}, u32[]{:S(2)}, u32[]{:S(2)}) collective-permute-start(bf16[144,512]{1,0:T(8,128)(2,1)} %get-tuple-element.144.refs_2_), channel_id=1, source_target_pairs={{0,4},{4,0},{8,12},{12,8},{16,20},{20,16},{24,28},{28,24},{1,5},{5... | collective-permute-start | bytes 442376 | tf_op jit(solution)/shard_map/ppermute | solution.py:577
  140.9 21.5 %collective-permute-start.17 = (bf16[144,512]{1,0:T(8,128)(2,1)}, bf16[144,512]{1,0:T(8,128)(2,1)S(1)}, u32[]{:S(2)}, u32[]{:S(2)}) collective-permute-start(bf16[144,512]{1,0:T(8,128)(2,1)} %get-tuple-element.145.refs_3_), channel_id=1, source_target_pairs={{0,8},{4,12},{8,0},{12,4},{16,24},{20,28},{24,16},{28,20},{1,9},{5... | collective-permute-start | bytes 442376 | tf_op jit(solution)/shard_map/ppermute | solution.py:577
  175.9 28.4 %collective-permute-start.23 = (bf16[144,512]{1,0:T(8,128)(2,1)}, bf16[144,512]{1,0:T(8,128)(2,1)S(1)}, u32[]{:S(2)}, u32[]{:S(2)}) collective-permute-start(bf16[144,512]{1,0:T(8,128)(2,1)} %get-tuple-element.154.refs_7_), channel_id=1, source_target_pairs={{0,4},{4,0},{8,12},{12,8},{16,20},{20,16},{24,28},{28,24},{1,5},{5... | collective-permute-start | bytes 442376 | tf_op jit(solution)/shard_map/ppermute | solution.py:577
  176.4 28.0 %collective-permute-start.24 = (bf16[144,512]{1,0:T(8,128)(2,1)}, bf16[144,512]{1,0:T(8,128)(2,1)S(1)}, u32[]{:S(2)}, u32[]{:S(2)}) collective-permute-start(bf16[144,512]{1,0:T(8,128)(2,1)} %get-tuple-element.155.refs_8_), channel_id=1, source_target_pairs={{0,8},{4,12},{8,0},{12,4},{16,24},{20,28},{24,16},{28,20},{1,9},{5... | collective-permute-start | bytes 442376 | tf_op jit(solution)/shard_map/ppermute | solution.py:577
  180.2 24.2 %collective-permute-start.25 = (bf16[144,512]{1,0:T(8,128)(2,1)}, bf16[144,512]{1,0:T(8,128)(2,1)S(1)}, u32[]{:S(2)}, u32[]{:S(2)}) collective-permute-start(bf16[144,512]{1,0:T(8,128)(2,1)} %get-tuple-element.156.refs_9_), channel_id=1, source_target_pairs={{0,12},{4,8},{8,4},{12,0},{16,28},{20,24},{24,20},{28,16},{1,13},{... | collective-permute-start | bytes 442376 | tf_op jit(solution)/shard_map/ppermute | solution.py:577
  181.5 22.9 %collective-permute-start.26 = (bf16[64,512]{1,0:T(8,128)(2,1)}, bf16[64,512]{1,0:T(8,128)(2,1)S(1)}, u32[]{:S(2)}, u32[]{:S(2)}) collective-permute-start(bf16[64,512]{1,0:T(8,128)(2,1)} %get-tuple-element.157.refs_10_), channel_id=1, source_target_pairs={{0,16},{4,20},{8,24},{12,28},{16,0},{20,4},{24,8},{28,12},{1,17},{... | collective-permute-start | bytes 196616 | tf_op jit(solution)/shard_map/ppermute | solution.py:577
  183.1 21.2 %collective-permute-start.29 = (bf16[48,512]{1,0:T(8,128)(2,1)}, bf16[48,512]{1,0:T(8,128)(2,1)S(1)}, u32[]{:S(2)}, u32[]{:S(2)}) collective-permute-start(bf16[48,512]{1,0:T(8,128)(2,1)} %get-tuple-element.160.refs_13_), channel_id=1, source_target_pairs={{0,28},{4,24},{8,20},{12,16},{16,12},{20,8},{24,4},{28,0},{1,29},{... | collective-permute-start | bytes 147464 | tf_op jit(solution)/shard_map/ppermute | solution.py:577
  219.3 37.3 %collective-permute-start.30 = (bf16[144,512]{1,0:T(8,128)(2,1)}, bf16[144,512]{1,0:T(8,128)(2,1)S(1)}, u32[]{:S(2)}, u32[]{:S(2)}) collective-permute-start(bf16[144,512]{1,0:T(8,128)(2,1)} %get-tuple-element.163.refs_11_.refs_10_), channel_id=1, source_target_pairs={{0,4},{4,0},{8,12},{12,8},{16,20},{20,16},{24,28},{28,24},{1,5},{5... | collective-permute-start | bytes 442376 | tf_op jit(solution)/shard_map/ppermute | solution.py:577
  219.4 37.2 %collective-permute-start.31 = (bf16[144,512]{1,0:T(8,128)(2,1)}, bf16[144,512]{1,0:T(8,128)(2,1)S(1)}, u32[]{:S(2)}, u32[]{:S(2)}) collective-permute-start(bf16[144,512]{1,0:T(8,128)(2,1)} %get-tuple-element.164.refs_12_.refs_11_), channel_id=1, source_target_pairs={{0,8},{4,12},{8,0},{12,4},{16,24},{20,28},{24,16},{28,20},{1,9},{5... | collective-permute-start | bytes 442376 | tf_op jit(solution)/shard_map/ppermute | solution.py:577
  221.2 35.4 %collective-permute-start.32 = (bf16[144,512]{1,0:T(8,128)(2,1)}, bf16[144,512]{1,0:T(8,128)(2,1)S(1)}, u32[]{:S(2)}, u32[]{:S(2)}) collective-permute-start(bf16[144,512]{1,0:T(8,128)(2,1)} %get-tuple-element.165.refs_13_.refs_12_), channel_id=1, source_target_pairs={{0,12},{4,8},{8,4},{12,0},{16,28},{20,24},{24,20},{28,16},{1,13},{... | collective-permute-start | bytes 442376 | tf_op jit(solution)/shard_map/ppermute | solution.py:577
  230.8 25.7 %collective-permute-start.33 = (bf16[64,512]{1,0:T(8,128)(2,1)S(1)}, bf16[64,512]{1,0:T(8,128)(2,1)S(1)}, u32[]{:S(2)}, u32[]{:S(2)}) collective-permute-start(bf16[64,512]{1,0:T(8,128)(2,1)S(1)} %copy-done.29), channel_id=1, source_target_pairs={{0,16},{4,20},{8,24},{12,28},{16,0},{20,4},{24,8},{28,12},{1,17},{... | collective-permute-start | bytes 196616 | tf_op jit(solution)/shard_map/ppermute | solution.py:577
  234.6 22.0 %collective-permute-start.36 = (bf16[48,512]{1,0:T(8,128)(2,1)S(1)}, bf16[48,512]{1,0:T(8,128)(2,1)S(1)}, u32[]{:S(2)}, u32[]{:S(2)}) collective-permute-start(bf16[48,512]{1,0:T(8,128)(2,1)S(1)} %copy-done.36), channel_id=1, source_target_pairs={{0,28},{4,24},{8,20},{12,16},{16,12},{20,8},{24,4},{28,0},{1,29},{... | collective-permute-start | bytes 147464 | tf_op jit(solution)/shard_map/ppermute | solution.py:577
  296.0 27.2 %collective-permute-start.44 = (bf16[256,1664]{1,0:T(8,128)(2,1)}, bf16[256,1664]{1,0:T(8,128)(2,1)S(1)}, u32[]{:S(2)}, u32[]{:S(2)}) collective-permute-start(bf16[256,1664]{1,0:T(8,128)(2,1)} %bitcast.270), channel_id=1, source_target_pairs={{0,1},{1,0},{2,3},{3,2},{4,5},{5,4},{6,7},{7,6},{8,9},{9,8},{10,11... | collective-permute-start | bytes 2555912 | tf_op jit(solution)/shard_map/ppermute | solution.py:577
  298.8 33.4 %collective-permute-start.37 = (bf16[144,512]{1,0:T(8,128)(2,1)}, bf16[144,512]{1,0:T(8,128)(2,1)S(1)}, u32[]{:S(2)}, u32[]{:S(2)}) collective-permute-start(bf16[144,512]{1,0:T(8,128)(2,1)} %get-tuple-element.182.refs_2_), channel_id=1, source_target_pairs={{0,4},{4,0},{8,12},{12,8},{16,20},{20,16},{24,28},{28,24},{1,5},{5... | collective-permute-start | bytes 442376 | tf_op jit(solution)/shard_map/ppermute | solution.py:577
  298.8 33.4 %collective-permute-start.38 = (bf16[144,512]{1,0:T(8,128)(2,1)}, bf16[144,512]{1,0:T(8,128)(2,1)S(1)}, u32[]{:S(2)}, u32[]{:S(2)}) collective-permute-start(bf16[144,512]{1,0:T(8,128)(2,1)} %get-tuple-element.183.refs_3_), channel_id=1, source_target_pairs={{0,8},{4,12},{8,0},{12,4},{16,24},{20,28},{24,16},{28,20},{1,9},{5... | collective-permute-start | bytes 442376 | tf_op jit(solution)/shard_map/ppermute | solution.py:577
  302.4 20.8 %collective-permute-start.42 = (bf16[48,512]{1,0:T(8,128)(2,1)}, bf16[48,512]{1,0:T(8,128)(2,1)S(1)}, u32[]{:S(2)}, u32[]{:S(2)}) collective-permute-start(bf16[48,512]{1,0:T(8,128)(2,1)} %get-tuple-element.187.refs_7_), channel_id=1, source_target_pairs={{0,24},{4,28},{8,16},{12,20},{16,8},{20,12},{24,0},{28,4},{1,25},{... | collective-permute-start | bytes 147464 | tf_op jit(solution)/shard_map/ppermute | solution.py:577
  330.2 27.7 %collective-permute-start.45 = (bf16[128,1664]{1,0:T(8,128)(2,1)S(1)}, bf16[128,1664]{1,0:T(8,128)(2,1)S(1)}, u32[]{:S(2)}, u32[]{:S(2)}) collective-permute-start(bf16[128,1664]{1,0:T(8,128)(2,1)S(1)} %bitcast.208), channel_id=1, source_target_pairs={{0,16},{16,0},{1,17},{17,1},{2,18},{18,2},{3,19},{19,3},{4,20},{20... | collective-permute-start | bytes 1277960 | tf_op jit(solution)/shard_map/ppermute | solution.py:577
  357.4 21.2 %collective-permute-start.47 = (bf16[256,2560]{1,0:T(8,128)(2,1)}, bf16[256,2560]{1,0:T(8,128)(2,1)S(1)}, u32[]{:S(2)}, u32[]{:S(2)}) collective-permute-start(bf16[256,2560]{1,0:T(8,128)(2,1)} %bitcast.266), channel_id=1, source_target_pairs={{0,1},{1,0},{2,3},{3,2},{4,5},{5,4},{6,7},{7,6},{8,9},{9,8},{10,11... | collective-permute-start | bytes 3932168 | tf_op jit(solution)/shard_map/ppermute | solution.py:577
  375.0 20.4 %collective-permute-start.49 = (bf16[32,1664]{1,0:T(8,128)(2,1)S(1)}, bf16[32,1664]{1,0:T(8,128)(2,1)S(1)}, u32[]{:S(2)}, u32[]{:S(2)}) collective-permute-start(bf16[32,1664]{1,0:T(8,128)(2,1)S(1)} %bitcast.261), channel_id=1, source_target_pairs={{0,4},{4,0},{8,12},{12,8},{1,5},{5,1},{9,13},{13,9},{2,6},{6,2},{1... | collective-permute-start | bytes 319496 | tf_op jit(solution)/shard_map/ppermute | solution.py:577
  (116 other events, 1044.9 us)
Sparse Core Ops, SparseCore 0:
  63.3 71.0 all-gather.1
  296.3 106.9 reduce-scatter.1

commit v4 on v3

--- a/solution.py
+++ b/solution.py
@@ -462,7 +462,9 @@
         self.token = None
 
 
-def call(kernel, grid, in_specs, out_specs, out_shape, flops, scratch=(), after=None):
+def call(
+    kernel, grid, in_specs, out_specs, out_shape, flops, scratch=(), after=None, aliases=None
+):
     waits = after.waits if after else []
     inputs = len(in_specs)
     single = not isinstance(out_shape, list)
@@ -486,6 +488,7 @@
         out_specs=out_specs,
         out_shape=out_shape,
         scratch_shapes=scratch,
+        input_output_aliases=aliases or {},
         cost_estimate=pl.CostEstimate(
             flops=int(flops), transcendentals=0, bytes_accessed=8 * 1024 * 1024
         ),
@@ -558,27 +561,37 @@
 
 
 class Flow:
-    def __init__(self):
+    def __init__(self, flags):
+        self.flags = flags
         self.live = []
         self.done = {}
 
     def start(self, name, task):
-        self.live.append((name, task, next(task)))
+        self.live.append((name, task, task.sends() if isinstance(task, Gather) else next(task)))
 
     def pending(self):
         return [value for _, _, sends in self.live for value, _, _ in sends]
 
     def step(self, token, names=None):
-        live = []
+        live, gathers = [], []
         for name, task, sends in self.live:
             if names is not None and name not in names:
                 live.append((name, task, sends))
                 continue
             came = [lax.ppermute(value, axis, pairs) for value, axis, pairs in sends]
+            if isinstance(task, Gather):
+                if len(task.steps) > 1:
+                    gathers.append((name, task, came[0]))
+                else:
+                    self.done[name] = task.last(came[0])
+                continue
             try:
                 live.append((name, task, task.send((came, token))))
             except StopIteration as end:
                 self.done[name] = end.value
+        if gathers:
+            merge([t for _, t, _ in gathers], [c for _, _, c in gathers], self.flags, token)
+        live += [(name, task, task.sends()) for name, task, _ in gathers]
         self.live = live
 
     def finish(self, name):
@@ -626,19 +639,45 @@
         out_refs[3 + kind][...] = sent[first : first + out_refs[3 + kind].shape[0]]
 
 
-def halo_pack(x, halo, onward, center=False, after=None):
+def part_rows(windows):
+    return [48 * (2 * windows - 1)] * 3 + [64, 48, 48, 48]
+
+
+def halo_pack(x, halo, onward, center=False, joined=False, after=None):
     windows, _, width = x.shape
     near, far = (jnp.asarray(m, BF16) for m in halo.sends(onward))
-    rows = [48 * (2 * windows - 1)] * 3 + [64, 48, 48, 48]
-    return functools.partial(call, after=after)(
-        functools.partial(pack_kernel, center, onward),
+    rows = part_rows(windows)
+
+    def kernel(near_ref, far_ref, x_ref, *refs):
+        if joined:
+            refs = [refs[0].at[pl.ds(sum(rows[:n]), rows[n])] for n in range(7)] + [refs[1]]
+        pack_kernel(center, onward, near_ref, far_ref, x_ref, *refs)
+
+    shapes = [(sum(rows), width)] if joined else [(n, width) for n in rows]
+    out = functools.partial(call, after=after)(
+        kernel,
         (1,),
         [whole_block(m.shape) for m in (near, far, x)],
-        [whole_block((n, width)) for n in rows],
-        [jax.ShapeDtypeStruct((n, width), BF16) for n in rows],
+        [whole_block(shape) for shape in shapes],
+        [jax.ShapeDtypeStruct(shape, BF16) for shape in shapes],
         2 * 640 * HALF * width,
         [pltpu.VMEM(x.shape, F32)],
     )(near, far, x)
+    return out[0] if joined else out
+
+
+def halo_gather(packed):
+    return lax.all_gather(packed, (TM, SPACE), axis=0, tiled=True)
+
+
+def halo_senders(onward):
+    ring, quads = lax.axis_size(TM), lax.axis_size(SPACE)
+    senders = []
+    for kind in KINDS:
+        step = 0 if not kind & 4 else (1 if onward else -1)
+        frame_at = (lax.axis_index(TM) + step + ring) % ring
+        senders.append(frame_at * quads + lax.axis_index(SPACE) ^ (kind & 3))
+    return jnp.stack([jnp.asarray(n, jnp.int32) for n in senders])
 
 
 def unpack_kernel(center, onward, add_mean, stay_ref, near_ref, far_ref, x_ref, *refs):
@@ -673,16 +712,32 @@
 
 def halo_unpack(x, came, halo, onward, dtype, center=False, mean_of=None, after=None):
     places = [jnp.asarray(m, BF16) for m in halo.places(onward)]
-    operands = places + [x] + ([] if mean_of is None else [mean_of]) + list(came)
+    operands = places + [x] + ([] if mean_of is None else [mean_of])
+    joined = not isinstance(came, list)
+    senders = [halo_senders(onward)] if joined else []
+    operands += [came] if joined else came
+    rows = part_rows(x.shape[0])
+
+    def kernel(*refs):
+        if joined:
+            sender_ref, refs = refs[0], refs[1:]
+            count = len(operands)
+            parts = []
+            for n in range(7):
+                first = sender_ref[n] * sum(rows) + sum(rows[:n])
+                parts.append(refs[count - 1].at[pl.ds(pl.multiple_of(first, 16), rows[n])])
+            refs = refs[: count - 1] + tuple(parts) + refs[count:]
+        unpack_kernel(center, onward, mean_of is not None, *refs)
+
     return functools.partial(call, after=after)(
-        functools.partial(unpack_kernel, center, onward, mean_of is not None),
+        kernel,
         (1,),
-        [whole_block(v.shape) for v in operands],
+        [flag_spec()] * joined + [whole_block(v.shape) for v in operands],
         whole_block(x.shape),
         jax.ShapeDtypeStruct(x.shape, dtype),
         8 * x.size * HALF,
         [pltpu.VMEM(x.shape, F32), pltpu.VMEM(x.shape, F32)],
-    )(*operands)
+    )(*senders, *operands)
 
 
 def index_bits():
@@ -706,20 +761,57 @@
     return inner + tm + clip + space, inner + clip + tm + space
 
 
-def gather_flow(shard, order):
-    bits = index_bits()
-    out = shard.reshape((1,) * len(bits) + shard.shape)
-    for axis, bit in reversed(order):
-        dim = bits.index((axis, bit))
-        (other,), token = yield [(out, axis, swap_pairs(axis, bit))]
-        if token is not None:
-            other = (other.astype(F32) + token.reshape(())).astype(BF16)
-        out = jnp.where(
-            bit_of(axis, bit) == 1,
-            jnp.concatenate([other, out], dim),
-            jnp.concatenate([out, other], dim),
-        )
-    return out.reshape((-1,) + shard.shape[1:])
+class Gather:
+    def __init__(self, shard, order):
+        self.bits, self.steps = index_bits(), list(reversed(order))
+        self.dims = [1] * len(self.bits)
+        self.rows, self.out = shard.shape[0], shard
+
+    def sends(self):
+        axis, bit = self.steps[0]
+        return [(self.out, axis, swap_pairs(axis, bit))]
+
+    def split(self):
+        dim = self.bits.index(self.steps.pop(0))
+        before, after = math.prod(self.dims[:dim]), math.prod(self.dims[dim + 1 :])
+        self.dims[dim] = 2
+        return before, after * self.rows, 4 + dim
+
+    def last(self, came):
+        here = bit_of(*self.steps[0])
+        before, after, _ = self.split()
+        own, came = (v.reshape(before, 1, after, -1) for v in (self.out, came))
+        pair = [jnp.concatenate(p, axis=1) for p in ((own, came), (came, own))]
+        return jnp.where(here == 1, pair[1], pair[0]).reshape(-1, own.shape[-1])
+
+
+def merge_kernel(places, flag_ref, *refs):
+    for n, place in enumerate(places):
+        own_ref, came_ref, out_ref = refs[2 * n], refs[2 * n + 1], refs[2 * len(places) + n]
+        here = flag_ref[place]
+        out_ref[:, here] = own_ref[...]
+        out_ref[:, 1 - here] = came_ref[...]
+
+
+def merge(tasks, came, flags, token):
+    places, operands, shapes = [], [], []
+    for task, piece in zip(tasks, came):
+        before, after, place = task.split()
+        width = piece.shape[-1]
+        places.append(place)
+        operands += [v.reshape(before, after, width) for v in (task.out, piece)]
+        shapes.append(jax.ShapeDtypeStruct((before, 2, after, width), BF16))
+    found = call(
+        functools.partial(merge_kernel, places),
+        (1,),
+        [flag_spec()] + [whole_block(v.shape) for v in operands],
+        [whole_block(v.shape) for v in shapes],
+        shapes,
+        1e6,
+        after=None if token is None else Order([token]),
+    )(flags, *operands)
+    for task, out in zip(tasks, found):
+        task.out = out.reshape(-1, out.shape[-1])
 
 
 def scatter_flow(own, sent, order):
@@ -803,20 +895,27 @@
         out_ref[0, key_frame * CELLS : (key_frame + 1) * CELLS, :] = turned[:, :TOKENS]
 
 
-def table_to_bias(tables, after=None):
+def table_to_bias(tables, rest=None, after=None):
     heads = tables.shape[0]
     slabs = tables.reshape(heads, STEPS, SPAN * SPAN)
     slabs = jnp.pad(slabs, ((0, 0), (0, 16 - STEPS), (0, 256 - SPAN * SPAN)))
     slabs = slabs.reshape(heads * 16, 256)
-    return functools.partial(call, after=after)(
-        bias_kernel,
+    held = [] if rest is None else [rest]
+    first = 0 if rest is None else heads
+
+    def kernel(slab_ref, pick_ref, *refs):
+        bias_kernel(slab_ref, pick_ref, *refs[len(held) :])
+
+    return functools.partial(call, after=after, aliases={2: 0} if held else {})(
+        kernel,
         (heads,),
-        [whole_block(slabs.shape), whole_block((WIN_HW, 256, 128))],
-        pl.BlockSpec((1, TOKENS, TOKENS), lambda h: (h, 0, 0)),
-        jax.ShapeDtypeStruct((heads, TOKENS, TOKENS), F32),
+        [whole_block(slabs.shape), whole_block((WIN_HW, 256, 128))]
+        + [pl.BlockSpec(memory_space=pl.ANY)] * len(held),
+        pl.BlockSpec((1, TOKENS, TOKENS), lambda h: (first + h, 0, 0)),
+        jax.ShapeDtypeStruct((2 * heads, TOKENS, TOKENS), F32),
         heads * 500_000_000,
         [pltpu.VMEM((heads * 128, 128), F32), pltpu.VMEM((56, WIDE), F32)],
-    )(slabs, jnp.asarray(column_pick(), BF16))
+    )(slabs, jnp.asarray(column_pick(), BF16), *held)
 
 
 def table_back_kernel(sums_ref, pick_ref, out_ref, row_ref):
@@ -960,18 +1059,18 @@
     log_ref[0, 0] = jnp.concatenate(logs + logs, axis=0)
 
 
-def run_attend(qkv, bias, flags, shifted, first, after=None):
+def run_attend(qkv, bias, flags, shifted, after=None):
     windows, _, width3 = qkv.shape
     width = width3 // 3
     wide = GROUP * (width // HEADS)
-    groups, count = HEADS // GROUP, bias.shape[0] // GROUP
+    groups = HEADS // GROUP
     qkv_specs = [
-        pl.BlockSpec((1, TOKENS, wide), lambda g, w, p=part: (w, 0, p * groups + first + g))
+        pl.BlockSpec((1, TOKENS, wide), lambda g, w, p=part: (w, 0, p * groups + g))
         for part in range(3)
     ]
     return functools.partial(call, after=after)(
         functools.partial(attend_kernel, shifted, width // HEADS),
-        (count, windows),
+        (groups, windows),
         [flag_spec()]
         + qkv_specs
         + [
@@ -984,10 +1083,10 @@
             pl.BlockSpec((1, 1, 2 * GROUP, TOKENS), lambda g, w: (w, g, 0, 0)),
         ],
         [
-            jax.ShapeDtypeStruct((windows, TOKENS, count * wide), BF16),
-            jax.ShapeDtypeStruct((windows, count, 2 * GROUP, TOKENS), F32),
+            jax.ShapeDtypeStruct((windows, TOKENS, width), BF16),
+            jax.ShapeDtypeStruct((windows, groups, 2 * GROUP, TOKENS), F32),
         ],
-        64 * windows * TOKENS * TOKENS * count * wide,
+        64 * windows * TOKENS * TOKENS * width,
     )(flags, qkv, qkv, qkv, bias, late_tokens(), late_tokens().T)
 
 
@@ -1048,11 +1147,11 @@
         dv_ref[w] = grad_v[w].astype(BF16)
 
 
-def run_attend_back(qkv, grad, attended, bias, flags, log, shifted, first, after=None):
+def run_attend_back(qkv, grad, attended, bias, flags, log, shifted, first, count, after=None):
     windows, _, width3 = qkv.shape
     width = width3 // 3
     wide = GROUP * (width // HEADS)
-    groups, count = HEADS // GROUP, bias.shape[0] // GROUP
+    groups = HEADS // GROUP
     qkv_specs = [
         pl.BlockSpec((windows, TOKENS, wide), lambda g, p=part: (0, 0, p * groups + first + g))
         for part in range(3)
@@ -1066,11 +1165,11 @@
         + qkv_specs
         + [
             pl.BlockSpec((windows, TOKENS, wide), lambda g: (0, 0, first + g)),
-            flat,
-            pl.BlockSpec((GROUP, TOKENS, TOKENS), lambda g: (g, 0, 0)),
+            pl.BlockSpec((windows, TOKENS, wide), lambda g: (0, 0, first + g)),
+            pl.BlockSpec((GROUP, TOKENS, TOKENS), lambda g: (first + g, 0, 0)),
             whole_block((TOKENS, 8)),
             whole_block((8, TOKENS)),
-            pl.BlockSpec((windows, 1, 2 * GROUP, TOKENS), lambda g: (0, g, 0, 0)),
+            pl.BlockSpec((windows, 1, 2 * GROUP, TOKENS), lambda g: (0, first + g, 0, 0)),
         ],
         [flat, flat, flat, pl.BlockSpec((GROUP, CELLS, WIDE), lambda g: (g, 0, 0))],
         [flat_shape] * 3 + [jax.ShapeDtypeStruct((count * GROUP, CELLS, WIDE), F32)],
@@ -1367,38 +1466,29 @@
     )(qkv, *vectors)
 
 
-def put_down(fc2_ref, layer, out_ref, first):
-    own, width = 16, fc2_ref.shape[2]
-    for part in range(fc2_ref.shape[1] // own):
-        at = first + part * width
-        out_ref[:, at : at + width] = fc2_ref[layer, part * own : (part + 1) * own, :]
-
-
-def pack_mid_kernel(out_ref, fc1_ref, fc2_ref, mid_ref, down_ref):
-    wide = fc1_ref.shape[2]
-    mid_ref[:, :wide] = fc1_ref[0]
-    mid_ref[:, wide:] = out_ref[0]
-    put_down(fc2_ref, 0, down_ref, 0)
-
-
-def pack_later_kernel(qkv_ref, out_ref, fc1_ref, fc2_ref, later_ref):
-    width, wide = out_ref.shape[2], fc1_ref.shape[2]
-    later_ref[:, :wide] = fc1_ref[1]
-    put_down(fc2_ref, 1, later_ref, wide)
-    later_ref[:, 2 * wide : 2 * wide + 3 * width] = qkv_ref[1]
-    later_ref[:, 2 * wide + 3 * width :] = out_ref[1]
-
-
-def pack_weights(kernel, widths, *weights, after=None):
-    own = weights[0].shape[1]
-    return functools.partial(call, after=after)(
-        kernel,
+def pack_branch_kernel(layer, out_ref, fc1_ref, fc2_ref, packed_ref):
+    own, width, wide = fc1_ref.shape[1], fc2_ref.shape[2], fc1_ref.shape[2]
+    packed_ref[:, :wide] = fc1_ref[layer]
+    for part in range(wide // width):
+        first = wide + part * width
+        packed_ref[:, first : first + width] = fc2_ref[layer, part * own : (part + 1) * own, :]
+    packed_ref[:, 2 * wide :] = out_ref[layer]
+
+
+def gather_branch(layer, weights, after=None):
+    own, wide = weights[1].shape[1:]
+    width = weights[0].shape[2]
+    packed = jax.ShapeDtypeStruct((own, 2 * wide + width), BF16)
+    shard = functools.partial(call, after=after)(
+        functools.partial(pack_branch_kernel, layer),
         (1,),
         [whole_block(w.shape) for w in weights],
-        [whole_block((own, w)) for w in widths],
-        [jax.ShapeDtypeStruct((own, w), BF16) for w in widths],
+        whole_block(packed.shape),
+        packed,
         1e6,
     )(*weights)
+    whole = lax.all_gather(shard, ALL, axis=0, tiled=True)
+    return ((whole, 2 * wide // width), (whole, 0), (whole, 1))
 
 
 def vector_slots():
@@ -1492,10 +1582,11 @@
     quadrant = lax.axis_index(SPACE)
     last = lax.axis_index(TM) == lax.axis_size(TM) - 1
     flags = [lax.axis_index(CLIP) % 2, last, quadrant // 2, quadrant % 2]
+    flags += [bit_of(axis, bit) for axis, bit in index_bits()]
     return jnp.stack([jnp.asarray(f, jnp.int32) for f in flags])
 
 
-FIRST, TABLES, MID, DOWN, ROLL, GRAD, OUT, BACK, D_MID, D_TWO, TABLE, D_QKV = range(12)
+FIRST, TABLES, LATER, ROLL, GRAD, BACK, D_MID, D_TWO, TABLE, D_QKV = range(10)
 
 
 def local_windows(
@@ -1519,12 +1610,11 @@
     windows = frames_here // WIN_T
     own = ln1_gain.shape[1]
     heads_here = pos_table.shape[2]
-    groups_here = heads_here // GROUP
     one, two = stage_orders()
     flat = (windows, TOKENS, width)
     flags = place_flags()
     halo = Halo()
-    flow = Flow()
+    flow = Flow(flags)
 
     def stepped(run, *args, names=None, waits=(), **options):
         order = Order(flow.pending() + list(waits))
@@ -1540,65 +1630,52 @@
         first = lax.axis_index(TM) == 0
         return jnp.where(first, tables, came), jnp.where(first, came, tables)
 
-    wide = fc1_weight.shape[2]
+    branch = (out_weight, fc1_weight, fc2_weight)
     first = pack_first(
         qkv_weight, ln1_gain, ln1_bias, qv_bias, out_bias, ln2_gain, ln2_bias, fc2_bias, fc1_bias
     )
-    flow.start(FIRST, gather_flow(first, one))
+    flow.start(FIRST, Gather(first, one))
     tables = pos_table.transpose(0, 2, 1)
     flow.start(TABLES, send_table())
-    mid, down = stepped(
-        pack_weights, pack_mid_kernel, (wide + width, wide), out_weight, fc1_weight, fc2_weight
-    )
+    weights0 = stepped(gather_branch, 0, branch)
     tables = flow.finish(TABLES)
-    flow.start(MID, gather_flow(mid, one))
-    flow.start(DOWN, gather_flow(down, two))
-    bias0 = [stepped(table_to_bias, tables[n][0]) for n in range(2)]
-    (later,) = stepped(
-        pack_weights, pack_later_kernel, (2 * wide + 4 * width,),
-        qkv_weight, out_weight, fc1_weight, fc2_weight, names=(FIRST,),
-    )
-    later = lax.all_gather(later, ALL, axis=0, tiled=True)
+    bias0 = stepped(table_to_bias, tables[0][0])
+    bias0 = stepped(table_to_bias, tables[1][0], bias0)
+    bias1 = stepped(table_to_bias, tables[0][1])
     first = flow.finish(FIRST)
+    flow.start(LATER, Gather(qkv_weight[1], one))
     vec = stepped(vectors_whole, first)
-    w_qkv = ((first, 0), (later, 8))
+    weights1 = gather_branch(1, branch, after=Order([vec]))
 
     stream0 = clips_in.reshape(flat)
-    qkv0 = stepped(run_qkv, stream0, vec[0], w_qkv[0], names=())
-    att0, log0 = [None, None], [None, None]
-    for n in range(2):
-        att0[n], log0[n] = stepped(run_attend, qkv0, bias0[n], flags, False, n * groups_here)
-    mid = flow.finish(MID)
-    weights = (
-        ((mid, 4), (mid, 0), (flow.finish(DOWN), 0)),
-        ((later, 11), (later, 0), (later, 1)),
-    )
-    mid0, hid0, slope0, stream1 = stepped(run_branch, stream0, att0, vec[0], weights[0], F32)
+    qkv0 = stepped(run_qkv, stream0, vec[0], (first, 0))
+    att0, log0 = stepped(run_attend, qkv0, bias0, flags, False)
+    grad_in = out_grad.reshape(flat)
+    mid0, hid0, slope0, stream1 = stepped(run_branch, stream0, [att0], vec[0], weights0, F32)
     halo_start(ROLL, halo_pack(stream1, halo, True, center=True), True)
-    table1 = jnp.concatenate([tables[0][1], tables[1][1]], axis=0)
-    bias1 = [stepped(table_to_bias, table1)]
+    bias1 = stepped(table_to_bias, tables[1][1], bias1)
+    later = flow.finish(LATER)
     rolled1 = halo_unpack(
-        stream1, flow.finish(ROLL), halo, True, F32, center=True, after=Order(bias1)
-    )
-    qkv1 = run_qkv(rolled1, vec[1], w_qkv[1])
-    grad_in = out_grad.reshape(flat)
+        stream1, flow.finish(ROLL), halo, True, F32, center=True, after=Order([bias1])
+    )
+    qkv1 = run_qkv(rolled1, vec[1], (later, 0))
     halo_start(GRAD, halo_pack(grad_in, halo, True, after=Order([qkv1])), True)
-    att1, log1 = stepped(run_attend, qkv1, bias1[0], flags, True, 0)
+    att1, log1 = stepped(run_attend, qkv1, bias1, flags, True)
     mid1, hid1, slope1, rolled_out = stepped(
-        run_branch, rolled1, [att1], vec[1], weights[1], F32, waits=flow.done[GRAD]
-    )
-    halo_start(OUT, halo_pack(rolled_out, halo, False), False)
+        run_branch, rolled1, [att1], vec[1], weights1, F32, waits=flow.done[GRAD]
+    )
+    out_parts = halo_gather(halo_pack(rolled_out, halo, False, joined=True))
     grad = stepped(halo_unpack, grad_in, flow.done[GRAD], halo, True, BF16, names=())
 
     kept = (
-        (stream0, qkv0, att0, log0, mid0, hid0, slope0, bias0),
-        (rolled1, qkv1, [att1], [log1], mid1, hid1, slope1, bias1),
+        (stream0, qkv0, att0, log0, mid0, hid0, slope0, bias0, weights0, (first, 0)),
+        (rolled1, qkv1, att1, log1, mid1, hid1, slope1, bias1, weights1, (later, 0)),
     )
     tables = [None] * LAYERS
     for layer in reversed(range(LAYERS)):
-        stream, qkv, att, log, mid, hid, slope, bias = kept[layer]
+        stream, qkv, att, log, mid, hid, slope, bias, weights, w_qkv = kept[layer]
         grad_mid, grad_att, rest, *halves = stepped(
-            run_branch_back, grad, mid, att, hid, slope, vec[layer], weights[layer], flags, layer == 0
+            run_branch_back, grad, mid, [att], hid, slope, vec[layer], weights, flags, layer == 0
         )
         if layer == 0:
             flow.start(D_MID, scatter_flow(*halves[:2], one))
@@ -1606,33 +1683,38 @@
         else:
             mid_share1 = lax.psum_scatter(halves[0], ALL, scatter_dimension=0, tiled=True)
         grads, sums = [], []
-        for n in range(len(att)):
+        calls = 1 if layer else 2
+        groups = HEADS // GROUP // calls
+        for n in range(calls):
             *parts, total = stepped(
-                run_attend_back, qkv, grad_att, att[n], bias[n], flags, log[n],
-                layer == 1, n * groups_here, waits=flow.done[OUT] if layer else (),
+                run_attend_back, qkv, grad_att, att, bias, flags, log, layer == 1, n * groups, groups,
             )
             grads.append(parts)
             sums.append(total)
         grads = [part for group in zip(*grads) for part in group]
+        if layer == 0:
+            tables[0] = [
+                stepped(sums_to_table, total, names=names) for total, names in zip(sums, ((), None))
+            ]
+            pairs = [jnp.stack([tables[layer][n] for layer in range(LAYERS)]) for n in range(2)]
+            flow.start(TABLE, table_flow(pairs, heads_here))
         grad_stream, *halves = stepped(
-            run_qkv_back, grads, stream, grad_mid, vec[layer], w_qkv[layer], rest, flags,
+            run_qkv_back, grads, stream, grad_mid, vec[layer], w_qkv, rest, flags,
             F32 if layer else BF16,
         )
         if layer:
             halo_start(BACK, halo_pack(grad_stream, halo, False), False)
         flow.start(D_QKV + layer, scatter_flow(*halves, one))
-        found = [stepped(sums_to_table, total) for total in sums]
-        tables[layer] = jnp.split(found[0], 2) if len(found) == 1 else found
         if layer:
+            found = [stepped(sums_to_table, sums[0])]
+            tables[1] = jnp.split(found[0], 2)
             grad = stepped(
                 halo_unpack, grad_stream, flow.finish(BACK), halo, False, F32, names=(),
                 waits=found,
             )
     in_grad = grad_stream
-    pairs = [jnp.stack([tables[layer][n] for layer in range(LAYERS)]) for n in range(2)]
-    flow.start(TABLE, table_flow(pairs, heads_here))
     clips_out = stepped(
-        halo_unpack, rolled_out, flow.done[OUT], halo, False, BF16, mean_of=stream1
+        halo_unpack, rolled_out, out_parts, halo, False, BF16, mean_of=stream1
     )
     while flow.live:
         flow.step(None)

time: 503 us -> 487 us (0.968)
  other arithmetic: 61.5 us -> 26.8 us
  Pallas kernels: 277 us -> 298 us
    pallas_call x33 -> x41, Pallas kernels: 277 us -> 298 us  [result(): found = run(*args, *waits)]
    convert_element_type x16 -> x0, other arithmetic: 14.1 us -> none  [gather_flow(): other = (other.astype(F32) + token.reshape(())).astype(BF16)]
    concatenate x23 -> x0, other arithmetic: 7.38 us -> none  [the longest x22 6.69 us: gather_flow(): jnp.concatenate([other, out], dim)]
    select_n x19 -> x2, other arithmetic: 9.89 us -> 4.16 us  [last(): return jnp.where(here == 1, pair[1], pair[0]).reshape(-1, own.shape[-1])]
    ppermute x69 -> x57, starting transfers between devices: 81.9 us -> 79 us  [step(): came = [lax.ppermute(value, axis, pairs) for value, axis, pairs in sends]]
    unnamed x144 -> x148, local copies, waits for them, and re-layouts: 10.5 us -> 13.3 us
    convert_element_type x6 -> x10, other arithmetic: 10.1 us -> 8.65 us  [scatter_flow(): own, sent = (half(here), half(1 - here).astype(BF16))]
    ppermute x69 -> x57, waiting for transfers between devices: 33.9 us -> 33.5 us  [step(): came = [lax.ppermute(value, axis, pairs) for value, axis, pairs in sends]]
  transfers between devices with their start and end apart: 71 -> 61, of which waited for: 12 -> 17; matrix products, arithmetic and copies ran while one was open for 16% -> 9% of each run, Pallas kernels for 43% -> 58%
where the time goes in v4:
time: 487 us; the launch traced here: 481 us
  Pallas kernels  298 us (61%)
  starting transfers between devices  79.3 us (16%)
  waiting for transfers between devices  33.6 us (7%)
  local copies, waits for them, and re-layouts  28.2 us (6%)
  other arithmetic  26.8 us (6%)
  between operations  15.4 us (3%)
    pallas_call x41, Pallas kernels, result(): found = run(*args, *waits)  298 us
    ppermute x57, starting transfers between devices, step(): came = [lax.ppermute(value, axis, pairs) for value, axis, pairs in sends]  79 us
    ppermute x57, waiting for transfers between devices, step(): came = [lax.ppermute(value, axis, pairs) for value, axis, pairs in sends]  33.5 us
    unnamed x148, local copies, waits for them, and re-layouts  13.3 us
  transfers between devices with their start and end apart: 61, of which 17 were waited for; matrix products, arithmetic and copies ran while one was open for 9% of the time, Pallas kernels for 58%

profile of v4, /device:TPU:0, one launch (start us, length us, event | category | flops | bytes accessed | tf_op | source)
XLA Modules:
  0.0 481.4 jit_solution(4466038856042513366)
XLA Ops:
  25.0 7.6 %shard_map.679 = (f32[16,392,392]{2,1,0:T(8,128)}, f32[1,1]{1,0:T(1,128)}) custom-call(bf16[128,256]{1,0:T(8,128)(2,1)} %bitcast.236, bf16[7,256,128]{2,1,0:T(8,128)(2,1)} %constant.228.clone.refs_1_, bf16[32,1664]{1,0:T(8,128)(2,1)} %bitcast.229), custom_call_target="tpu_custom_call" | custom-call | flops 4000000000 | bytes 8388608 | tf_op jit(solution)/shard_map/pallas_call | solution.py:499
  38.0 7.7 %shard_map.681 = (f32[16,392,392]{2,1,0:T(8,128)}, f32[1,1]{1,0:T(1,128)}) custom-call(bf16[128,256]{1,0:T(8,128)(2,1)} %bitcast.235, bf16[7,256,128]{2,1,0:T(8,128)(2,1)} %constant.228.clone.refs_1_, f32[16,392,392]{2,1,0:T(8,128)} %get-tuple-element.131.refs_2_, bf16[64,1664]{1,0:T(8,128)(2,1)} %bitcast.207), custom_call_target="tpu_custom_call", output_to_operand_aliasing={{0}: (2, {})} | custom-call | flops 4000000000 | bytes 8388608 | tf_op jit(solution)/shard_map/pallas_call | solution.py:499
  50.3 7.7 %shard_map.683 = (f32[16,392,392]{2,1,0:T(8,128)}, f32[1,1]{1,0:T(1,128)}) custom-call(bf16[128,256]{1,0:T(8,128)(2,1)} %bitcast.237, bf16[7,256,128]{2,1,0:T(8,128)(2,1)} %constant.228.clone.refs_1_, bf16[128,1664]{1,0:T(8,128)(2,1)} %bitcast.185), custom_call_target="tpu_custom_call" | custom-call | flops 4000000000 | bytes 8388608 | tf_op jit(solution)/shard_map/pallas_call | solution.py:499
  82.5 4.7 shard_map.687
  91.6 18.1 %shard_map.689 = (bf16[2,392,512]{2,1,0:T(8,128)(2,1)}, f32[2,4,8,392]{3,2,1,0:T(8,128)}, f32[1,1]{1,0:T(1,128)}) custom-call(s32[9]{0:T(128)} %stack.81.refs_0_, bf16[2,392,1536]{2,1,0:T(8,128)(2,1)} %get-tuple-element.139.refs_1_.refs_2_.refs_3_, bf16[2,392,1536]{2,1,0:T(8,128)(2,1)} %get-tuple-element.139.refs_1_.refs_2_.refs_3_, ...), custom_call_target="tpu_custom_call" | custom-call | flops 10070523904 | bytes 8388608 | tf_op jit(solution)/shard_map/pallas_call | solution.py:499
  113.6 11.5 %shard_map.691 = (f32[2,392,512]{2,1,0:T(8,128)}, bf16[2,392,2048]{2,1,0:T(8,128)(2,1)}, bf16[2,392,2048]{2,1,0:T(8,128)(2,1)}, f32[2,392,512]{2,1,0:T(8,128)}, f32[1,1]{1,0:T(1,128)}) custom-call(bf16[2,392,512]{2,1,0:T(8,128)(2,1)} %get-tuple-element.143.refs_0_.refs_1_.refs_5_, bf16[2,392,512]{2,1,0:T(8,128)(2,1)} %reshape.268.refs_0_.refs_1_.refs_7_, ...), custom_call_target="tpu_custom_call" | custom-call | flops 3699376128 | bytes 8388608 | tf_op jit(solution)/shard_map/pallas_call | solution.py:499
  146.3 7.6 %shard_map.694 = (f32[16,392,392]{2,1,0:T(8,128)}, f32[1,1]{1,0:T(1,128)}) custom-call(bf16[128,256]{1,0:T(8,128)(2,1)} %bitcast.199, bf16[7,256,128]{2,1,0:T(8,128)(2,1)} %constant.228.clone.refs_1_, f32[16,392,392]{2,1,0:T(8,128)} %get-tuple-element.155.refs_2_, bf16[256,1536]{1,0:T(8,128)(2,1)} %bitcast.147, ...), custom_call_target="tpu_custom_call", output_to_operand_aliasing={{0}: (2, {})} | custom-call | flops 4000000000 | bytes 8388608 | tf_op jit(solution)/shard_map/pallas_call | solution.py:499
  163.8 4.7 shard_map.696.refs_3_.refs_1_.refs_2_
  170.9 5.7 %collective-permute-start.22 = (bf16[48,512]{1,0:T(8,128)(2,1)}, bf16[48,512]{1,0:T(8,128)(2,1)S(1)}, u32[]{:S(2)}, u32[]{:S(2)}) collective-permute-start(bf16[48,512]{1,0:T(8,128)(2,1)} %get-tuple-element.164.refs_11_), channel_id=1, source_target_pairs={{0,20},{4,16},{8,28},{12,24},{16,4},{20,0},{24,12},{28,8},{1,21},{... | collective-permute-start | bytes 147464 | tf_op jit(solution)/shard_map/ppermute | solution.py:581
  185.3 19.3 %shard_map.698 = (bf16[2,392,512]{2,1,0:T(8,128)(2,1)}, f32[2,4,8,392]{3,2,1,0:T(8,128)}, f32[1,1]{1,0:T(1,128)}) custom-call(s32[9]{0:T(128)} %stack.81.refs_0_, bf16[2,392,1536]{2,1,0:T(8,128)(2,1)} %shard_map.696.refs_3_.refs_1_.refs_2_, bf16[2,392,1536]{2,1,0:T(8,128)(2,1)} %shard_map.696.refs_3_.refs_1_.refs_2_, ...), custom_call_target="tpu_custom_call" | custom-call | flops 10070523904 | bytes 8388608 | tf_op jit(solution)/shard_map/pallas_call | solution.py:499
  205.4 11.6 %shard_map.700 = (f32[2,392,512]{2,1,0:T(8,128)}, bf16[2,392,2048]{2,1,0:T(8,128)(2,1)}, bf16[2,392,2048]{2,1,0:T(8,128)(2,1)}, f32[2,392,512]{2,1,0:T(8,128)}, f32[1,1]{1,0:T(1,128)}) custom-call(bf16[2,392,512]{2,1,0:T(8,128)(2,1)} %get-tuple-element.167.refs_0_.refs_1_.refs_5_, f32[2,392,512]{2,1,0:T(8,128)} %get-tuple-element.159.refs_0_.refs_1_.refs_4_, ...), custom_call_target="tpu_custom_call" | custom-call | flops 3699376128 | bytes 8388608 | tf_op jit(solution)/shard_map/pallas_call | solution.py:499
  222.7 19.3 %shard_map.703 = (f32[2,392,512]{2,1,0:T(8,128)}, bf16[2,392,512]{2,1,0:T(8,128)(2,1)}, f32[16,512]{1,0:T(8,128)}, bf16[512,4608]{1,0:T(8,128)(2,1)}, f32[1,1]{1,0:T(1,128)}) custom-call(s32[9]{0:T(128)} %stack.81.refs_0_, bf16[2,392,512]{2,1,0:T(8,128)(2,1)} %get-tuple-element.167.refs_0_.refs_1_.refs_5_, bf16[2,392,512]{2,1,0:T(8,128)(2,1)} %get-tuple-element.170.refs_2_, ...), custom_call_target="tpu_custom_call" | custom-call | flops 7398752256 | bytes 8388608 | tf_op jit(solution)/shard_map/pallas_call | solution.py:499
  242.0 27.8 %shard_map.704 = (bf16[2,392,512]{2,1,0:T(8,128)(2,1)}, bf16[2,392,512]{2,1,0:T(8,128)(2,1)}, bf16[2,392,512]{2,1,0:T(8,128)(2,1)}, f32[16,49,768]{2,1,0:T(8,128)}, f32[1,1]{1,0:T(1,128)}) custom-call(s32[9]{0:T(128)} %stack.81.refs_0_, bf16[2,392,1536]{2,1,0:T(8,128)(2,1)} %shard_map.696.refs_3_.refs_1_.refs_2_, ...), custom_call_target="tpu_custom_call" | custom-call | flops 25176309760 | bytes 8388608 | tf_op jit(solution)/shard_map/pallas_call | solution.py:499
  269.9 10.8 %shard_map.705 = (f32[2,392,512]{2,1,0:T(8,128)}, f32[16,16,1664]{2,1,0:T(8,128)}, bf16[16,16,1664]{2,1,0:T(8,128)(2,1)}, f32[1,1]{1,0:T(1,128)}) custom-call(s32[9]{0:T(128)} %stack.81.refs_0_, bf16[2,392,512]{2,1,0:T(8,128)(2,1)} %get-tuple-element.176.refs_1_, bf16[2,392,512]{2,1,0:T(8,128)(2,1)} %get-tuple-element.177.refs_2_, ...), custom_call_target="tpu_custom_call" | custom-call | flops 2466250752 | bytes 8388608 | tf_op jit(solution)/shard_map/pallas_call | solution.py:499
  290.3 10.9 %shard_map.707 = (f32[256,256]{1,0:T(8,128)}, f32[1,1]{1,0:T(1,128)}) custom-call(f32[16,49,768]{2,1,0:T(8,128)} %get-tuple-element.191.refs_0_, bf16[7,256,128]{2,1,0:T(8,128)(2,1)} %constant.228.clone.refs_1_, bf16[144,512]{1,0:T(8,128)(2,1)} %get-tuple-element.182.refs_2_, bf16[144,512]{1,0:T(8,128)(2,1)} %get-tuple-element.183.refs_3_, ...), custom_call_target="tpu_custom_call" | custom-call | flops 4800000000 | bytes 8388608 | tf_op jit(solution)/shard_map/pallas_call | solution.py:499
  313.2 4.9 %collective-permute-done.31.refs_10_ = bf16[48,512]{1,0:T(8,128)(2,1)S(1)} collective-permute-done((bf16[48,512]{1,0:T(8,128)(2,1)S(1)}, bf16[48,512]{1,0:T(8,128)(2,1)S(1)}, u32[]{:S(2)}, u32[]{:S(2)}) %collective-permute-start.31) | collective-permute-done | bytes 49184 | tf_op jit(solution)/shard_map/ppermute | solution.py:581
  323.7 20.5 %shard_map.709 = (f32[2,392,512]{2,1,0:T(8,128)}, bf16[2,392,512]{2,1,0:T(8,128)(2,1)}, f32[16,512]{1,0:T(8,128)}, f32[16,16,2560]{2,1,0:T(8,128)}, bf16[16,16,2...) custom-call(s32[9]{0:T(128)} %stack.81.refs_0_, ...), custom_call_target="tpu_custom_call" | custom-call | flops 7398752256 | bytes 8388608 | tf_op jit(solution)/shard_map/pallas_call | solution.py:499
  347.1 15.1 %shard_map.710 = (bf16[2,392,256]{2,1,0:T(8,128)(2,1)}, bf16[2,392,256]{2,1,0:T(8,128)(2,1)}, bf16[2,392,256]{2,1,0:T(8,128)(2,1)}, f32[8,49,768]{2,1,0:T(8,128)}, f32[1,1]{1,0:T(1,128)}) custom-call(s32[9]{0:T(128)} %stack.81.refs_0_, bf16[2,392,1536]{2,1,0:T(8,128)(2,1)} %get-tuple-element.139.refs_1_.refs_2_.refs_3_, ...), custom_call_target="tpu_custom_call" | custom-call | flops 12588154880 | bytes 8388608 | tf_op jit(solution)/shard_map/pallas_call | solution.py:499
  372.5 15.7 %shard_map.711 = (bf16[2,392,256]{2,1,0:T(8,128)(2,1)}, bf16[2,392,256]{2,1,0:T(8,128)(2,1)}, bf16[2,392,256]{2,1,0:T(8,128)(2,1)}, f32[8,49,768]{2,1,0:T(8,128)}, f32[1,1]{1,0:T(1,128)}) custom-call(s32[9]{0:T(128)} %stack.81.refs_0_, bf16[2,392,1536]{2,1,0:T(8,128)(2,1)} %get-tuple-element.139.refs_1_.refs_2_.refs_3_, ...), custom_call_target="tpu_custom_call" | custom-call | flops 12588154880 | bytes 8388608 | tf_op jit(solution)/shard_map/pallas_call | solution.py:499
  391.5 5.0 %collective-permute-done.35 = bf16[128,2560]{1,0:T(8,128)(2,1)S(1)} collective-permute-done((bf16[128,2560]{1,0:T(8,128)(2,1)S(1)}, bf16[128,2560]{1,0:T(8,128)(2,1)S(1)}, u32[]{:S(2)}, u32[]{:S(2)}) %collective-permute-start.35) | collective-permute-done | bytes 655392 | tf_op jit(solution)/shard_map/ppermute | solution.py:581
  398.2 6.1 %shard_map.713 = (f32[128,256]{1,0:T(8,128)}, f32[1,1]{1,0:T(1,128)}) custom-call(f32[8,49,768]{2,1,0:T(8,128)} %get-tuple-element.218.refs_0_, bf16[7,256,128]{2,1,0:T(8,128)(2,1)} %constant.228.clone.refs_1_, bf16[16,1664]{1,0:T(8,128)(2,1)} %fusion.2.refs_2_, bf16[64,2560]{1,0:T(8,128)(2,1)} %bitcast.194, bf16[256,512]{1,0:T(8,128)(2,1)} %bitcast.202), custom_call_target="tpu_custom_call" | custom-call | flops 2400000000 | bytes 8388608 | tf_op jit(solution)/shard_map/pallas_call | solution.py:499
  405.3 6.1 %shard_map.712 = (f32[128,256]{1,0:T(8,128)}, f32[1,1]{1,0:T(1,128)}) custom-call(f32[8,49,768]{2,1,0:T(8,128)} %get-tuple-element.207.refs_0_, bf16[7,256,128]{2,1,0:T(8,128)(2,1)} %constant.228.clone.refs_1_, bf16[16,1664]{1,0:T(8,128)(2,1)} %fusion.2.refs_2_, bf16[64,2560]{1,0:T(8,128)(2,1)} %bitcast.195, bf16[256,512]{1,0:T(8,128)(2,1)} %bitcast.203), custom_call_target="tpu_custom_call" | custom-call | flops 2400000000 | bytes 8388608 | tf_op jit(solution)/shard_map/pallas_call | solution.py:499
  418.2 10.4 %shard_map.714 = (bf16[2,392,512]{2,1,0:T(8,128)(2,1)}, f32[16,16,1664]{2,1,0:T(8,128)}, bf16[16,16,1664]{2,1,0:T(8,128)(2,1)}, f32[1,1]{1,0:T(1,128)}) custom-call(s32[9]{0:T(128)} %stack.81.refs_0_, bf16[2,392,256]{2,1,0:T(8,128)(2,1)} %get-tuple-element.209.refs_1_, bf16[2,392,256]{2,1,0:T(8,128)(2,1)} %get-tuple-element.210.refs_2_, ...), custom_call_target="tpu_custom_call" | custom-call | flops 2466250752 | bytes 8388608 | tf_op jit(solution)/shard_map/pallas_call | solution.py:499
  432.4 5.4 %shard_map.715 = (bf16[2,392,512]{2,1,0:T(8,128)(2,1)}, f32[1,1]{1,0:T(1,128)}) custom-call(s32[7]{0:T(128)} %stack.72.refs_0_, bf16[196,196]{1,0:T(8,128)(2,1)} %constant.241.clone.refs_0_.refs_1_, bf16[196,144]{1,0:T(8,128)(2,1)} %constant.242.clone.refs_1_.refs_2_, bf16[196,208]{1,0:T(8,128)(2,1)} %constant.243.clone.refs_2_.refs_3_, ...), custom_call_target="tpu_custom_call" | custom-call | flops 629407744 | bytes 8388608 | tf_op jit(solution)/shard_map/pallas_call | solution.py:499
  (345 shorter events, 201.8 us)
Async XLA Ops:
  7.2 106.4 %all-gather.4.cloned.1.call-start = ((), (), s32[]{:S(2)}) async-start(), calls=%async_computation.1 | async-start | bytes 4866048 | tf_op jit(solution)/shard_map/all_gather | solution.py:1490
  10.5 194.3 %all-gather.6.cloned.1.call-start = ((), (), s32[]{:S(2)}) async-start(), calls=%async_computation.2 | async-start | bytes 4866048 | tf_op jit(solution)/shard_map/all_gather | solution.py:1490
  72.3 360.2 %all-gather.8.cloned.1.call-start = ((), (), s32[]{:S(2)}) async-start(), calls=%async_computation.3 | async-start | bytes 5898240 | tf_op jit(solution)/shard_map/all_gather | solution.py:670
  90.1 19.6 %collective-permute-start.8 = (bf16[64,1536]{1,0:T(8,128)(2,1)}, bf16[64,1536]{1,0:T(8,128)(2,1)S(1)}, u32[]{:S(2)}, u32[]{:S(2)}) collective-permute-start(bf16[64,1536]{1,0:T(8,128)(2,1)} %bitcast.213), channel_id=1, source_target_pairs={{0,2},{1,3},{2,0},{3,1},{4,6},{5,7},{6,4},{7,5},{8,10},{9,11},{10,... | collective-permute-start | bytes 589832 | tf_op jit(solution)/shard_map/ppermute | solution.py:581
  128.6 34.0 %collective-permute-start.17 = (bf16[256,1536]{1,0:T(8,128)(2,1)}, bf16[256,1536]{1,0:T(8,128)(2,1)S(1)}, u32[]{:S(2)}, u32[]{:S(2)}) collective-permute-start(bf16[256,1536]{1,0:T(8,128)(2,1)} %bitcast.146), channel_id=1, source_target_pairs={{0,1},{1,0},{2,3},{3,2},{4,5},{5,4},{6,7},{7,6},{8,9},{9,8},{10,11... | collective-permute-start | bytes 2359304 | tf_op jit(solution)/shard_map/ppermute | solution.py:581
  177.1 27.6 %collective-permute-start.18 = (bf16[144,512]{1,0:T(8,128)(2,1)}, bf16[144,512]{1,0:T(8,128)(2,1)S(1)}, u32[]{:S(2)}, u32[]{:S(2)}) collective-permute-start(bf16[144,512]{1,0:T(8,128)(2,1)} %get-tuple-element.160.refs_7_), channel_id=1, source_target_pairs={{0,4},{4,0},{8,12},{12,8},{16,20},{20,16},{24,28},{28,24},{1,5},{5... | collective-permute-start | bytes 442376 | tf_op jit(solution)/shard_map/ppermute | solution.py:581
  178.5 26.2 %collective-permute-start.19 = (bf16[144,512]{1,0:T(8,128)(2,1)}, bf16[144,512]{1,0:T(8,128)(2,1)S(1)}, u32[]{:S(2)}, u32[]{:S(2)}) collective-permute-start(bf16[144,512]{1,0:T(8,128)(2,1)} %get-tuple-element.161.refs_8_), channel_id=1, source_target_pairs={{0,8},{4,12},{8,0},{12,4},{16,24},{20,28},{24,16},{28,20},{1,9},{5... | collective-permute-start | bytes 442376 | tf_op jit(solution)/shard_map/ppermute | solution.py:581
  180.0 24.7 %collective-permute-start.20 = (bf16[144,512]{1,0:T(8,128)(2,1)}, bf16[144,512]{1,0:T(8,128)(2,1)S(1)}, u32[]{:S(2)}, u32[]{:S(2)}) collective-permute-start(bf16[144,512]{1,0:T(8,128)(2,1)} %get-tuple-element.162.refs_9_), channel_id=1, source_target_pairs={{0,12},{4,8},{8,4},{12,0},{16,28},{20,24},{24,20},{28,16},{1,13},{... | collective-permute-start | bytes 442376 | tf_op jit(solution)/shard_map/ppermute | solution.py:581
  181.5 23.1 %collective-permute-start.21 = (bf16[64,512]{1,0:T(8,128)(2,1)}, bf16[64,512]{1,0:T(8,128)(2,1)S(1)}, u32[]{:S(2)}, u32[]{:S(2)}) collective-permute-start(bf16[64,512]{1,0:T(8,128)(2,1)} %get-tuple-element.163.refs_10_), channel_id=1, source_target_pairs={{0,16},{4,20},{8,24},{12,28},{16,0},{20,4},{24,8},{28,12},{1,17},{... | collective-permute-start | bytes 196616 | tf_op jit(solution)/shard_map/ppermute | solution.py:581
  183.4 21.2 %collective-permute-start.24 = (bf16[48,512]{1,0:T(8,128)(2,1)}, bf16[48,512]{1,0:T(8,128)(2,1)S(1)}, u32[]{:S(2)}, u32[]{:S(2)}) collective-permute-start(bf16[48,512]{1,0:T(8,128)(2,1)} %get-tuple-element.166.refs_13_), channel_id=1, source_target_pairs={{0,28},{4,24},{8,20},{12,16},{16,12},{20,8},{24,4},{28,0},{1,29},{... | collective-permute-start | bytes 147464 | tf_op jit(solution)/shard_map/ppermute | solution.py:581
  219.8 252.6 %reduce-scatter.2.cloned.1.call-start = ((), (), s32[]{:S(2)}) async-start(), calls=%async_computation.4 | async-start | bytes 4866048 | tf_op jit(solution)/shard_map/reduce_scatter | solution.py:1684
  280.7 28.8 %collective-permute-start.32 = (bf16[256,1664]{1,0:T(8,128)(2,1)}, bf16[256,1664]{1,0:T(8,128)(2,1)S(1)}, u32[]{:S(2)}, u32[]{:S(2)}) collective-permute-start(bf16[256,1664]{1,0:T(8,128)(2,1)} %bitcast.244), channel_id=1, source_target_pairs={{0,1},{1,0},{2,3},{3,2},{4,5},{5,4},{6,7},{7,6},{8,9},{9,8},{10,11... | collective-permute-start | bytes 2555912 | tf_op jit(solution)/shard_map/ppermute | solution.py:581
  284.1 34.7 %collective-permute-start.25 = (bf16[144,512]{1,0:T(8,128)(2,1)}, bf16[144,512]{1,0:T(8,128)(2,1)S(1)}, u32[]{:S(2)}, u32[]{:S(2)}) collective-permute-start(bf16[144,512]{1,0:T(8,128)(2,1)} %get-tuple-element.182.refs_2_), channel_id=1, source_target_pairs={{0,4},{4,0},{8,12},{12,8},{16,20},{20,16},{24,28},{28,24},{1,5},{5... | collective-permute-start | bytes 442376 | tf_op jit(solution)/shard_map/ppermute | solution.py:581
  284.3 34.5 %collective-permute-start.26 = (bf16[144,512]{1,0:T(8,128)(2,1)}, bf16[144,512]{1,0:T(8,128)(2,1)S(1)}, u32[]{:S(2)}, u32[]{:S(2)}) collective-permute-start(bf16[144,512]{1,0:T(8,128)(2,1)} %get-tuple-element.183.refs_3_), channel_id=1, source_target_pairs={{0,8},{4,12},{8,0},{12,4},{16,24},{20,28},{24,16},{28,20},{1,9},{5... | collective-permute-start | bytes 442376 | tf_op jit(solution)/shard_map/ppermute | solution.py:581
  289.4 20.1 %collective-permute-start.30 = (bf16[48,512]{1,0:T(8,128)(2,1)}, bf16[48,512]{1,0:T(8,128)(2,1)S(1)}, u32[]{:S(2)}, u32[]{:S(2)}) collective-permute-start(bf16[48,512]{1,0:T(8,128)(2,1)} %get-tuple-element.187.refs_7_), channel_id=1, source_target_pairs={{0,24},{4,28},{8,16},{12,20},{16,8},{20,12},{24,0},{28,4},{1,25},{... | collective-permute-start | bytes 147464 | tf_op jit(solution)/shard_map/ppermute | solution.py:581
  318.2 26.6 %collective-permute-start.34 = (bf16[128,1664]{1,0:T(8,128)(2,1)S(1)}, bf16[128,1664]{1,0:T(8,128)(2,1)S(1)}, u32[]{:S(2)}, u32[]{:S(2)}) collective-permute-start(bf16[128,1664]{1,0:T(8,128)(2,1)S(1)} %bitcast.151), channel_id=1, source_target_pairs={{0,16},{16,0},{1,17},{17,1},{2,18},{18,2},{3,19},{19,3},{4,20},{20... | collective-permute-start | bytes 1277960 | tf_op jit(solution)/shard_map/ppermute | solution.py:581
  344.2 22.7 %collective-permute-start.37 = (bf16[1024,512]{1,0:T(8,128)(2,1)}, bf16[1024,512]{1,0:T(8,128)(2,1)S(1)}, u32[]{:S(2)}, u32[]{:S(2)}) collective-permute-start(bf16[1024,512]{1,0:T(8,128)(2,1)} %bitcast.242), channel_id=1, source_target_pairs={{0,1},{1,0},{2,3},{3,2},{4,5},{5,4},{6,7},{7,6},{8,9},{9,8},{10,11... | collective-permute-start | bytes 3145736 | tf_op jit(solution)/shard_map/ppermute | solution.py:581
  344.3 25.0 %collective-permute-start.33 = (bf16[256,2560]{1,0:T(8,128)(2,1)}, bf16[256,2560]{1,0:T(8,128)(2,1)S(1)}, u32[]{:S(2)}, u32[]{:S(2)}) collective-permute-start(bf16[256,2560]{1,0:T(8,128)(2,1)} %bitcast.240), channel_id=1, source_target_pairs={{0,1},{1,0},{2,3},{3,2},{4,5},{5,4},{6,7},{7,6},{8,9},{9,8},{10,11... | collective-permute-start | bytes 3932168 | tf_op jit(solution)/shard_map/ppermute | solution.py:581
  362.9 25.3 %collective-permute-start.39 = (bf16[32,1664]{1,0:T(8,128)(2,1)S(1)}, bf16[32,1664]{1,0:T(8,128)(2,1)S(1)}, u32[]{:S(2)}, u32[]{:S(2)}) collective-permute-start(bf16[32,1664]{1,0:T(8,128)(2,1)S(1)} %bitcast.232), channel_id=1, source_target_pairs={{0,4},{4,0},{8,12},{12,8},{1,5},{5,1},{9,13},{13,9},{2,6},{6,2},{1... | collective-permute-start | bytes 319496 | tf_op jit(solution)/shard_map/ppermute | solution.py:581
  368.0 21.4 %collective-permute-start.40 = (bf16[512,512]{1,0:T(8,128)(2,1)S(1)}, bf16[512,512]{1,0:T(8,128)(2,1)S(1)}, u32[]{:S(2)}, u32[]{:S(2)}) collective-permute-start(bf16[512,512]{1,0:T(8,128)(2,1)S(1)} %bitcast.179), channel_id=1, source_target_pairs={{0,2},{1,3},{2,0},{3,1},{4,6},{5,7},{6,4},{7,5},{8,10},{9,11},{10,... | collective-permute-start | bytes 1572872 | tf_op jit(solution)/shard_map/ppermute | solution.py:581
  370.3 26.2 %collective-permute-start.35 = (bf16[128,2560]{1,0:T(8,128)(2,1)S(1)}, bf16[128,2560]{1,0:T(8,128)(2,1)S(1)}, u32[]{:S(2)}, u32[]{:S(2)}) collective-permute-start(bf16[128,2560]{1,0:T(8,128)(2,1)S(1)} %bitcast.171), channel_id=1, source_target_pairs={{0,16},{16,0},{1,17},{17,1},{2,18},{18,2},{3,19},{19,3},{4,20},{20... | collective-permute-start | bytes 1966088 | tf_op jit(solution)/shard_map/ppermute | solution.py:581
  389.5 52.5 %collective-permute-start.50 = (bf16[16,1664]{1,0:T(8,128)(2,1)}, bf16[16,1664]{1,0:T(8,128)(2,1)}, u32[]{:S(2)}, u32[]{:S(2)}) collective-permute-start(bf16[16,1664]{1,0:T(8,128)(2,1)} %fusion.2.refs_2_), channel_id=1, source_target_pairs={{0,8},{4,12},{8,0},{12,4},{1,9},{5,13},{9,1},{13,5},{2,10},{6,14},... | collective-permute-start | bytes 159752 | tf_op jit(solution)/shard_map/ppermute | solution.py:581
  390.3 24.2 %collective-permute-start.42 = (bf16[256,512]{1,0:T(8,128)(2,1)S(1)}, bf16[256,512]{1,0:T(8,128)(2,1)S(1)}, u32[]{:S(2)}, u32[]{:S(2)}) collective-permute-start(bf16[256,512]{1,0:T(8,128)(2,1)S(1)} %bitcast.201), channel_id=1, source_target_pairs={{0,16},{16,0},{1,17},{17,1},{2,18},{18,2},{3,19},{19,3},{4,20},{20... | collective-permute-start | bytes 786440 | tf_op jit(solution)/shard_map/ppermute | solution.py:581
  397.4 17.9 %collective-permute-start.38 = (bf16[64,2560]{1,0:T(8,128)(2,1)S(1)}, bf16[64,2560]{1,0:T(8,128)(2,1)S(1)}, u32[]{:S(2)}, u32[]{:S(2)}) collective-permute-start(bf16[64,2560]{1,0:T(8,128)(2,1)S(1)} %bitcast.193), channel_id=1, source_target_pairs={{0,2},{1,3},{2,0},{3,1},{4,6},{5,7},{6,4},{7,5},{8,10},{9,11},{10,... | collective-permute-start | bytes 983048 | tf_op jit(solution)/shard_map/ppermute | solution.py:581
  (108 other events, 752.9 us)
Sparse Core Ops, SparseCore 0:
  11.5 66.5 all-gather.3
  81.5 74.6 all-gather.5
  219.9 98.1 all-gather.7
  323.5 119.1 reduce-scatter.1
